TPU v7x, 512 devices: a whole 4x8x8 slice. The times are simulated.
512 devices in a mesh: peer: 64 (over x, z, core), tp: 8 (over y).
Axes of the slice: x: 4, y: 8, z: 8, core: 2. Of those that a mesh axis runs over, the one named last changes fastest.
Arguments:
- activations: bfloat16 [16384, 8192], P('peer', 'tp'), may hold values from -24 to 24
- targets: bfloat16 [16384, 1024], P('peer', 'tp'), may hold values from -6 to 6
- routes: int32 [2048, 1], P('peer'), may hold values from 0 to 63; in each aligned block of 32 rows (0 to 31, 32 to 63, ...) no two rows name the same one
- value_weights: bfloat16 [64, 8192, 1024], P('peer', 'tp'), may hold values from -0.0625 to 0.0625
- norm_gains: float32 [64, 8192], P('peer', 'tp'), may hold values from 0.1 to 1.9
Outputs:
- grad_rows: bfloat16 [16384, 8192], P('peer', 'tp')
- values: bfloat16 [16384, 1024], P('peer', 'tp')
- weight_grad: float32 [1024, 8192], P('peer', 'tp')
- gain_grad: float32 [8192], P('tp')
Inputs may be any that keep to these rules, and one draw needn't show every extreme that they name: `routes`: one source device sends at most 1 of its 32 pieces to one destination, and some source sends exactly 1 piece to one destination.
All inputs are finite; a program needn't handle non-finite values.
Results may differ from a plain program's by a relative error of at most 0.019.
Values may be sent and summed in bfloat16 or wider, within the bound.
No kernel may reach another device: no remote copies, remote signals or barrier semaphores. Data moves between devices by JAX's collectives and lax.ppermute only.
A program may use at most 64 MiB of HBM per device.

v0:
```python
import jax
import jax.numpy as jnp
from jax import lax
from jax.sharding import PartitionSpec as P

D = 8192
KV = 1024
PIECES = 32


epsilon = 1e-05


def slot_table(routes, slot_count, per_pair):
    target_peer = routes[:, 0]
    pieces = target_peer.shape[0]
    counter = jnp.arange(pieces, dtype=jnp.int32)
    earlier = (counter[None, :] < counter[:, None]) & (target_peer[None, :] == target_peer[:, None])
    position = jnp.sum(earlier.astype(jnp.int32), axis=1)
    slot_index = target_peer * per_pair + position
    columns = jnp.arange(slot_count, dtype=jnp.int32)
    return (columns[:, None] == slot_index[None, :]).astype(jnp.bfloat16)


def body(activations, targets, routes, value_weights, norm_gains):
    peer_count = lax.axis_size("peer")
    tp_count = lax.axis_size("tp")
    per_pair = max(1, 2 * PIECES // peer_count)
    local_rows, width_local = activations.shape
    column_count = KV // tp_count
    piece_rows = local_rows // PIECES
    slot_rows = per_pair * piece_rows
    slot_total = peer_count * slot_rows
    grad_scale = (local_rows * peer_count) ** (-0.5)
    selector = slot_table(routes, peer_count * per_pair, per_pair)
    weights = value_weights[0]
    gain_row = norm_gains[0]

    def to_slots(source_block):
        breadth = source_block.shape[1]
        flattened = source_block.reshape(PIECES, piece_rows * breadth)
        packed = jnp.dot(selector, flattened, preferred_element_type=jnp.float32)
        return packed.astype(source_block.dtype).reshape(peer_count, slot_rows, breadth)

    def from_slots(slot_block):
        breadth = slot_block.shape[2]
        flattened = slot_block.reshape(peer_count * per_pair, piece_rows * breadth)
        unpacked = jnp.dot(selector.T, flattened, preferred_element_type=jnp.float32)
        return unpacked.astype(slot_block.dtype).reshape(local_rows, breadth)

    goal_part = lax.all_gather(targets, "tp", axis=1, tiled=True)
    arrived, goal_slots = (
        lax.all_to_all(to_slots(activations), "peer", split_axis=0, concat_axis=0, tiled=True),
        lax.all_to_all(to_slots(goal_part), "peer", split_axis=0, concat_axis=0, tiled=True),
    )
    rows_in = arrived.reshape(slot_total, width_local)
    goals_in = goal_slots.reshape(slot_total, goal_part.shape[1])
    rows_float = rows_in.astype(jnp.float32)
    squares = lax.psum(jnp.sum(rows_float * rows_float, axis=1), "tp")
    scales = lax.rsqrt(squares / D + epsilon)
    normal = rows_float * scales[:, None]
    normed = (normal * gain_row[None, :]).astype(jnp.bfloat16)
    partial_value = jnp.dot(normed, weights, preferred_element_type=jnp.float32)
    value_sum = lax.psum(partial_value.astype(jnp.bfloat16), "tp").astype(jnp.float32)
    grad_values = (value_sum - goals_in.astype(jnp.float32)).astype(jnp.bfloat16)
    grad_normed = lax.dot_general(
        grad_values, weights, (((1,), (1,)), ((), ())), preferred_element_type=jnp.float32
    )
    grad_gained = grad_normed * gain_row[None, :]
    row_dot = lax.psum(jnp.sum(grad_gained * normal, axis=1), "tp")
    grad_in = (scales[:, None] * (grad_gained - normal * (row_dot / D)[:, None])).astype(
        jnp.bfloat16
    )
    gain_part = jnp.sum(grad_normed * normal, axis=0)
    weight_share = lax.psum_scatter(
        lax.dot_general(
            grad_values, normed, (((0,), (0,)), ((), ())), preferred_element_type=jnp.float32
        ),
        "peer",
        scatter_dimension=0,
        tiled=True,
    )
    gain_total = lax.psum(gain_part, "peer")
    column_start = lax.axis_index("tp") * column_count
    value_send = value_sum.astype(jnp.bfloat16)
    grad_back, value_back = (
        lax.all_to_all(
            grad_in.reshape(peer_count, slot_rows, width_local),
            "peer",
            split_axis=0,
            concat_axis=0,
            tiled=True,
        ),
        lax.all_to_all(
            value_send.reshape(peer_count, slot_rows, value_send.shape[1]),
            "peer",
            split_axis=0,
            concat_axis=0,
            tiled=True,
        ),
    )
    grad_rows = from_slots(grad_back)
    values = from_slots(value_back)
    values = lax.dynamic_slice_in_dim(values, column_start, column_count, 1)
    return (grad_rows, values, weight_share * grad_scale, gain_total * grad_scale)


def solution(mesh):
    return jax.shard_map(
        body,
        mesh=mesh,
        in_specs=(
            P("peer", "tp"),
            P("peer", "tp"),
            P("peer", None),
            P("peer", "tp", None),
            P("peer", "tp"),
        ),
        out_specs=(P("peer", "tp"), P("peer", "tp"), P("peer", "tp"), P("tp")),
        check_vma=False,
    )
```

profile of v0, /device:TPU:1, one launch (start us, length us, event | category | flops | bytes accessed | tf_op | source)
XLA Modules:
  0.0 402.1 jit_solution(12739826078499012633)
XLA Ops:
  7.2 0.0 copy-start
  7.2 1.0 convert_reduce_fusion
  8.2 0.7 bitcast_add_fusion
  8.8 1.3 reshape.65
  10.1 0.4 convolution_convert_fusion.1
  10.5 0.0 copy-start.1
  10.6 1.6 copy.9
  12.2 14.8 %all-to-all-start = ((bf16[64,8,1024]{2,1,0:T(8,128)(2,1)}), bf16[64,8,1024]{2,1,0:T(8,128)(2,1)S(1)}, u32[]{:S(2)}, u32[]{:S(2)}) async-start(bf16[64,8,1024]{2,1,0:T(8,128)(2,1)} %bitcast.67), calls=%async_computation | async-start | bytes 2097152 | tf_op jit(solution)/shard_map/all_to_all | solution.py:53
  27.0 0.0 copy-done.1
  27.0 24.0 %all_gather.3 = bf16[256,1024]{1,0:T(8,128)(2,1)} all-gather(bf16[256,128]{1,0:T(8,128)(2,1)S(1)} %copy-done.1), channel_id=1, replica_groups=mesh['peer'=64,'tp'=8] {'tp'}, dimensions={1}, use_global_device_ids=true | all-gather | bytes 589824 | tf_op jit(solution)/shard_map/all_gather | solution.py:51
  51.0 2.1 reshape.67
  53.1 1.4 convolution_convert_fusion
  54.6 1.6 copy.10
  56.2 0.0 copy-start.2
  56.2 0.0 all-to-all-done
  56.2 14.5 %all-to-all-start.1 = ((bf16[64,8,1024]{2,1,0:T(8,128)(2,1)}), bf16[64,8,1024]{2,1,0:T(8,128)(2,1)}, u32[]{:S(2)}, u32[]{:S(2)}) async-start(bf16[64,8,1024]{2,1,0:T(8,128)(2,1)} %bitcast.65), calls=%async_computation.1 | async-start | bytes 2097152 | tf_op jit(solution)/shard_map/all_to_all | solution.py:54
  70.6 0.0 all-reduce.2.cloned.1.call-start
  70.7 0.3 fusion
  71.0 0.1 reduce_sum.40
  71.1 12.5 %psum.28 = f32[512]{0:T(512)S(1)} all-reduce(f32[512]{0:T(512)S(1)} %reduce_sum.40), channel_id=1, replica_groups=mesh['peer'=64,'tp'=8] {'tp'}, use_global_device_ids=true, to_apply=%region_2.0 | all-reduce | flops 512 | bytes 4096 | tf_op jit(solution)/shard_map/psum | solution.py:59
  83.6 0.1 mul.77
  83.7 0.0 copy-done
  83.7 0.0 copy-done.2
  83.7 2.3 fusion.19
  86.1 0.0 all-reduce.2.cloned.1.call-update
  86.1 0.0 reduce-scatter.2.cloned.1.call-start
  86.1 13.0 %all-to-all-done.1 = bf16[64,8,1024]{2,1,0:T(8,128)(2,1)} async-done(((bf16[64,8,1024]{2,1,0:T(8,128)(2,1)}), bf16[64,8,1024]{2,1,0:T(8,128)(2,1)}, u32[]{:S(2)}, u32[]{:S(2)}) %all-to-all-start.1) | async-done | bytes 1048608 | tf_op jit(solution)/shard_map/all_to_all | solution.py:54
  99.1 64.6 %all-reduce.2.cloned.1.call-done = bf16[512,1024]{1,0:T(8,128)(2,1)} async-done(((bf16[512,1024]{1,0:T(8,128)(2,1)}), bf16[512,1024]{1,0:T(8,128)(2,1)}) %all-reduce.2.cloned.1.call-update) | async-done | bytes 1048592 | tf_op jit(solution)/shard_map/psum | solution.py:64
  163.7 5.0 %fusion.22 = f32[1024,1024]{1,0:T(8,128)} fusion(bf16[64,8,1024]{2,1,0:T(8,128)(2,1)S(1)} %all-to-all-done, f32[1024]{0:T(1024)S(1)} %bitcast.73, f32[512]{0:T(512)S(1)} %add_rsqrt_fusion, bf16[512,1024]{1,0:T(8,128)(2,1)} %all-reduce.2.cloned.1.call-done, bf16[64,8,1024]{2,1,0:T(8,128)(2,1)} %all-to-all-done.1), kind=kOutput, calls=%fused_computation.28 | convolution fusion | flops 1077936128 | bytes 7346176 | tf_op jit(solution)/shard_map/dot_general | solution.py:76
  168.7 0.0 reduce-scatter.2.cloned.1.call-update
  168.7 4.4 %fusion.13 = (f32[1024]{0:T(1024)S(1)}, f32[512]{0:T(512)S(1)}, f32[512,1024]{1,0:T(8,128)}) fusion(bf16[64,8,1024]{2,1,0:T(8,128)(2,1)S(1)} %all-to-all-done, f32[512]{0:T(512)S(1)} %add_rsqrt_fusion, f32[1024]{0:T(1024)S(1)} %bitcast.74, bf16[1,1024,1024]{2,1,0:T(8,128)(2,1)S(1)} %copy-done, bf16[512,1024]{1,0:T(8,128)(2,1)} %all-reduce.2.cloned.1.call-done, ...), kind=kOutput, calls=%fused_computation.20 | convolution fusion | flops 1079507456 | bytes 7352320 | tf_op jit(solution)/shard_map/dot_general | solution.py:66
  173.1 12.1 %psum.30 = f32[512]{0:T(512)S(1)} all-reduce(f32[512]{0:T(512)S(1)} %get-tuple-element.5), channel_id=1, replica_groups=mesh['peer'=64,'tp'=8] {'tp'}, use_global_device_ids=true, to_apply=%region_5.0 | all-reduce | flops 512 | bytes 4096 | tf_op jit(solution)/shard_map/psum | solution.py:70
  185.2 2.1 fusion.24
  187.3 48.0 %all_to_all.20 = bf16[64,8,1024]{2,1,0:T(8,128)(2,1)} all-to-all(bf16[64,8,1024]{2,1,0:T(8,128)(2,1)S(1)} %fusion.24), channel_id=1, replica_groups=mesh['peer'=64,'tp'=8] {'peer'}, dimensions={0} | all-to-all | bytes 2097152 | tf_op jit(solution)/shard_map/all_to_all | solution.py:87
  235.3 6.2 %all-to-all-start.3 = ((bf16[64,8,1024]{2,1,0:T(8,128)(2,1)}), bf16[64,8,1024]{2,1,0:T(8,128)(2,1)S(1)}, u32[]{:S(2)}, u32[]{:S(2)}) async-start(bf16[64,8,1024]{2,1,0:T(8,128)(2,1)} %bitcast.7), calls=%async_computation.3 | async-start | bytes 2097152 | tf_op jit(solution)/shard_map/all_to_all | solution.py:94
  241.5 144.8 %psum.31 = f32[1024]{0:T(1024)S(1)} all-reduce(f32[1024]{0:T(1024)S(1)} %get-tuple-element.4), channel_id=1, replica_groups=mesh['peer'=64,'tp'=8] {'peer'}, use_global_device_ids=true, to_apply=%region_8.0 | all-reduce | flops 1024 | bytes 8192 | tf_op jit(solution)/shard_map/psum | solution.py:83
  386.3 0.6 broadcast_multiply_fusion.1
  386.9 1.8 copy.11
  388.7 1.1 convolution_convert_fusion.3
  389.9 2.1 reshape.71
  391.9 0.0 all-to-all-done.3
  391.9 0.6 copy.12
  392.5 0.4 convolution_convert_fusion.2
  392.9 0.2 reshape.74
  393.2 0.7 constant_dynamic-slice_fusion
  393.8 0.0 reduce-scatter.2.cloned.1.call-done
  393.8 1.5 broadcast_multiply_fusion
  (2 shorter events, 0.0 us)
Async XLA Ops:
  7.2 76.5 %copy-start = (bf16[1,1024,1024]{2,1,0:T(8,128)(2,1)S(1)}, bf16[1,1024,1024]{2,1,0:T(8,128)(2,1)}, u32[]{:S(2)}) copy-start(bf16[1,1024,1024]{2,1,0:T(8,128)(2,1)} %param.8) | copy-start | bytes 6291460
  10.5 16.5 %copy-start.1 = (bf16[256,128]{1,0:T(8,128)(2,1)S(1)}, bf16[256,128]{1,0:T(8,128)(2,1)}, u32[]{:S(2)}) copy-start(bf16[256,128]{1,0:T(8,128)(2,1)} %param.6) | copy-start | bytes 196612
  12.2 44.0 %all-to-all-start = ((bf16[64,8,1024]{2,1,0:T(8,128)(2,1)}), bf16[64,8,1024]{2,1,0:T(8,128)(2,1)S(1)}, u32[]{:S(2)}, u32[]{:S(2)}) async-start(bf16[64,8,1024]{2,1,0:T(8,128)(2,1)} %bitcast.67), calls=%async_computation | async-start | bytes 2097152 | tf_op jit(solution)/shard_map/all_to_all | solution.py:53
  56.2 27.6 %copy-start.2 = (f32[1,1024]{1,0:T(1,128)S(1)}, f32[1,1024]{1,0:T(1,128)}, u32[]{:S(2)}) copy-start(f32[1,1024]{1,0:T(1,128)} %param.9) | copy-start | bytes 12292
  56.2 43.0 %all-to-all-start.1 = ((bf16[64,8,1024]{2,1,0:T(8,128)(2,1)}), bf16[64,8,1024]{2,1,0:T(8,128)(2,1)}, u32[]{:S(2)}, u32[]{:S(2)}) async-start(bf16[64,8,1024]{2,1,0:T(8,128)(2,1)} %bitcast.65), calls=%async_computation.1 | async-start | bytes 2097152 | tf_op jit(solution)/shard_map/all_to_all | solution.py:54
  70.6 93.1 %all-reduce.2.cloned.1.call-start = ((), (), s32[]{:S(2)}) async-start(), calls=%async_computation.5 | async-start | bytes 2097152 | tf_op jit(solution)/shard_map/psum | solution.py:64
  86.1 307.7 %reduce-scatter.2.cloned.1.call-start = ((), (), s32[]{:S(2)}) async-start(), calls=%async_computation.6 | async-start | bytes 4259840 | tf_op jit(solution)/shard_map/reduce_scatter | solution.py:75
  235.3 156.7 %all-to-all-start.3 = ((bf16[64,8,1024]{2,1,0:T(8,128)(2,1)}), bf16[64,8,1024]{2,1,0:T(8,128)(2,1)S(1)}, u32[]{:S(2)}, u32[]{:S(2)}) async-start(bf16[64,8,1024]{2,1,0:T(8,128)(2,1)} %bitcast.7), calls=%async_computation.3 | async-start | bytes 2097152 | tf_op jit(solution)/shard_map/all_to_all | solution.py:94
Sparse Core Ops, SparseCore 0:
  86.2 77.4 all-reduce.1
  168.9 154.2 reduce-scatter.1
where the time goes:
time: 403 us; the launch traced here: 402 us
  blocking collectives  241 us (60%)
  waiting for transfers between devices  77.6 us (19%)
  starting transfers between devices  35.6 us (9%)
  matrix products  15.1 us (4%)
  between operations  14.2 us (4%)
  local copies, waits for them, and re-layouts  12.2 us (3%)
  other arithmetic  6.12 us (2%)
    psum x1, blocking collectives, body(): gain_total = lax.psum(gain_part, 'peer')  145 us
    psum x1, waiting for transfers between devices, body(): lax.psum(partial_value.astype(jnp.bfloat16), 'tp').astype(jnp.float32)  64.6 us
    all_to_all x1, blocking collectives, body(): lax.all_to_all(grad_in.reshape(peer_count, slot_rows, width_local), 'peer...  48 us
    all_gather x1, blocking collectives, body(): goal_part = lax.all_gather(targets, 'tp', axis=1, tiled=True)  24 us
    all_to_all x1, starting transfers between devices, body(): lax.all_to_all(to_slots(activations), 'peer', split_axis=0, concat_axis=0...  14.8 us
    all_to_all x1, starting transfers between devices, body(): lax.all_to_all(to_slots(goal_part), 'peer', split_axis=0, concat_axis=0,...  14.5 us
    all_to_all x1, waiting for transfers between devices, body(): lax.all_to_all(to_slots(goal_part), 'peer', split_axis=0, concat_axis=0,...  13 us
    psum x1, blocking collectives, body(): squares = lax.psum(jnp.sum(rows_float * rows_float, axis=1), 'tp')  12.5 us
  transfers between devices with their start and end apart: 5, of which 2 were waited for; matrix products, arithmetic and copies ran while one was open for 5% of the time, Pallas kernels for 0%

commit v1 on v0

v1 whole, which is shorter than its diff:
```python
import jax
import jax.numpy as jnp
from jax import lax
from jax.experimental import pallas as pl
from jax.experimental.pallas import tpu as pltpu
from jax.sharding import Mesh, PartitionSpec as P

D = 8192
KV = 1024
PIECES = 32
MB = 8
F = 1024
C = 128
NP = 64
NT = 8
X, Z, CORES = 4, 8, 2
ROWS = NP * MB
TILE = 128
NTILES = ROWS // TILE
EXTRA = 16
GRAD_SCALE = (ROWS // 2 * NP) ** (-0.5)

epsilon = 1e-05
f32 = jnp.float32
bf16 = jnp.bfloat16
VMEM = pl.BlockSpec(memory_space=pltpu.VMEM)
SMEM = pl.BlockSpec(memory_space=pltpu.SMEM)


def call(kernel, outs, in_specs, scratch=(), flops=0, size=4 << 20, name=None):
    return pl.pallas_call(
        kernel,
        out_shape=outs,
        in_specs=in_specs,
        out_specs=jax.tree.map(lambda _: VMEM, outs),
        scratch_shapes=scratch,
        compiler_params=pltpu.CompilerParams(vmem_limit_bytes=40 << 20),
        cost_estimate=pl.CostEstimate(flops=flops, bytes_accessed=size, transcendentals=0),
        name=name,
    )


def parts(v):
    high = v.astype(bf16).astype(f32)
    rest = v - high
    mid = rest.astype(bf16).astype(f32)
    return high, mid, rest - mid


def to_lanes(square):
    return jnp.sum(square.T, axis=0, keepdims=True)


def to_rows(lanes):
    return jnp.broadcast_to(lanes, (TILE, TILE)).T


def pack_kernel(routes, acts, goals, out, slot_of):
    def clear(d, _):
        slot_of[d] = -1
        return 0

    lax.fori_loop(0, NP, clear, 0)

    def note(m, _):
        slot_of[routes[m]] = m
        return 0

    lax.fori_loop(0, PIECES, note, 0)

    def fill(d, _):
        m = slot_of[d]

        @pl.when(m >= 0)
        def _():
            out[d, :, :F] = acts[m]
            out[d, :, F:] = goals[m]

        @pl.when(m < 0)
        def _():
            out[d] = jnp.zeros((MB, F + C), bf16)

        return 0

    lax.fori_loop(0, NP, fill, 0)


def value_kernel(rows, gain, weights, out, squares):
    def tile(i, _):
        x = rows[pl.ds(i * 16, 16), :, :F].astype(f32).reshape(TILE, F)
        sq = x * x
        folded = sq[:, :128]
        for j in range(1, F // 128):
            folded = folded + sq[:, j * 128 : (j + 1) * 128]
        squares[pl.ds(i, 1), :] = to_lanes(folded)
        partial = jnp.dot((x * gain[...]).astype(bf16), weights[...], preferred_element_type=f32)
        for t in range(NT):
            out[t, pl.ds(pl.multiple_of(i * TILE, TILE), TILE), :] = partial[:, t * C : (t + 1) * C].astype(bf16)
        return 0

    lax.fori_loop(0, NTILES, tile, 0)
    high, mid, low = parts(squares[0:4, :])
    tail = jnp.concatenate([high, mid, low, jnp.zeros_like(high)], axis=0).astype(bf16)
    for t in range(NT):
        out[t, ROWS:, :] = tail


def loss_kernel(got, goals, value_out, send, scales, dots):
    tail = got[0, ROWS:, :].astype(f32)
    for t in range(1, NT):
        tail = tail + got[t, ROWS:, :].astype(f32)
    total = tail[0:4] + tail[4:8] + tail[8:12]
    scales[0:4, :] = lax.rsqrt(total / D + epsilon)
    scales[4:8, :] = jnp.zeros((4, 128), f32)

    def tile(i, _):
        here = pl.ds(pl.multiple_of(i * TILE, TILE), TILE)
        total = got[0, here, :].astype(f32)
        for t in range(1, NT):
            total = total + got[t, here, :].astype(f32)
        value = total * to_rows(scales[pl.ds(i, 1), :])
        value_out[pl.ds(i * 16, 16)] = value.reshape(16, MB, C).astype(bf16)
        goal = goals[pl.ds(i * 16, 16), :, F:].astype(f32).reshape(TILE, C)
        grad = (value - goal).astype(bf16)
        send[here, :] = grad
        dots[pl.ds(i, 1), :] = to_lanes(grad.astype(f32) * value)
        return 0

    lax.fori_loop(0, NTILES, tile, 0)
    high, mid, low = parts(dots[0:4, :])
    send[ROWS:, :] = jnp.concatenate([high, mid, low, jnp.zeros_like(high)], axis=0).astype(bf16)


def grad_kernel(got, rows, gain, weights, scales, value, back, share, normed, grads, dots, gains):
    tail = got[0, ROWS:, :].astype(f32)
    for t in range(1, NT):
        tail = tail + got[t, ROWS:, :].astype(f32)
    dots[0:4, :] = (tail[0:4] + tail[4:8] + tail[8:12]) / D
    gains[...] = jnp.zeros_like(gains)

    def tile(i, _):
        here = pl.ds(pl.multiple_of(i * TILE, TILE), TILE)
        slots = pl.ds(i * 16, 16)
        for t in range(NT):
            grads[here, t * C : (t + 1) * C] = got[t, here, :]
        grad_normed = lax.dot_general(
            grads[here, :], weights[...], (((1,), (1,)), ((), ())), preferred_element_type=f32
        )
        scale = to_rows(scales[pl.ds(i, 1), :])[:, :1]
        dot = to_rows(dots[pl.ds(i, 1), :])[:, :1]
        normal = rows[slots, :, :F].astype(f32).reshape(TILE, F) * scale
        gained = grad_normed * gain[...]
        row_grad = scale * (gained - normal * dot)
        back[slots, :, :F] = row_grad.reshape(16, MB, F).astype(bf16)
        back[slots, :, F:] = value[slots]
        gains[...] += jnp.sum((grad_normed * normal).reshape(TILE // 8, 8, F), axis=0)
        normed[here, :] = (normal * gain[...]).astype(bf16)
        return 0

    lax.fori_loop(0, NTILES, tile, 0)

    def block(i, _):
        mine = lax.dot_general(
            grads[:, pl.ds(pl.multiple_of(i * 256, 256), 256)],
            normed[...],
            (((0,), (0,)), ((), ())),
            preferred_element_type=f32,
        ).astype(bf16)
        for j in range(16):
            at = pl.multiple_of(i * 128 + (j // 2) * 16, 16)
            share[j % 2, pl.ds(at, 16), :] = mine[j * 16 : (j + 1) * 16, :]
        return 0

    lax.fori_loop(0, KV // 256, block, 0)
    tail = gain_tail(jnp.sum(gains[...], axis=0, keepdims=True))
    for c in range(CORES):
        share[c, 512:, :] = tail


def gain_tail(total):
    high, mid, low = parts(total)
    return jnp.concatenate([high, mid, low, jnp.zeros((EXTRA - 3, F), f32)], axis=0).astype(bf16)


def sum_kernel(given, taken, count, got, out):
    for i in range(taken):
        total = got[0, i * count : (i + 1) * count, :].astype(f32)
        for g in range(1, given):
            total = total + got[g, i * count : (i + 1) * count, :].astype(f32)
        out[i, :count, :] = total.astype(bf16)
    tail = got[0, taken * count :, :].astype(f32)
    for g in range(1, given):
        tail = tail + got[g, taken * count :, :].astype(f32)
    tail = gain_tail(jnp.sum(tail, axis=0, keepdims=True))
    for i in range(taken):
        out[i, count:, :] = tail


def last_kernel(got, weight_out, gain_out):
    total = got[0].astype(f32)
    for g in range(1, Z):
        total = total + got[g].astype(f32)
    weight_out[...] = total[:16] * GRAD_SCALE
    gain_out[...] = jnp.sum(total[16:], axis=0, keepdims=True) * GRAD_SCALE


def unpack_kernel(routes, got, rows, values):
    def take(m, _):
        d = routes[m]
        rows[m] = got[d, :, :F]
        values[m] = got[d, :, F:]
        return 0

    lax.fori_loop(0, PIECES, take, 0)


def shape(*dims, dtype=bf16):
    return jax.ShapeDtypeStruct(dims, dtype)


def exchange(v, axes):
    return lax.all_to_all(v, axes, split_axis=0, concat_axis=0, tiled=True)


def body(activations, targets, routes, value_weights, norm_gains):
    peer = ("x", "z", "core")
    weights = value_weights[0]
    order = routes[:, 0]
    sends = call(
        pack_kernel,
        shape(NP, MB, F + C),
        [SMEM, VMEM, VMEM],
        [pltpu.SMEM((NP,), jnp.int32)],
        name="pack",
    )(order, activations.reshape(PIECES, MB, F), targets.reshape(PIECES, MB, C))
    arrived = exchange(sends, peer)
    partials = call(
        value_kernel,
        shape(NT, ROWS + EXTRA, C),
        [VMEM] * 3,
        [pltpu.VMEM((8, 128), f32)],
        flops=2 * ROWS * F * KV,
        name="partial_values",
    )(arrived, norm_gains, weights)
    value, grad_part, scales = call(
        loss_kernel,
        (shape(NP, MB, C), shape(ROWS + EXTRA, C), shape(8, 128, dtype=f32)),
        [VMEM] * 2,
        [pltpu.VMEM((8, 128), f32)],
        name="loss",
    )(exchange(partials, "tp"), arrived)
    grads = lax.all_gather(grad_part, "tp", axis=0, tiled=False)
    back, share = call(
        grad_kernel,
        (shape(NP, MB, F + C), shape(CORES, KV // CORES + EXTRA, F)),
        [VMEM] * 6,
        [
            pltpu.VMEM((ROWS, F), bf16),
            pltpu.VMEM((ROWS, KV), bf16),
            pltpu.VMEM((8, 128), f32),
            pltpu.VMEM((8, F), f32),
        ],
        flops=4 * ROWS * F * KV,
        size=8 << 20,
        name="grads",
    )(grads, arrived, norm_gains, weights, scales, value)

    rows_back = exchange(back, peer)
    by_core = exchange(share, "core")
    by_core = call(
        lambda *refs: sum_kernel(CORES, X, 128, *refs), shape(X, 128 + EXTRA, F), [VMEM], name="sum_core"
    )(by_core)
    by_x = exchange(by_core, "x")
    by_x = call(lambda *refs: sum_kernel(X, Z, 16, *refs), shape(Z, 16 + EXTRA, F), [VMEM], name="sum_x")(by_x)
    by_z = exchange(by_x, "z")
    weight_grad, gain_grad = call(
        last_kernel, (shape(16, F, dtype=f32), shape(1, F, dtype=f32)), [VMEM], name="sum_z"
    )(by_z)
    grad_rows, values = call(
        unpack_kernel,
        (shape(PIECES, MB, F), shape(PIECES, MB, C)),
        [SMEM, VMEM],
        name="unpack",
    )(order, rows_back)
    return (
        grad_rows.reshape(PIECES * MB, F),
        values.reshape(PIECES * MB, C),
        weight_grad,
        gain_grad[0],
    )


def solution(mesh):
    split = Mesh(mesh.devices.reshape(X, Z, CORES, NT), ("x", "z", "core", "tp"))
    peer = ("x", "z", "core")
    return jax.shard_map(
        body,
        mesh=split,
        in_specs=(
            P(peer, "tp"),
            P(peer, "tp"),
            P(peer, None),
            P(peer, "tp", None),
            P(peer, "tp"),
        ),
        out_specs=(P(peer, "tp"), P(peer, "tp"), P(peer, "tp"), P("tp")),
        check_vma=False,
    )
```

time: 403 us -> 234 us (0.58)
  blocking collectives: 241 us -> 133 us
  starting transfers between devices: 35.6 us -> 8.12 us
  waiting for transfers between devices: 77.6 us -> 59.9 us
  matrix products: 15.1 us -> 0 us
  Pallas kernels: 0 us -> 14.9 us
  local copies, waits for them, and re-layouts: 12.2 us -> 3.78 us
  other arithmetic: 6.12 us -> 0 us
    psum x3 -> x0, blocking collectives: 169 us -> none  [the longest x1 145 us: body(): gain_total = lax.psum(gain_part, 'peer')]
    all_to_all x1 -> x5, blocking collectives: 48 us -> 133 us  [exchange(): return lax.all_to_all(v, axes, split_axis=0, concat_axis=0, tiled=True)]
    psum x1 -> x0, waiting for transfers between devices: 64.6 us -> none  [body(): lax.psum(partial_value.astype(jnp.bfloat16), 'tp').astype(jnp.float32)]
    all_gather x0 -> x1, waiting for transfers between devices: none -> 29.1 us  [body(): grads = lax.all_gather(grad_part, 'tp', axis=0, tiled=False)]
    all_to_all x3 -> x1, starting transfers between devices: 35.5 us -> 8.08 us  [exchange(): return lax.all_to_all(v, axes, split_axis=0, concat_axis=0, tiled=True)]
    all_gather x1 -> x0, blocking collectives: 24 us -> none  [body(): goal_part = lax.all_gather(targets, 'tp', axis=1, tiled=True)]
    all_to_all x3 -> x1, waiting for transfers between devices: 13 us -> 30.7 us  [exchange(): return lax.all_to_all(v, axes, split_axis=0, concat_axis=0, tiled=True)]
    dot_general x7 -> x0, matrix products: 15.1 us -> none  [the longest x1 4.97 us: body(): lax.dot_general(grad_values, normed, (((0,), (0,)), ((), ())), preferred_...]
  transfers between devices with their start and end apart: 5 -> 2, of which waited for: 2 -> 2; matrix products, arithmetic and copies ran while one was open for 5% -> 0% of each run, Pallas kernels for 0% -> 0%
where the time goes in v1:
time: 234 us; the launch traced here: 233 us
  blocking collectives  133 us (57%)
  waiting for transfers between devices  59.9 us (26%)
  Pallas kernels  14.9 us (6%)
  between operations  14.1 us (6%)
  starting transfers between devices  8.12 us (3%)
  local copies, waits for them, and re-layouts  3.78 us (2%)
    all_to_all x5, blocking collectives, exchange(): return lax.all_to_all(v, axes, split_axis=0, concat_axis=0, tiled=True)  133 us
    all_to_all x1, waiting for transfers between devices, exchange(): return lax.all_to_all(v, axes, split_axis=0, concat_axis=0, tiled=True)  30.7 us
    all_gather x1, waiting for transfers between devices, body(): grads = lax.all_gather(grad_part, 'tp', axis=0, tiled=False)  29.1 us
    all_to_all x1, starting transfers between devices, exchange(): return lax.all_to_all(v, axes, split_axis=0, concat_axis=0, tiled=True)  8.08 us
    pallas_call x1, Pallas kernels, body(): call(grad_kernel, (shape(NP, MB, F + C), shape(CORES, KV // CORES + EXTRA...  6.47 us
  transfers between devices with their start and end apart: 2, of which 2 were waited for; matrix products, arithmetic and copies ran while one was open for 0% of the time, Pallas kernels for 0%

profile of v1, /device:TPU:1, one launch (start us, length us, event | category | flops | bytes accessed | tf_op | source)
XLA Modules:
  0.0 233.5 jit_solution(3595904089988172517)
XLA Ops:
  7.2 0.0 all-gather.3.cloned.1.call-start
  7.2 0.0 copy-start.1
  7.2 1.0 copy-done.1
  8.3 0.0 copy-start.2
  8.3 0.8 copy-done.2
  9.1 0.0 copy-start.4
  9.1 0.7 copy-done.4
  9.8 2.4 %pack.1 = bf16[64,8,1152]{2,1,0:T(8,128)(2,1)S(1)} custom-call(s32[32]{0:T(128)S(1)} %bitcast.12, bf16[32,8,1024]{2,1,0:T(8,128)(2,1)S(1)} %bitcast.10, bf16[32,8,128]{2,1,0:T(8,128)(2,1)S(1)} %bitcast.11), custom_call_target="tpu_custom_call" | custom-call | bytes 4194304 | tf_op jit(solution)/shard_map/pack/pallas_call | solution.py:229
  12.2 0.0 copy-start
  12.2 0.0 copy-start.3
  12.2 46.1 %all_to_all.30.rows.goals = bf16[64,8,1152]{2,1,0:T(8,128)(2,1)S(1)} all-to-all(bf16[64,8,1152]{2,1,0:T(8,128)(2,1)S(1)} %pack.1), channel_id=1, replica_groups=mesh['x'=4,'z'=8,'core'=2,'tp'=8] {'x','z','core'}, dimensions={0} | all-to-all | bytes 2359296 | tf_op jit(solution)/shard_map/all_to_all | solution.py:222
  58.3 0.0 copy-done
  58.3 0.0 copy-done.3
  58.3 1.9 partial_values.1
  60.2 36.2 %all_to_all.31.got = bf16[8,528,128]{2,1,0:T(8,128)(2,1)S(1)} all-to-all(bf16[8,528,128]{2,1,0:T(8,128)(2,1)S(1)} %partial_values.1), channel_id=1, replica_groups=mesh['x'=4,'z'=8,'core'=2,'tp'=8] {'tp'}, dimensions={0} | all-to-all | bytes 2162688 | tf_op jit(solution)/shard_map/all_to_all | solution.py:222
  96.4 1.4 loss.1
  97.8 0.0 all-gather.3.cloned.1.call-update
  97.8 29.1 %all-gather.3.cloned.1.call-done = bf16[4224,128]{1,0:T(8,128)(2,1)} async-done(((bf16[528,128]{1,0:T(8,128)(2,1)}), bf16[4224,128]{1,0:T(8,128)(2,1)}) %all-gather.3.cloned.1.call-update) | async-done | bytes 1081360 | tf_op jit(solution)/shard_map/all_gather | solution.py:252
  127.0 0.0 copy-start.6
  127.0 1.2 copy-done.6
  128.2 6.5 %grads.1 = (bf16[64,8,1152]{2,1,0:T(8,128)(2,1)}, bf16[2,528,1024]{2,1,0:T(8,128)(2,1)S(1)}) custom-call(bf16[8,528,128]{2,1,0:T(8,128)(2,1)S(1)} %bitcast.14, bf16[64,8,1152]{2,1,0:T(8,128)(2,1)S(1)} %all_to_all.30.rows.goals, f32[1,1024]{1,0:T(1,128)S(1)} %copy-done.3, bf16[1024,1024]{1,0:T(8,128)(2,1)S(1)} %bitcast.9, ...), custom_call_target="tpu_custom_call" | custom-call | flops 2147483648 | bytes 8388608 | tf_op jit(solution)/shard_map/grads/pallas_call | solution.py:253
  134.7 9.5 %all_to_all.32.refs_0_ = bf16[2,528,1024]{2,1,0:T(8,128)(2,1)S(1)} all-to-all(bf16[2,528,1024]{2,1,0:T(8,128)(2,1)S(1)} %get-tuple-element.19), channel_id=1, replica_groups=mesh['x'=4,'z'=8,'core'=2,'tp'=8] {'core'}, dimensions={0} | all-to-all | bytes 4325376 | tf_op jit(solution)/shard_map/all_to_all | solution.py:222
  144.2 0.3 sum_core.1
  144.5 19.4 %all_to_all.33.refs_0_ = bf16[4,144,1024]{2,1,0:T(8,128)(2,1)S(1)} all-to-all(bf16[4,144,1024]{2,1,0:T(8,128)(2,1)S(1)} %sum_core.1), channel_id=1, replica_groups=mesh['x'=4,'z'=8,'core'=2,'tp'=8] {'x'}, dimensions={0} | all-to-all | bytes 2359296 | tf_op jit(solution)/shard_map/all_to_all | solution.py:222
  163.9 0.2 sum_x.1
  164.1 21.5 %all_to_all.34.got = bf16[8,32,1024]{2,1,0:T(8,128)(2,1)S(1)} all-to-all(bf16[8,32,1024]{2,1,0:T(8,128)(2,1)S(1)} %sum_x.1), channel_id=1, replica_groups=mesh['x'=4,'z'=8,'core'=2,'tp'=8] {'z'}, dimensions={0} | all-to-all | bytes 1048576 | tf_op jit(solution)/shard_map/all_to_all | solution.py:222
  185.5 0.0 copy-start.5
  185.6 8.1 %all-to-all-start.2 = ((bf16[64,8,1152]{2,1,0:T(8,128)(2,1)}), bf16[64,8,1152]{2,1,0:T(8,128)(2,1)S(1)}, u32[]{:S(2)}, u32[]{:S(2)}) async-start(bf16[64,8,1152]{2,1,0:T(8,128)(2,1)} %get-tuple-element.16), calls=%async_computation.2 | async-start | bytes 2359296 | tf_op jit(solution)/shard_map/all_to_all | solution.py:222
  193.6 0.7 sum_z.1
  194.3 30.7 %all-to-all-done.2.got = bf16[64,8,1152]{2,1,0:T(8,128)(2,1)S(1)} async-done(((bf16[64,8,1152]{2,1,0:T(8,128)(2,1)}), bf16[64,8,1152]{2,1,0:T(8,128)(2,1)S(1)}, u32[]{:S(2)}, u32[]{:S(2)}) %all-to-all-start.2) | async-done | bytes 1179680 | tf_op jit(solution)/shard_map/all_to_all | solution.py:222
  225.0 0.0 copy-done.5
  225.0 1.6 unpack.1
Async XLA Ops:
  7.2 119.8 %all-gather.3.cloned.1.call-start = ((), (), s32[]{:S(2)}) async-start(), calls=%async_computation.6 | async-start | bytes 1216512 | tf_op jit(solution)/shard_map/all_gather | solution.py:252
  7.2 1.0 copy-start.1
  8.3 0.8 copy-start.2
  9.1 0.7 copy-start.4
  12.2 46.2 %copy-start = (bf16[1,1024,1024]{2,1,0:T(8,128)(2,1)S(1)}, bf16[1,1024,1024]{2,1,0:T(8,128)(2,1)}, u32[]{:S(2)}) copy-start(bf16[1,1024,1024]{2,1,0:T(8,128)(2,1)} %param.8) | copy-start | bytes 6291460
  12.2 46.1 %copy-start.3 = (f32[1,1024]{1,0:T(1,128)S(1)}, f32[1,1024]{1,0:T(1,128)}, u32[]{:S(2)}) copy-start(f32[1,1024]{1,0:T(1,128)} %gain.3) | copy-start | bytes 12292
  127.0 1.2 copy-start.6
  185.5 39.5 %copy-start.5 = (s32[32,1]{0,1:T(1,128)S(1)}, s32[32,1]{0,1:T(1,128)}, u32[]{:S(2)}) copy-start(s32[32,1]{0,1:T(1,128)} %param.7) | copy-start | bytes 388
  185.6 39.5 %all-to-all-start.2 = ((bf16[64,8,1152]{2,1,0:T(8,128)(2,1)}), bf16[64,8,1152]{2,1,0:T(8,128)(2,1)S(1)}, u32[]{:S(2)}, u32[]{:S(2)}) async-start(bf16[64,8,1152]{2,1,0:T(8,128)(2,1)} %get-tuple-element.16), calls=%async_computation.2 | async-start | bytes 2359296 | tf_op jit(solution)/shard_map/all_to_all | solution.py:222
Sparse Core Ops, SparseCore 0:
  97.9 28.9 all-gather.2

commit v2 on v1

--- a/solution.py
+++ b/solution.py
@@ -24,6 +24,7 @@
 f32 = jnp.float32
 bf16 = jnp.bfloat16
 VMEM = pl.BlockSpec(memory_space=pltpu.VMEM)
+ANY = pl.BlockSpec(memory_space=pl.ANY)
 SMEM = pl.BlockSpec(memory_space=pltpu.SMEM)
 
 
@@ -55,34 +56,26 @@
     return jnp.broadcast_to(lanes, (TILE, TILE)).T
 
 
-def pack_kernel(routes, acts, goals, out, slot_of):
+def pack_kernel(routes, acts, goals, out, order, route_sem, row_sem, goal_sem):
+    fetch = pltpu.make_async_copy(routes, order, route_sem)
+    fetch.start()
+
     def clear(d, _):
-        slot_of[d] = -1
-        return 0
-
-    lax.fori_loop(0, NP, clear, 0)
-
-    def note(m, _):
-        slot_of[routes[m]] = m
-        return 0
-
-    lax.fori_loop(0, PIECES, note, 0)
-
-    def fill(d, _):
-        m = slot_of[d]
-
-        @pl.when(m >= 0)
-        def _():
-            out[d, :, :F] = acts[m]
-            out[d, :, F:] = goals[m]
-
-        @pl.when(m < 0)
-        def _():
-            out[d] = jnp.zeros((MB, F + C), bf16)
-
-        return 0
-
-    lax.fori_loop(0, NP, fill, 0)
+        out[pl.ds(d * 4, 4)] = jnp.zeros((4, MB, F + C), bf16)
+        return 0
+
+    lax.fori_loop(0, NP // 4, clear, 0)
+    fetch.wait()
+
+    def send(m, _):
+        d = order[m]
+        pltpu.make_async_copy(acts.at[m], out.at[d, :, pl.ds(0, F)], row_sem).start()
+        pltpu.make_async_copy(goals.at[m], out.at[d, :, pl.ds(F, C)], goal_sem).start()
+        return 0
+
+    lax.fori_loop(0, PIECES, send, 0)
+    pltpu.make_async_copy(acts, out.at[pl.ds(0, PIECES), :, pl.ds(0, F)], row_sem).wait()
+    pltpu.make_async_copy(goals, out.at[pl.ds(0, PIECES), :, pl.ds(F, C)], goal_sem).wait()
 
 
 def value_kernel(rows, gain, weights, out, squares):
@@ -122,16 +115,19 @@
         value_out[pl.ds(i * 16, 16)] = value.reshape(16, MB, C).astype(bf16)
         goal = goals[pl.ds(i * 16, 16), :, F:].astype(f32).reshape(TILE, C)
         grad = (value - goal).astype(bf16)
-        send[here, :] = grad
+        for t in range(NT):
+            send[t, here, :] = grad
         dots[pl.ds(i, 1), :] = to_lanes(grad.astype(f32) * value)
         return 0
 
     lax.fori_loop(0, NTILES, tile, 0)
     high, mid, low = parts(dots[0:4, :])
-    send[ROWS:, :] = jnp.concatenate([high, mid, low, jnp.zeros_like(high)], axis=0).astype(bf16)
-
-
-def grad_kernel(got, rows, gain, weights, scales, value, back, share, normed, grads, dots, gains):
+    tail = jnp.concatenate([high, mid, low, jnp.zeros_like(high)], axis=0).astype(bf16)
+    for t in range(NT):
+        send[t, ROWS:, :] = tail
+
+
+def grad_kernel(got, rows, gain, weights, scales, value, back, normed, grads, gains, dots):
     tail = got[0, ROWS:, :].astype(f32)
     for t in range(1, NT):
         tail = tail + got[t, ROWS:, :].astype(f32)
@@ -159,22 +155,29 @@
 
     lax.fori_loop(0, NTILES, tile, 0)
 
+
+def share_kernel(grads, normed, gains, keep, send):
+    first = lax.axis_index("core") == 0
+
     def block(i, _):
         mine = lax.dot_general(
             grads[:, pl.ds(pl.multiple_of(i * 256, 256), 256)],
             normed[...],
             (((0,), (0,)), ((), ())),
             preferred_element_type=f32,
-        ).astype(bf16)
-        for j in range(16):
-            at = pl.multiple_of(i * 128 + (j // 2) * 16, 16)
-            share[j % 2, pl.ds(at, 16), :] = mine[j * 16 : (j + 1) * 16, :]
+        )
+        for j in range(8):
+            at = pl.ds(pl.multiple_of(i * 128 + j * 16, 16), 16)
+            even = mine[j * 32 : j * 32 + 16, :]
+            odd = mine[j * 32 + 16 : j * 32 + 32, :]
+            keep[at, :] = jnp.where(first, even, odd)
+            send[at, :] = jnp.where(first, odd, even).astype(bf16)
         return 0
 
     lax.fori_loop(0, KV // 256, block, 0)
-    tail = gain_tail(jnp.sum(gains[...], axis=0, keepdims=True))
-    for c in range(CORES):
-        share[c, 512:, :] = tail
+    total = jnp.sum(gains[...], axis=0, keepdims=True)
+    keep[KV // 2 :, :] = jnp.concatenate([total, jnp.zeros((EXTRA - 1, F), f32)], axis=0)
+    send[KV // 2 :, :] = gain_tail(total)
 
 
 def gain_tail(total):
@@ -182,18 +185,34 @@
     return jnp.concatenate([high, mid, low, jnp.zeros((EXTRA - 3, F), f32)], axis=0).astype(bf16)
 
 
-def sum_kernel(given, taken, count, got, out):
-    for i in range(taken):
-        total = got[0, i * count : (i + 1) * count, :].astype(f32)
-        for g in range(1, given):
-            total = total + got[g, i * count : (i + 1) * count, :].astype(f32)
-        out[i, :count, :] = total.astype(bf16)
-    tail = got[0, taken * count :, :].astype(f32)
-    for g in range(1, given):
-        tail = tail + got[g, taken * count :, :].astype(f32)
+def core_kernel(keep, got, own, *sends):
+    me = lax.axis_index("x")
+    tail = keep[KV // 2 :, :] + got[KV // 2 :, :].astype(f32)
+    tail = jnp.sum(tail, axis=0, keepdims=True)
+    here = pl.ds(pl.multiple_of(me * 128, 128), 128)
+    own[:128, :] = keep[here, :] + got[here, :].astype(f32)
+    own[128:, :] = jnp.concatenate([tail, jnp.zeros((EXTRA - 1, F), f32)], axis=0)
+    tail = gain_tail(tail)
+    for d, send in enumerate(sends):
+        there = pl.ds(pl.multiple_of(lax.rem(me + d + 1, X) * 128, 128), 128)
+        send[:128, :] = (keep[there, :] + got[there, :].astype(f32)).astype(bf16)
+        send[128:, :] = tail
+
+
+def x_kernel(own, *refs):
+    *got, out = refs
+    for i in range(Z):
+        at = slice(i * 16, (i + 1) * 16)
+        total = own[at, :]
+        for g in got:
+            total = total + g[at, :].astype(f32)
+        out[i, :16, :] = total.astype(bf16)
+    tail = own[128:, :]
+    for g in got:
+        tail = tail + g[128:, :].astype(f32)
     tail = gain_tail(jnp.sum(tail, axis=0, keepdims=True))
-    for i in range(taken):
-        out[i, count:, :] = tail
+    for i in range(Z):
+        out[i, 16:, :] = tail
 
 
 def last_kernel(got, weight_out, gain_out):
@@ -229,8 +248,8 @@
     sends = call(
         pack_kernel,
         shape(NP, MB, F + C),
-        [SMEM, VMEM, VMEM],
-        [pltpu.SMEM((NP,), jnp.int32)],
+        [ANY] * 3,
+        [pltpu.SMEM((PIECES,), jnp.int32)] + [pltpu.SemaphoreType.DMA] * 3,
         name="pack",
     )(order, activations.reshape(PIECES, MB, F), targets.reshape(PIECES, MB, C))
     arrived = exchange(sends, peer)
@@ -244,34 +263,38 @@
     )(arrived, norm_gains, weights)
     value, grad_part, scales = call(
         loss_kernel,
-        (shape(NP, MB, C), shape(ROWS + EXTRA, C), shape(8, 128, dtype=f32)),
+        (shape(NP, MB, C), shape(NT, ROWS + EXTRA, C), shape(8, 128, dtype=f32)),
         [VMEM] * 2,
         [pltpu.VMEM((8, 128), f32)],
         name="loss",
     )(exchange(partials, "tp"), arrived)
-    grads = lax.all_gather(grad_part, "tp", axis=0, tiled=False)
-    back, share = call(
+    back, normed, grads, gains = call(
         grad_kernel,
-        (shape(NP, MB, F + C), shape(CORES, KV // CORES + EXTRA, F)),
+        (shape(NP, MB, F + C), shape(ROWS, F), shape(ROWS, KV), shape(8, F, dtype=f32)),
         [VMEM] * 6,
-        [
-            pltpu.VMEM((ROWS, F), bf16),
-            pltpu.VMEM((ROWS, KV), bf16),
-            pltpu.VMEM((8, 128), f32),
-            pltpu.VMEM((8, F), f32),
-        ],
-        flops=4 * ROWS * F * KV,
+        [pltpu.VMEM((8, 128), f32)],
+        flops=2 * ROWS * F * KV,
         size=8 << 20,
         name="grads",
-    )(grads, arrived, norm_gains, weights, scales, value)
-
+    )(exchange(grad_part, "tp"), arrived, norm_gains, weights, scales, value)
     rows_back = exchange(back, peer)
-    by_core = exchange(share, "core")
-    by_core = call(
-        lambda *refs: sum_kernel(CORES, X, 128, *refs), shape(X, 128 + EXTRA, F), [VMEM], name="sum_core"
-    )(by_core)
-    by_x = exchange(by_core, "x")
-    by_x = call(lambda *refs: sum_kernel(X, Z, 16, *refs), shape(Z, 16 + EXTRA, F), [VMEM], name="sum_x")(by_x)
+
+    half = (KV // CORES + EXTRA, F)
+    keep, send = call(
+        share_kernel,
+        (shape(*half, dtype=f32), shape(*half)),
+        [VMEM] * 3,
+        flops=2 * ROWS * F * KV,
+        name="share",
+    )(grads, normed, gains)
+    got = lax.ppermute(send, "core", [(0, 1), (1, 0)])
+    block = (KV // CORES // X + EXTRA, F)
+    own, *sends = call(
+        core_kernel, (shape(*block, dtype=f32),) + (shape(*block),) * (X - 1), [VMEM] * 2, name="sum_core"
+    )(keep, got)
+    got = [lax.ppermute(v, "x", [(i, (i + d + 1) % X) for i in range(X)]) for d, v in enumerate(sends)]
+    by_x = call(x_kernel, shape(Z, 16 + EXTRA, F), [VMEM] * X, name="sum_x")(own, *got)
+    by_x, rows_back = lax.optimization_barrier((by_x, rows_back))
     by_z = exchange(by_x, "z")
     weight_grad, gain_grad = call(
         last_kernel, (shape(16, F, dtype=f32), shape(1, F, dtype=f32)), [VMEM], name="sum_z"

time: 234 us -> 194 us (0.83)
  waiting for transfers between devices: 59.9 us -> 34.6 us
  blocking collectives: 133 us -> 113 us
  starting transfers between devices: 8.12 us -> 27.7 us
  between operations: 14.1 us -> 0.73 us
    all_gather x1 -> x0, waiting for transfers between devices: 29.1 us -> none  [body(): grads = lax.all_gather(grad_part, 'tp', axis=0, tiled=False)]
    all_to_all x5 -> x3, blocking collectives: 133 us -> 113 us  [exchange(): return lax.all_to_all(v, axes, split_axis=0, concat_axis=0, tiled=True)]
    ppermute x0 -> x4, waiting for transfers between devices: none -> 18.9 us  [the longest x3 16.6 us: body(): lax.ppermute(v, 'x', [(i, (i + d + 1) % X) for i in range(X)])]
    all_to_all x1 -> x2, waiting for transfers between devices: 30.7 us -> 15.8 us  [exchange(): return lax.all_to_all(v, axes, split_axis=0, concat_axis=0, tiled=True)]
    ppermute x0 -> x4, starting transfers between devices: none -> 13.1 us  [the longest x3 10.7 us: body(): lax.ppermute(v, 'x', [(i, (i + d + 1) % X) for i in range(X)])]
    all_to_all x1 -> x2, starting transfers between devices: 8.08 us -> 14.7 us  [exchange(): return lax.all_to_all(v, axes, split_axis=0, concat_axis=0, tiled=True)]
    pallas_call x5 -> x6, Pallas kernels: 10.8 us -> 10.1 us  [the longest x1 4.61 us: body(): call(grad_kernel, (shape(NP, MB, F + C), shape(ROWS, F), shape(ROWS, KV),...]
  transfers between devices with their start and end apart: 2 -> 6, of which waited for: 2 -> 4; matrix products, arithmetic and copies ran while one was open for 0% -> 0% of each run, Pallas kernels for 0% -> 2%
where the time goes in v2:
time: 194 us; the launch traced here: 193 us
  blocking collectives  113 us (58%)
  waiting for transfers between devices  34.6 us (18%)
  starting transfers between devices  27.7 us (14%)
  Pallas kernels  14.2 us (7%)
  local copies, waits for them, and re-layouts  2.54 us (1%)
    all_to_all x3, blocking collectives, exchange(): return lax.all_to_all(v, axes, split_axis=0, concat_axis=0, tiled=True)  113 us
    ppermute x3, waiting for transfers between devices, body(): lax.ppermute(v, 'x', [(i, (i + d + 1) % X) for i in range(X)])  16.6 us
    all_to_all x2, waiting for transfers between devices, exchange(): return lax.all_to_all(v, axes, split_axis=0, concat_axis=0, tiled=True)  15.8 us
    all_to_all x2, starting transfers between devices, exchange(): return lax.all_to_all(v, axes, split_axis=0, concat_axis=0, tiled=True)  14.7 us
    ppermute x3, starting transfers between devices, body(): lax.ppermute(v, 'x', [(i, (i + d + 1) % X) for i in range(X)])  10.7 us
    pallas_call x1, Pallas kernels, body(): call(grad_kernel, (shape(NP, MB, F + C), shape(ROWS, F), shape(ROWS, KV),...  4.61 us
  transfers between devices with their start and end apart: 6, of which 4 were waited for; matrix products, arithmetic and copies ran while one was open for 0% of the time, Pallas kernels for 2%

profile of v2, /device:TPU:1, one launch (start us, length us, event | category | flops | bytes accessed | tf_op | source)
XLA Modules:
  0.0 192.6 jit_solution(3888607440230767365)
XLA Ops:
  0.6 0.0 copy-start.1
  0.6 1.0 copy-done.1
  1.7 0.0 copy-start.2
  1.7 0.8 copy-done.2
  2.5 0.0 copy-start.4
  2.5 0.7 copy-done.4
  3.2 1.6 pack.1
  4.8 0.0 copy-start
  4.8 0.0 copy-start.3
  4.8 46.1 %all_to_all.25.rows.goals = bf16[64,8,1152]{2,1,0:T(8,128)(2,1)S(1)} all-to-all(bf16[64,8,1152]{2,1,0:T(8,128)(2,1)S(1)} %pack.1), channel_id=1, replica_groups=mesh['x'=4,'z'=8,'core'=2,'tp'=8] {'x','z','core'}, dimensions={0} | all-to-all | bytes 2359296 | tf_op jit(solution)/shard_map/all_to_all | solution.py:241
  50.9 0.0 copy-done
  50.9 0.0 copy-done.3
  50.9 1.9 partial_values.1
  52.8 36.2 %all_to_all.26.got = bf16[8,528,128]{2,1,0:T(8,128)(2,1)S(1)} all-to-all(bf16[8,528,128]{2,1,0:T(8,128)(2,1)S(1)} %partial_values.1), channel_id=1, replica_groups=mesh['x'=4,'z'=8,'core'=2,'tp'=8] {'tp'}, dimensions={0} | all-to-all | bytes 2162688 | tf_op jit(solution)/shard_map/all_to_all | solution.py:241
  89.0 0.8 loss.1
  89.8 30.5 %all_to_all.27.got = bf16[8,528,128]{2,1,0:T(8,128)(2,1)S(1)} all-to-all(bf16[8,528,128]{2,1,0:T(8,128)(2,1)S(1)} %get-tuple-element.23), channel_id=1, replica_groups=mesh['x'=4,'z'=8,'core'=2,'tp'=8] {'tp'}, dimensions={0} | all-to-all | bytes 2162688 | tf_op jit(solution)/shard_map/all_to_all | solution.py:241
  120.2 4.6 %grads.1 = (bf16[64,8,1152]{2,1,0:T(8,128)(2,1)}, bf16[512,1024]{1,0:T(8,128)(2,1)S(1)}, bf16[512,1024]{1,0:T(8,128)(2,1)S(1)}, f32[8,1024]{1,0:T(8,128)S(1)}) custom-call(bf16[8,528,128]{2,1,0:T(8,128)(2,1)S(1)} %all_to_all.27.got, bf16[64,8,1152]{2,1,0:T(8,128)(2,1)S(1)} %all_to_all.25.rows.goals, f32[1,1024]{1,0:T(1,128)S(1)} %copy-done.3, ...), custom_call_target="tpu_custom_call" | custom-call | flops 1073741824 | bytes 8388608 | tf_op jit(solution)/shard_map/grads/pallas_call | solution.py:271
  124.8 8.3 %all-to-all-start.3 = ((bf16[64,8,1152]{2,1,0:T(8,128)(2,1)}), bf16[64,8,1152]{2,1,0:T(8,128)(2,1)S(1)}, u32[]{:S(2)}, u32[]{:S(2)}) async-start(bf16[64,8,1152]{2,1,0:T(8,128)(2,1)} %get-tuple-element.35), calls=%async_computation.3 | async-start | bytes 2359296 | tf_op jit(solution)/shard_map/all_to_all | solution.py:241
  133.2 1.9 %share.1 = (f32[528,1024]{1,0:T(8,128)S(1)}, bf16[528,1024]{1,0:T(8,128)(2,1)S(1)}) custom-call(bf16[512,1024]{1,0:T(8,128)(2,1)S(1)} %get-tuple-element.26.grads, bf16[512,1024]{1,0:T(8,128)(2,1)S(1)} %get-tuple-element.27.normed, f32[8,1024]{1,0:T(8,128)S(1)} %get-tuple-element.28.gains), custom_call_target="tpu_custom_call" | custom-call | flops 1073741824 | bytes 4194304 | tf_op jit(solution)/shard_map/share/pallas_call | solution.py:283
  135.1 2.4 %collective-permute-start = (bf16[528,1024]{1,0:T(8,128)(2,1)S(1)}, bf16[528,1024]{1,0:T(8,128)(2,1)S(1)}, u32[]{:S(2)}, u32[]{:S(2)}) collective-permute-start(bf16[528,1024]{1,0:T(8,128)(2,1)S(1)} %get-tuple-element.30), channel_id=1, source_target_pairs={{0,8},{8,0},{1,9},{9,1},{2,10},{10,2},{3,11},{11,3},{4,12},{12,4},... | collective-permute-start | bytes 3244040 | tf_op jit(solution)/shard_map/ppermute | solution.py:290
  137.5 2.3 %collective-permute-done.got = bf16[528,1024]{1,0:T(8,128)(2,1)S(1)} collective-permute-done((bf16[528,1024]{1,0:T(8,128)(2,1)S(1)}, bf16[528,1024]{1,0:T(8,128)(2,1)S(1)}, u32[]{:S(2)}, u32[]{:S(2)}) %collective-permute-start) | collective-permute-done | bytes 1081376 | tf_op jit(solution)/shard_map/ppermute | solution.py:290
  139.8 0.2 sum_core.1
  140.0 3.2 %collective-permute-start.1 = (bf16[144,1024]{1,0:T(8,128)(2,1)S(1)}, bf16[144,1024]{1,0:T(8,128)(2,1)S(1)}, u32[]{:S(2)}, u32[]{:S(2)}) collective-permute-start(bf16[144,1024]{1,0:T(8,128)(2,1)S(1)} %get-tuple-element.32), channel_id=1, source_target_pairs={{0,128},{128,256},{256,384},{384,0},{1,129},{129,257},{257,385},{3... | collective-permute-start | bytes 884744 | tf_op jit(solution)/shard_map/ppermute | solution.py:295
  143.2 4.5 %collective-permute-start.2 = (bf16[144,1024]{1,0:T(8,128)(2,1)S(1)}, bf16[144,1024]{1,0:T(8,128)(2,1)S(1)}, u32[]{:S(2)}, u32[]{:S(2)}) collective-permute-start(bf16[144,1024]{1,0:T(8,128)(2,1)S(1)} %get-tuple-element.33), channel_id=1, source_target_pairs={{0,256},{128,384},{256,0},{384,128},{1,257},{129,385},{257,1},{385... | collective-permute-start | bytes 884744 | tf_op jit(solution)/shard_map/ppermute | solution.py:295
  147.8 3.0 %collective-permute-start.3 = (bf16[144,1024]{1,0:T(8,128)(2,1)S(1)}, bf16[144,1024]{1,0:T(8,128)(2,1)S(1)}, u32[]{:S(2)}, u32[]{:S(2)}) collective-permute-start(bf16[144,1024]{1,0:T(8,128)(2,1)S(1)} %get-tuple-element.34), channel_id=1, source_target_pairs={{0,384},{128,0},{256,128},{384,256},{1,385},{129,1},{257,129},{385... | collective-permute-start | bytes 884744 | tf_op jit(solution)/shard_map/ppermute | solution.py:295
  150.7 6.8 %collective-permute-done.1.refs_0_ = bf16[144,1024]{1,0:T(8,128)(2,1)S(1)} collective-permute-done((bf16[144,1024]{1,0:T(8,128)(2,1)S(1)}, bf16[144,1024]{1,0:T(8,128)(2,1)S(1)}, u32[]{:S(2)}, u32[]{:S(2)}) %collective-permute-start.1) | collective-permute-done | bytes 294944 | tf_op jit(solution)/shard_map/ppermute | solution.py:295
  157.5 9.8 %collective-permute-done.2.refs_1_ = bf16[144,1024]{1,0:T(8,128)(2,1)S(1)} collective-permute-done((bf16[144,1024]{1,0:T(8,128)(2,1)S(1)}, bf16[144,1024]{1,0:T(8,128)(2,1)S(1)}, u32[]{:S(2)}, u32[]{:S(2)}) %collective-permute-start.2) | collective-permute-done | bytes 294944 | tf_op jit(solution)/shard_map/ppermute | solution.py:295
  167.3 0.0 collective-permute-done.3.refs_2_
  167.3 0.0 copy-start.5
  167.3 1.0 sum_x.1
  168.3 0.0 all-to-all-done.3.got
  168.3 6.3 %all-to-all-start.4 = ((bf16[8,32,1024]{2,1,0:T(8,128)(2,1)}), bf16[8,32,1024]{2,1,0:T(8,128)(2,1)S(1)}, u32[]{:S(2)}, u32[]{:S(2)}) async-start(bf16[8,32,1024]{2,1,0:T(8,128)(2,1)} %sum_x.1), calls=%async_computation.4 | async-start | bytes 1048576 | tf_op jit(solution)/shard_map/all_to_all | solution.py:241
  174.6 0.0 copy-done.5
  174.6 1.6 unpack.1
  176.2 15.8 %all-to-all-done.4.got = bf16[8,32,1024]{2,1,0:T(8,128)(2,1)S(1)} async-done(((bf16[8,32,1024]{2,1,0:T(8,128)(2,1)}), bf16[8,32,1024]{2,1,0:T(8,128)(2,1)S(1)}, u32[]{:S(2)}, u32[]{:S(2)}) %all-to-all-start.4) | async-done | bytes 524320 | tf_op jit(solution)/shard_map/all_to_all | solution.py:241
  192.0 0.7 sum_z.1
Async XLA Ops:
  0.6 1.0 copy-start.1
  1.7 0.8 copy-start.2
  2.5 0.7 copy-start.4
  4.8 46.2 %copy-start = (bf16[1,1024,1024]{2,1,0:T(8,128)(2,1)S(1)}, bf16[1,1024,1024]{2,1,0:T(8,128)(2,1)}, u32[]{:S(2)}) copy-start(bf16[1,1024,1024]{2,1,0:T(8,128)(2,1)} %param.8) | copy-start | bytes 6291460
  4.8 46.1 %copy-start.3 = (f32[1,1024]{1,0:T(1,128)S(1)}, f32[1,1024]{1,0:T(1,128)}, u32[]{:S(2)}) copy-start(f32[1,1024]{1,0:T(1,128)} %gain.3) | copy-start | bytes 12292
  124.8 43.4 %all-to-all-start.3 = ((bf16[64,8,1152]{2,1,0:T(8,128)(2,1)}), bf16[64,8,1152]{2,1,0:T(8,128)(2,1)S(1)}, u32[]{:S(2)}, u32[]{:S(2)}) async-start(bf16[64,8,1152]{2,1,0:T(8,128)(2,1)} %get-tuple-element.35), calls=%async_computation.3 | async-start | bytes 2359296 | tf_op jit(solution)/shard_map/all_to_all | solution.py:241
  135.1 4.7 %collective-permute-start = (bf16[528,1024]{1,0:T(8,128)(2,1)S(1)}, bf16[528,1024]{1,0:T(8,128)(2,1)S(1)}, u32[]{:S(2)}, u32[]{:S(2)}) collective-permute-start(bf16[528,1024]{1,0:T(8,128)(2,1)S(1)} %get-tuple-element.30), channel_id=1, source_target_pairs={{0,8},{8,0},{1,9},{9,1},{2,10},{10,2},{3,11},{11,3},{4,12},{12,4},... | collective-permute-start | bytes 3244040 | tf_op jit(solution)/shard_map/ppermute | solution.py:290
  140.0 17.5 %collective-permute-start.1 = (bf16[144,1024]{1,0:T(8,128)(2,1)S(1)}, bf16[144,1024]{1,0:T(8,128)(2,1)S(1)}, u32[]{:S(2)}, u32[]{:S(2)}) collective-permute-start(bf16[144,1024]{1,0:T(8,128)(2,1)S(1)} %get-tuple-element.32), channel_id=1, source_target_pairs={{0,128},{128,256},{256,384},{384,0},{1,129},{129,257},{257,385},{3... | collective-permute-start | bytes 884744 | tf_op jit(solution)/shard_map/ppermute | solution.py:295
  143.2 24.1 %collective-permute-start.2 = (bf16[144,1024]{1,0:T(8,128)(2,1)S(1)}, bf16[144,1024]{1,0:T(8,128)(2,1)S(1)}, u32[]{:S(2)}, u32[]{:S(2)}) collective-permute-start(bf16[144,1024]{1,0:T(8,128)(2,1)S(1)} %get-tuple-element.33), channel_id=1, source_target_pairs={{0,256},{128,384},{256,0},{384,128},{1,257},{129,385},{257,1},{385... | collective-permute-start | bytes 884744 | tf_op jit(solution)/shard_map/ppermute | solution.py:295
  147.8 19.5 %collective-permute-start.3 = (bf16[144,1024]{1,0:T(8,128)(2,1)S(1)}, bf16[144,1024]{1,0:T(8,128)(2,1)S(1)}, u32[]{:S(2)}, u32[]{:S(2)}) collective-permute-start(bf16[144,1024]{1,0:T(8,128)(2,1)S(1)} %get-tuple-element.34), channel_id=1, source_target_pairs={{0,384},{128,0},{256,128},{384,256},{1,385},{129,1},{257,129},{385... | collective-permute-start | bytes 884744 | tf_op jit(solution)/shard_map/ppermute | solution.py:295
  167.3 7.3 %copy-start.5 = (s32[32,1]{0,1:T(1,128)S(1)}, s32[32,1]{0,1:T(1,128)}, u32[]{:S(2)}) copy-start(s32[32,1]{0,1:T(1,128)} %param.7) | copy-start | bytes 388
  168.3 23.7 %all-to-all-start.4 = ((bf16[8,32,1024]{2,1,0:T(8,128)(2,1)}), bf16[8,32,1024]{2,1,0:T(8,128)(2,1)S(1)}, u32[]{:S(2)}, u32[]{:S(2)}) async-start(bf16[8,32,1024]{2,1,0:T(8,128)(2,1)} %sum_x.1), calls=%async_computation.4 | async-start | bytes 1048576 | tf_op jit(solution)/shard_map/all_to_all | solution.py:241

commit v3 on v2

--- a/solution.py
+++ b/solution.py
@@ -24,7 +24,7 @@
 f32 = jnp.float32
 bf16 = jnp.bfloat16
 VMEM = pl.BlockSpec(memory_space=pltpu.VMEM)
-ANY = pl.BlockSpec(memory_space=pl.ANY)
+HBM = pl.BlockSpec(memory_space=pltpu.HBM)
 SMEM = pl.BlockSpec(memory_space=pltpu.SMEM)
 
 
@@ -78,7 +78,7 @@
     pltpu.make_async_copy(goals, out.at[pl.ds(0, PIECES), :, pl.ds(F, C)], goal_sem).wait()
 
 
-def value_kernel(rows, gain, weights, out, squares):
+def value_kernel(rows, gain, weights, out, gained, squares):
     def tile(i, _):
         x = rows[pl.ds(i * 16, 16), :, :F].astype(f32).reshape(TILE, F)
         sq = x * x
@@ -86,12 +86,14 @@
         for j in range(1, F // 128):
             folded = folded + sq[:, j * 128 : (j + 1) * 128]
         squares[pl.ds(i, 1), :] = to_lanes(folded)
-        partial = jnp.dot((x * gain[...]).astype(bf16), weights[...], preferred_element_type=f32)
-        for t in range(NT):
-            out[t, pl.ds(pl.multiple_of(i * TILE, TILE), TILE), :] = partial[:, t * C : (t + 1) * C].astype(bf16)
+        gained[pl.ds(pl.multiple_of(i * TILE, TILE), TILE), :] = (x * gain[...]).astype(bf16)
         return 0
 
     lax.fori_loop(0, NTILES, tile, 0)
+    for i in range(KV // 256):
+        partial = jnp.dot(gained[...], weights[:, i * 256 : (i + 1) * 256], preferred_element_type=f32).astype(bf16)
+        out[2 * i, :ROWS, :] = partial[:, :C]
+        out[2 * i + 1, :ROWS, :] = partial[:, C:]
     high, mid, low = parts(squares[0:4, :])
     tail = jnp.concatenate([high, mid, low, jnp.zeros_like(high)], axis=0).astype(bf16)
     for t in range(NT):
@@ -127,33 +129,40 @@
         send[t, ROWS:, :] = tail
 
 
-def grad_kernel(got, rows, gain, weights, scales, value, back, normed, grads, gains, dots):
+def normed_kernel(rows, gain, scales, normed):
+    def tile(i, _):
+        scale = to_rows(scales[pl.ds(i, 1), :])[:, :1]
+        normal = rows[pl.ds(i * 16, 16), :, :F].astype(f32).reshape(TILE, F) * scale
+        normed[pl.ds(pl.multiple_of(i * TILE, TILE), TILE), :] = (normal * gain[...]).astype(bf16)
+        return 0
+
+    lax.fori_loop(0, NTILES, tile, 0)
+
+
+def grad_kernel(got, rows, gain, weights, scales, value, back, grads, gains, scale_of, dot_of):
     tail = got[0, ROWS:, :].astype(f32)
     for t in range(1, NT):
         tail = tail + got[t, ROWS:, :].astype(f32)
-    dots[0:4, :] = (tail[0:4] + tail[4:8] + tail[8:12]) / D
-    gains[...] = jnp.zeros_like(gains)
-
-    def tile(i, _):
-        here = pl.ds(pl.multiple_of(i * TILE, TILE), TILE)
-        slots = pl.ds(i * 16, 16)
-        for t in range(NT):
-            grads[here, t * C : (t + 1) * C] = got[t, here, :]
+    dots = (tail[0:4] + tail[4:8] + tail[8:12]) / D
+    for i in range(NTILES):
+        here = slice(i * TILE, (i + 1) * TILE)
+        scale = scales[i : i + 1, :]
+        scale_of[here, :] = to_rows(scale)
+        dot_of[here, :] = to_rows(scale * scale * dots[i : i + 1, :])
+    for t in range(NT):
+        grads[:, t * C : (t + 1) * C] = got[t, :ROWS, :]
+    back[:, :, F:] = value[...]
+
+    for i in range(F // 256):
+        at = slice(i * 256, (i + 1) * 256)
         grad_normed = lax.dot_general(
-            grads[here, :], weights[...], (((1,), (1,)), ((), ())), preferred_element_type=f32
+            grads[...], weights[at, :], (((1,), (1,)), ((), ())), preferred_element_type=f32
         )
-        scale = to_rows(scales[pl.ds(i, 1), :])[:, :1]
-        dot = to_rows(dots[pl.ds(i, 1), :])[:, :1]
-        normal = rows[slots, :, :F].astype(f32).reshape(TILE, F) * scale
-        gained = grad_normed * gain[...]
-        row_grad = scale * (gained - normal * dot)
-        back[slots, :, :F] = row_grad.reshape(16, MB, F).astype(bf16)
-        back[slots, :, F:] = value[slots]
-        gains[...] += jnp.sum((grad_normed * normal).reshape(TILE // 8, 8, F), axis=0)
-        normed[here, :] = (normal * gain[...]).astype(bf16)
-        return 0
-
-    lax.fori_loop(0, NTILES, tile, 0)
+        scaled = grad_normed * scale_of[:, :1]
+        x = rows[:, :, at].astype(f32).reshape(ROWS, 256)
+        row_grad = scaled * gain[:, at] - x * dot_of[:, :1]
+        back[:, :, at] = row_grad.reshape(NP, MB, 256).astype(bf16)
+        gains[:, at] = jnp.sum((scaled * x).reshape(ROWS // 8, 8, 256), axis=0)
 
 
 def share_kernel(grads, normed, gains, keep, send):
@@ -177,50 +186,61 @@
     lax.fori_loop(0, KV // 256, block, 0)
     total = jnp.sum(gains[...], axis=0, keepdims=True)
     keep[KV // 2 :, :] = jnp.concatenate([total, jnp.zeros((EXTRA - 1, F), f32)], axis=0)
-    send[KV // 2 :, :] = gain_tail(total)
+    high, mid, low = parts(total)
+    tail = jnp.concatenate([high, mid, low, jnp.zeros((EXTRA - 3, F), f32)], axis=0)
+    send[KV // 2 :, :] = tail.astype(bf16)
 
 
 def gain_tail(total):
-    high, mid, low = parts(total)
-    return jnp.concatenate([high, mid, low, jnp.zeros((EXTRA - 3, F), f32)], axis=0).astype(bf16)
+    high = total.astype(bf16).astype(f32)
+    return jnp.concatenate([high, total - high], axis=0).astype(bf16)
 
 
 def core_kernel(keep, got, own, *sends):
     me = lax.axis_index("x")
     tail = keep[KV // 2 :, :] + got[KV // 2 :, :].astype(f32)
     tail = jnp.sum(tail, axis=0, keepdims=True)
-    here = pl.ds(pl.multiple_of(me * 128, 128), 128)
-    own[:128, :] = keep[here, :] + got[here, :].astype(f32)
-    own[128:, :] = jnp.concatenate([tail, jnp.zeros((EXTRA - 1, F), f32)], axis=0)
-    tail = gain_tail(tail)
+    tail = jnp.concatenate([tail[:, j * 128 : (j + 1) * 128] for j in range(F // 128)], axis=0)
+
+    def put(out, d, tail):
+        there = pl.ds(pl.multiple_of(lax.rem(me + d, X) * 128, 128), 128)
+        total = keep[there, :] + got[there, :].astype(f32)
+        for j in range(F // 128):
+            out[j * 128 : (j + 1) * 128, :] = total[:, j * 128 : (j + 1) * 128].astype(out.dtype)
+        out[F:, :] = tail
+
     for d, send in enumerate(sends):
-        there = pl.ds(pl.multiple_of(lax.rem(me + d + 1, X) * 128, 128), 128)
-        send[:128, :] = (keep[there, :] + got[there, :].astype(f32)).astype(bf16)
-        send[128:, :] = tail
+        put(send, d + 1, gain_tail(tail))
+    put(own, 0, jnp.concatenate([tail, jnp.zeros_like(tail)], axis=0))
 
 
 def x_kernel(own, *refs):
     *got, out = refs
-    for i in range(Z):
-        at = slice(i * 16, (i + 1) * 16)
-        total = own[at, :]
-        for g in got:
-            total = total + g[at, :].astype(f32)
-        out[i, :16, :] = total.astype(bf16)
-    tail = own[128:, :]
+    for z in range(Z):
+        for j in range(F // 128):
+            at = slice(j * 128 + z * 16, j * 128 + z * 16 + 16)
+            total = own[at, :]
+            for g in got:
+                total = total + g[at, :].astype(f32)
+            out[z, j * 16 : (j + 1) * 16, :] = total.astype(bf16)
+    tail = own[F:, :]
     for g in got:
-        tail = tail + g[128:, :].astype(f32)
-    tail = gain_tail(jnp.sum(tail, axis=0, keepdims=True))
-    for i in range(Z):
-        out[i, 16:, :] = tail
+        tail = tail + g[F:, :].astype(f32)
+    tail = gain_tail(tail[:8] + tail[8:])
+    for z in range(Z):
+        out[z, 128:, :] = tail
 
 
 def last_kernel(got, weight_out, gain_out):
     total = got[0].astype(f32)
-    for g in range(1, Z):
-        total = total + got[g].astype(f32)
-    weight_out[...] = total[:16] * GRAD_SCALE
-    gain_out[...] = jnp.sum(total[16:], axis=0, keepdims=True) * GRAD_SCALE
+    for z in range(1, Z):
+        total = total + got[z].astype(f32)
+    total = total * GRAD_SCALE
+    tail = total[128:136] + total[136:]
+    for j in range(F // 128):
+        at = slice(j * 128, (j + 1) * 128)
+        weight_out[:, at] = total[j * 16 : (j + 1) * 16]
+        gain_out[:, at] = tail[j : j + 1]
 
 
 def unpack_kernel(routes, got, rows, values):
@@ -245,19 +265,20 @@
     peer = ("x", "z", "core")
     weights = value_weights[0]
     order = routes[:, 0]
+    given = order, activations.reshape(PIECES, MB, F), targets.reshape(PIECES, MB, C)
     sends = call(
         pack_kernel,
         shape(NP, MB, F + C),
-        [ANY] * 3,
+        [HBM] * 3,
         [pltpu.SMEM((PIECES,), jnp.int32)] + [pltpu.SemaphoreType.DMA] * 3,
         name="pack",
-    )(order, activations.reshape(PIECES, MB, F), targets.reshape(PIECES, MB, C))
+    )(*[pltpu.with_memory_space_constraint(v, pltpu.HBM) for v in given])
     arrived = exchange(sends, peer)
     partials = call(
         value_kernel,
         shape(NT, ROWS + EXTRA, C),
         [VMEM] * 3,
-        [pltpu.VMEM((8, 128), f32)],
+        [pltpu.VMEM((ROWS, F), bf16), pltpu.VMEM((8, 128), f32)],
         flops=2 * ROWS * F * KV,
         name="partial_values",
     )(arrived, norm_gains, weights)
@@ -268,11 +289,12 @@
         [pltpu.VMEM((8, 128), f32)],
         name="loss",
     )(exchange(partials, "tp"), arrived)
-    back, normed, grads, gains = call(
+    normed = call(normed_kernel, shape(ROWS, F), [VMEM] * 3, name="normed")(arrived, norm_gains, scales)
+    back, grads, gains = call(
         grad_kernel,
-        (shape(NP, MB, F + C), shape(ROWS, F), shape(ROWS, KV), shape(8, F, dtype=f32)),
+        (shape(NP, MB, F + C), shape(ROWS, KV), shape(8, F, dtype=f32)),
         [VMEM] * 6,
-        [pltpu.VMEM((8, 128), f32)],
+        [pltpu.VMEM((ROWS, 128), f32)] * 2,
         flops=2 * ROWS * F * KV,
         size=8 << 20,
         name="grads",
@@ -288,12 +310,12 @@
         name="share",
     )(grads, normed, gains)
     got = lax.ppermute(send, "core", [(0, 1), (1, 0)])
-    block = (KV // CORES // X + EXTRA, F)
+    block = (F + EXTRA, 128)
     own, *sends = call(
         core_kernel, (shape(*block, dtype=f32),) + (shape(*block),) * (X - 1), [VMEM] * 2, name="sum_core"
     )(keep, got)
     got = [lax.ppermute(v, "x", [(i, (i + d + 1) % X) for i in range(X)]) for d, v in enumerate(sends)]
-    by_x = call(x_kernel, shape(Z, 16 + EXTRA, F), [VMEM] * X, name="sum_x")(own, *got)
+    by_x = call(x_kernel, shape(Z, 128 + EXTRA, 128), [VMEM] * X, name="sum_x")(own, *got)
     by_x, rows_back = lax.optimization_barrier((by_x, rows_back))
     by_z = exchange(by_x, "z")
     weight_grad, gain_grad = call(

time: 194 us -> 184 us (0.948); the launches traced: 193 us -> 181 us
  waiting for transfers between devices: 34.6 us -> 26.7 us
  local copies, waits for them, and re-layouts: 2.54 us -> 0.02 us
    all_to_all x2, waiting for transfers between devices: 15.8 us -> 9.09 us  [exchange(): return lax.all_to_all(v, axes, split_axis=0, concat_axis=0, tiled=True)]
    unnamed x12 -> x6, local copies, waits for them, and re-layouts: 2.54 us -> 0.02 us
    pallas_call x4 -> x5, Pallas kernels: 9.06 us -> 8.08 us  [the longest x1 2.75 us: body(): call(grad_kernel, (shape(NP, MB, F + C), shape(ROWS, KV), shape(8, F, dty...]
  transfers between devices with their start and end apart: 6 -> 6, of which waited for: 4 -> 4; matrix products, arithmetic and copies ran while one was open for 0% -> 0% of each run, Pallas kernels for 2% -> 3%
where the time goes in v3:
time: 184 us; the launch traced here: 181 us
  blocking collectives  113 us (61%)
  starting transfers between devices  27 us (15%)
  waiting for transfers between devices  26.7 us (15%)
  Pallas kernels  13.2 us (7%)
    all_to_all x3, blocking collectives, exchange(): return lax.all_to_all(v, axes, split_axis=0, concat_axis=0, tiled=True)  113 us
    ppermute x3, waiting for transfers between devices, body(): lax.ppermute(v, 'x', [(i, (i + d + 1) % X) for i in range(X)])  15.3 us
    all_to_all x2, starting transfers between devices, exchange(): return lax.all_to_all(v, axes, split_axis=0, concat_axis=0, tiled=True)  13.9 us
    ppermute x3, starting transfers between devices, body(): lax.ppermute(v, 'x', [(i, (i + d + 1) % X) for i in range(X)])  10.7 us
    all_to_all x2, waiting for transfers between devices, exchange(): return lax.all_to_all(v, axes, split_axis=0, concat_axis=0, tiled=True)  9.09 us
  transfers between devices with their start and end apart: 6, of which 4 were waited for; matrix products, arithmetic and copies ran while one was open for 0% of the time, Pallas kernels for 3%

profile of v3, /device:TPU:1, one launch (start us, length us, event | category | flops | bytes accessed | tf_op | source)
XLA Modules:
  0.0 180.5 jit_solution(3132963864227060214)
XLA Ops:
  0.6 1.8 %pack.1 = bf16[64,8,1152]{2,1,0:T(8,128)(2,1)S(1)} custom-call(s32[32]{0:T(128)} %bitcast.9, bf16[32,8,1024]{2,1,0:T(8,128)(2,1)} %bitcast.11, bf16[32,8,128]{2,1,0:T(8,128)(2,1)} %bitcast.12), custom_call_target="tpu_custom_call" | custom-call | bytes 4194304 | tf_op jit(solution)/shard_map/pack/pallas_call | solution.py:269
  2.5 0.0 copy-start
  2.5 0.0 copy-start.1
  2.5 46.1 %all_to_all.25.rows.goals = bf16[64,8,1152]{2,1,0:T(8,128)(2,1)S(1)} all-to-all(bf16[64,8,1152]{2,1,0:T(8,128)(2,1)S(1)} %pack.1), channel_id=1, replica_groups=mesh['x'=4,'z'=8,'core'=2,'tp'=8] {'x','z','core'}, dimensions={0} | all-to-all | bytes 2359296 | tf_op jit(solution)/shard_map/all_to_all | solution.py:261
  48.6 0.0 copy-done
  48.6 0.0 copy-done.1
  48.6 1.9 %partial_values.1 = bf16[8,528,128]{2,1,0:T(8,128)(2,1)S(1)} custom-call(bf16[64,8,1152]{2,1,0:T(8,128)(2,1)S(1)} %all_to_all.25.rows.goals, f32[1,1024]{1,0:T(1,128)S(1)} %copy-done.1, bf16[1024,1024]{1,0:T(8,128)(2,1)S(1)} %bitcast.7), custom_call_target="tpu_custom_call" | custom-call | flops 1073741824 | bytes 4194304 | tf_op jit(solution)/shard_map/partial_values/pallas_call | solution.py:277
  50.5 36.2 %all_to_all.26.got = bf16[8,528,128]{2,1,0:T(8,128)(2,1)S(1)} all-to-all(bf16[8,528,128]{2,1,0:T(8,128)(2,1)S(1)} %partial_values.1), channel_id=1, replica_groups=mesh['x'=4,'z'=8,'core'=2,'tp'=8] {'tp'}, dimensions={0} | all-to-all | bytes 2162688 | tf_op jit(solution)/shard_map/all_to_all | solution.py:261
  86.7 0.8 loss.1
  87.4 30.5 %all_to_all.27.got = bf16[8,528,128]{2,1,0:T(8,128)(2,1)S(1)} all-to-all(bf16[8,528,128]{2,1,0:T(8,128)(2,1)S(1)} %get-tuple-element.22), channel_id=1, replica_groups=mesh['x'=4,'z'=8,'core'=2,'tp'=8] {'tp'}, dimensions={0} | all-to-all | bytes 2162688 | tf_op jit(solution)/shard_map/all_to_all | solution.py:261
  117.9 2.8 %grads.1 = (bf16[64,8,1152]{2,1,0:T(8,128)(2,1)}, bf16[512,1024]{1,0:T(8,128)(2,1)S(1)}, f32[8,1024]{1,0:T(8,128)S(1)}) custom-call(bf16[8,528,128]{2,1,0:T(8,128)(2,1)S(1)} %all_to_all.27.got, bf16[64,8,1152]{2,1,0:T(8,128)(2,1)S(1)} %all_to_all.25.rows.goals, f32[1,1024]{1,0:T(1,128)S(1)} %copy-done.1, bf16[1024,1024]{1,0:T(8,128)(2,1)S(1)} %bitcast.8, ...), custom_call_target="tpu_custom_call" | custom-call | flops 1073741824 | bytes 8388608 | tf_op jit(solution)/shard_map/grads/pallas_call | solution.py:293
  120.6 8.3 %all-to-all-start.3 = ((bf16[64,8,1152]{2,1,0:T(8,128)(2,1)}), bf16[64,8,1152]{2,1,0:T(8,128)(2,1)S(1)}, u32[]{:S(2)}, u32[]{:S(2)}) async-start(bf16[64,8,1152]{2,1,0:T(8,128)(2,1)} %get-tuple-element.33), calls=%async_computation.3 | async-start | bytes 2359296 | tf_op jit(solution)/shard_map/all_to_all | solution.py:261
  129.0 0.8 normed.1
  129.8 1.9 %share.1 = (f32[528,1024]{1,0:T(8,128)S(1)}, bf16[528,1024]{1,0:T(8,128)(2,1)S(1)}) custom-call(bf16[512,1024]{1,0:T(8,128)(2,1)S(1)} %get-tuple-element.25.grads, bf16[512,1024]{1,0:T(8,128)(2,1)S(1)} %normed.1, f32[8,1024]{1,0:T(8,128)S(1)} %get-tuple-element.26.gains), custom_call_target="tpu_custom_call" | custom-call | flops 1073741824 | bytes 4194304 | tf_op jit(solution)/shard_map/share/pallas_call | solution.py:305
  131.7 2.4 %collective-permute-start = (bf16[528,1024]{1,0:T(8,128)(2,1)S(1)}, bf16[528,1024]{1,0:T(8,128)(2,1)S(1)}, u32[]{:S(2)}, u32[]{:S(2)}) collective-permute-start(bf16[528,1024]{1,0:T(8,128)(2,1)S(1)} %get-tuple-element.28), channel_id=1, source_target_pairs={{0,8},{8,0},{1,9},{9,1},{2,10},{10,2},{3,11},{11,3},{4,12},{12,4},... | collective-permute-start | bytes 3244040 | tf_op jit(solution)/shard_map/ppermute | solution.py:312
  134.1 2.3 %collective-permute-done.got = bf16[528,1024]{1,0:T(8,128)(2,1)S(1)} collective-permute-done((bf16[528,1024]{1,0:T(8,128)(2,1)S(1)}, bf16[528,1024]{1,0:T(8,128)(2,1)S(1)}, u32[]{:S(2)}, u32[]{:S(2)}) %collective-permute-start) | collective-permute-done | bytes 1081376 | tf_op jit(solution)/shard_map/ppermute | solution.py:312
  136.4 0.2 sum_core.1
  136.6 0.0 copy-start.2
  136.6 3.2 %collective-permute-start.1 = (bf16[1040,128]{1,0:T(8,128)(2,1)S(1)}, bf16[1040,128]{1,0:T(8,128)(2,1)S(1)}, u32[]{:S(2)}, u32[]{:S(2)}) collective-permute-start(bf16[1040,128]{1,0:T(8,128)(2,1)S(1)} %get-tuple-element.30), channel_id=1, source_target_pairs={{0,128},{128,256},{256,384},{384,0},{1,129},{129,257},{257,385},{3... | collective-permute-start | bytes 798728 | tf_op jit(solution)/shard_map/ppermute | solution.py:317
  139.8 4.5 %collective-permute-start.2 = (bf16[1040,128]{1,0:T(8,128)(2,1)S(1)}, bf16[1040,128]{1,0:T(8,128)(2,1)S(1)}, u32[]{:S(2)}, u32[]{:S(2)}) collective-permute-start(bf16[1040,128]{1,0:T(8,128)(2,1)S(1)} %get-tuple-element.31), channel_id=1, source_target_pairs={{0,256},{128,384},{256,0},{384,128},{1,257},{129,385},{257,1},{385... | collective-permute-start | bytes 798728 | tf_op jit(solution)/shard_map/ppermute | solution.py:317
  144.4 3.0 %collective-permute-start.3 = (bf16[1040,128]{1,0:T(8,128)(2,1)S(1)}, bf16[1040,128]{1,0:T(8,128)(2,1)S(1)}, u32[]{:S(2)}, u32[]{:S(2)}) collective-permute-start(bf16[1040,128]{1,0:T(8,128)(2,1)S(1)} %get-tuple-element.32), channel_id=1, source_target_pairs={{0,384},{128,0},{256,128},{384,256},{1,385},{129,1},{257,129},{385... | collective-permute-start | bytes 798728 | tf_op jit(solution)/shard_map/ppermute | solution.py:317
  147.3 5.4 %collective-permute-done.1.refs_0_ = bf16[1040,128]{1,0:T(8,128)(2,1)S(1)} collective-permute-done((bf16[1040,128]{1,0:T(8,128)(2,1)S(1)}, bf16[1040,128]{1,0:T(8,128)(2,1)S(1)}, u32[]{:S(2)}, u32[]{:S(2)}) %collective-permute-start.1) | collective-permute-done | bytes 266272 | tf_op jit(solution)/shard_map/ppermute | solution.py:317
  152.8 9.9 %collective-permute-done.2.refs_1_ = bf16[1040,128]{1,0:T(8,128)(2,1)S(1)} collective-permute-done((bf16[1040,128]{1,0:T(8,128)(2,1)S(1)}, bf16[1040,128]{1,0:T(8,128)(2,1)S(1)}, u32[]{:S(2)}, u32[]{:S(2)}) %collective-permute-start.2) | collective-permute-done | bytes 266272 | tf_op jit(solution)/shard_map/ppermute | solution.py:317
  162.7 0.0 collective-permute-done.3.refs_2_
  162.7 0.9 sum_x.1
  163.6 0.0 all-to-all-done.3.got
  163.6 5.6 %all-to-all-start.4 = ((bf16[8,144,128]{2,1,0:T(8,128)(2,1)}), bf16[8,144,128]{2,1,0:T(8,128)(2,1)S(1)}, u32[]{:S(2)}, u32[]{:S(2)}) async-start(bf16[8,144,128]{2,1,0:T(8,128)(2,1)} %sum_x.1), calls=%async_computation.4 | async-start | bytes 589824 | tf_op jit(solution)/shard_map/all_to_all | solution.py:261
  169.2 0.0 copy-done.2
  169.2 1.6 unpack.1
  170.8 9.1 %all-to-all-done.4.got = bf16[8,144,128]{2,1,0:T(8,128)(2,1)S(1)} async-done(((bf16[8,144,128]{2,1,0:T(8,128)(2,1)}), bf16[8,144,128]{2,1,0:T(8,128)(2,1)S(1)}, u32[]{:S(2)}, u32[]{:S(2)}) %all-to-all-start.4) | async-done | bytes 294944 | tf_op jit(solution)/shard_map/all_to_all | solution.py:261
  179.8 0.7 sum_z.1
Async XLA Ops:
  2.5 46.2 %copy-start = (bf16[1,1024,1024]{2,1,0:T(8,128)(2,1)S(1)}, bf16[1,1024,1024]{2,1,0:T(8,128)(2,1)}, u32[]{:S(2)}) copy-start(bf16[1,1024,1024]{2,1,0:T(8,128)(2,1)} %param.8) | copy-start | bytes 6291460
  2.5 46.1 %copy-start.1 = (f32[1,1024]{1,0:T(1,128)S(1)}, f32[1,1024]{1,0:T(1,128)}, u32[]{:S(2)}) copy-start(f32[1,1024]{1,0:T(1,128)} %gain.5) | copy-start | bytes 12292
  120.6 42.9 %all-to-all-start.3 = ((bf16[64,8,1152]{2,1,0:T(8,128)(2,1)}), bf16[64,8,1152]{2,1,0:T(8,128)(2,1)S(1)}, u32[]{:S(2)}, u32[]{:S(2)}) async-start(bf16[64,8,1152]{2,1,0:T(8,128)(2,1)} %get-tuple-element.33), calls=%async_computation.3 | async-start | bytes 2359296 | tf_op jit(solution)/shard_map/all_to_all | solution.py:261
  131.7 4.7 %collective-permute-start = (bf16[528,1024]{1,0:T(8,128)(2,1)S(1)}, bf16[528,1024]{1,0:T(8,128)(2,1)S(1)}, u32[]{:S(2)}, u32[]{:S(2)}) collective-permute-start(bf16[528,1024]{1,0:T(8,128)(2,1)S(1)} %get-tuple-element.28), channel_id=1, source_target_pairs={{0,8},{8,0},{1,9},{9,1},{2,10},{10,2},{3,11},{11,3},{4,12},{12,4},... | collective-permute-start | bytes 3244040 | tf_op jit(solution)/shard_map/ppermute | solution.py:312
  136.6 32.5 %copy-start.2 = (s32[32,1]{0,1:T(1,128)S(1)}, s32[32,1]{0,1:T(1,128)}, u32[]{:S(2)}) copy-start(s32[32,1]{0,1:T(1,128)} %param.7) | copy-start | bytes 388
  136.6 16.1 %collective-permute-start.1 = (bf16[1040,128]{1,0:T(8,128)(2,1)S(1)}, bf16[1040,128]{1,0:T(8,128)(2,1)S(1)}, u32[]{:S(2)}, u32[]{:S(2)}) collective-permute-start(bf16[1040,128]{1,0:T(8,128)(2,1)S(1)} %get-tuple-element.30), channel_id=1, source_target_pairs={{0,128},{128,256},{256,384},{384,0},{1,129},{129,257},{257,385},{3... | collective-permute-start | bytes 798728 | tf_op jit(solution)/shard_map/ppermute | solution.py:317
  139.8 22.8 %collective-permute-start.2 = (bf16[1040,128]{1,0:T(8,128)(2,1)S(1)}, bf16[1040,128]{1,0:T(8,128)(2,1)S(1)}, u32[]{:S(2)}, u32[]{:S(2)}) collective-permute-start(bf16[1040,128]{1,0:T(8,128)(2,1)S(1)} %get-tuple-element.31), channel_id=1, source_target_pairs={{0,256},{128,384},{256,0},{384,128},{1,257},{129,385},{257,1},{385... | collective-permute-start | bytes 798728 | tf_op jit(solution)/shard_map/ppermute | solution.py:317
  144.4 18.3 %collective-permute-start.3 = (bf16[1040,128]{1,0:T(8,128)(2,1)S(1)}, bf16[1040,128]{1,0:T(8,128)(2,1)S(1)}, u32[]{:S(2)}, u32[]{:S(2)}) collective-permute-start(bf16[1040,128]{1,0:T(8,128)(2,1)S(1)} %get-tuple-element.32), channel_id=1, source_target_pairs={{0,384},{128,0},{256,128},{384,256},{1,385},{129,1},{257,129},{385... | collective-permute-start | bytes 798728 | tf_op jit(solution)/shard_map/ppermute | solution.py:317
  163.6 16.3 %all-to-all-start.4 = ((bf16[8,144,128]{2,1,0:T(8,128)(2,1)}), bf16[8,144,128]{2,1,0:T(8,128)(2,1)S(1)}, u32[]{:S(2)}, u32[]{:S(2)}) async-start(bf16[8,144,128]{2,1,0:T(8,128)(2,1)} %sum_x.1), calls=%async_computation.4 | async-start | bytes 589824 | tf_op jit(solution)/shard_map/all_to_all | solution.py:261

commit v4 on v3

--- a/solution.py
+++ b/solution.py
@@ -1,3 +1,5 @@
+import functools
+
 import jax
 import jax.numpy as jnp
 from jax import lax
@@ -35,7 +37,7 @@
         in_specs=in_specs,
         out_specs=jax.tree.map(lambda _: VMEM, outs),
         scratch_shapes=scratch,
-        compiler_params=pltpu.CompilerParams(vmem_limit_bytes=40 << 20),
+        compiler_params=pltpu.CompilerParams(vmem_limit_bytes=18 << 20),
         cost_estimate=pl.CostEstimate(flops=flops, bytes_accessed=size, transcendentals=0),
         name=name,
     )
@@ -129,17 +131,44 @@
         send[t, ROWS:, :] = tail
 
 
-def normed_kernel(rows, gain, scales, normed):
+def normal_kernel(rows, scales, normal):
     def tile(i, _):
         scale = to_rows(scales[pl.ds(i, 1), :])[:, :1]
-        normal = rows[pl.ds(i * 16, 16), :, :F].astype(f32).reshape(TILE, F) * scale
-        normed[pl.ds(pl.multiple_of(i * TILE, TILE), TILE), :] = (normal * gain[...]).astype(bf16)
+        x = rows[pl.ds(i * 16, 16), :, :F].astype(f32).reshape(TILE, F)
+        normal[pl.ds(pl.multiple_of(i * TILE, TILE), TILE), :] = (x * scale).astype(bf16)
         return 0
 
     lax.fori_loop(0, NTILES, tile, 0)
 
 
-def grad_kernel(got, rows, gain, weights, scales, value, back, grads, gains, scale_of, dot_of):
+def share_kernel(got, normal, gain, flipped, keep, send, grads, gains):
+    first = lax.axis_index("core") == 0
+    gains[...] = jnp.zeros_like(gains)
+
+    def block(i, _):
+        both = jnp.concatenate([got[2 * i, :ROWS, :], got[2 * i + 1, :ROWS, :]], axis=1)
+        grads[i] = both
+        mine = lax.dot_general(both, normal[...], (((0,), (0,)), ((), ())), preferred_element_type=f32)
+        here = pl.ds(pl.multiple_of(i * 256, 256), 256)
+        gains[...] += jnp.sum((mine * flipped[here, :].astype(f32)).reshape(32, 8, F), axis=0)
+        mine = mine * gain[...]
+        for j in range(8):
+            at = pl.ds(pl.multiple_of(i * 128 + j * 16, 16), 16)
+            even = mine[j * 32 : j * 32 + 16, :]
+            odd = mine[j * 32 + 16 : j * 32 + 32, :]
+            keep[at, :] = jnp.where(first, even, odd)
+            send[at, :] = jnp.where(first, odd, even).astype(bf16)
+        return 0
+
+    lax.fori_loop(0, KV // 256, block, 0)
+    total = jnp.sum(gains[...], axis=0, keepdims=True)
+    keep[KV // 2 :, :] = jnp.concatenate([total, jnp.zeros((EXTRA - 1, F), f32)], axis=0)
+    high, mid, low = parts(total)
+    tail = jnp.concatenate([high, mid, low, jnp.zeros((EXTRA - 3, F), f32)], axis=0)
+    send[KV // 2 :, :] = tail.astype(bf16)
+
+
+def grad_kernel(got, grads, rows, gain, flipped, scales, value, back, scale_of, dot_of):
     tail = got[0, ROWS:, :].astype(f32)
     for t in range(1, NT):
         tail = tail + got[t, ROWS:, :].astype(f32)
@@ -149,51 +178,27 @@
         scale = scales[i : i + 1, :]
         scale_of[here, :] = to_rows(scale)
         dot_of[here, :] = to_rows(scale * scale * dots[i : i + 1, :])
-    for t in range(NT):
-        grads[:, t * C : (t + 1) * C] = got[t, :ROWS, :]
     back[:, :, F:] = value[...]
 
     for i in range(F // 256):
         at = slice(i * 256, (i + 1) * 256)
-        grad_normed = lax.dot_general(
-            grads[...], weights[at, :], (((1,), (1,)), ((), ())), preferred_element_type=f32
-        )
-        scaled = grad_normed * scale_of[:, :1]
+        grad_normed = jnp.zeros((ROWS, 256), f32)
+        for k in range(KV // 256):
+            grad_normed += jnp.dot(
+                grads[k], flipped[k * 256 : (k + 1) * 256, at], preferred_element_type=f32
+            )
         x = rows[:, :, at].astype(f32).reshape(ROWS, 256)
-        row_grad = scaled * gain[:, at] - x * dot_of[:, :1]
+        row_grad = grad_normed * scale_of[:, :1] * gain[:, at] - x * dot_of[:, :1]
         back[:, :, at] = row_grad.reshape(NP, MB, 256).astype(bf16)
-        gains[:, at] = jnp.sum((scaled * x).reshape(ROWS // 8, 8, 256), axis=0)
-
-
-def share_kernel(grads, normed, gains, keep, send):
-    first = lax.axis_index("core") == 0
-
-    def block(i, _):
-        mine = lax.dot_general(
-            grads[:, pl.ds(pl.multiple_of(i * 256, 256), 256)],
-            normed[...],
-            (((0,), (0,)), ((), ())),
-            preferred_element_type=f32,
-        )
-        for j in range(8):
-            at = pl.ds(pl.multiple_of(i * 128 + j * 16, 16), 16)
-            even = mine[j * 32 : j * 32 + 16, :]
-            odd = mine[j * 32 + 16 : j * 32 + 32, :]
-            keep[at, :] = jnp.where(first, even, odd)
-            send[at, :] = jnp.where(first, odd, even).astype(bf16)
-        return 0
-
-    lax.fori_loop(0, KV // 256, block, 0)
-    total = jnp.sum(gains[...], axis=0, keepdims=True)
-    keep[KV // 2 :, :] = jnp.concatenate([total, jnp.zeros((EXTRA - 1, F), f32)], axis=0)
-    high, mid, low = parts(total)
-    tail = jnp.concatenate([high, mid, low, jnp.zeros((EXTRA - 3, F), f32)], axis=0)
-    send[KV // 2 :, :] = tail.astype(bf16)
 
 
 def gain_tail(total):
     high = total.astype(bf16).astype(f32)
     return jnp.concatenate([high, total - high], axis=0).astype(bf16)
+
+
+def own_tail(total):
+    return jnp.concatenate([total, jnp.zeros_like(total)], axis=0)
 
 
 def core_kernel(keep, got, own, *sends):
@@ -211,31 +216,48 @@
 
     for d, send in enumerate(sends):
         put(send, d + 1, gain_tail(tail))
-    put(own, 0, jnp.concatenate([tail, jnp.zeros_like(tail)], axis=0))
+    put(own, 0, own_tail(tail))
 
 
 def x_kernel(own, *refs):
-    *got, out = refs
-    for z in range(Z):
-        for j in range(F // 128):
-            at = slice(j * 128 + z * 16, j * 128 + z * 16 + 16)
-            total = own[at, :]
-            for g in got:
-                total = total + g[at, :].astype(f32)
-            out[z, j * 16 : (j + 1) * 16, :] = total.astype(bf16)
+    *got, keep, send = refs
+    bit = lax.rem(lax.axis_index("z"), 2)
+
+    def put(out, bit, tail):
+        for q in range(Z // 2):
+            for j in range(F // 128):
+                at = pl.ds(pl.multiple_of(j * 128 + (2 * q + bit) * 16, 16), 16)
+                total = own[at, :]
+                for g in got:
+                    total = total + g[at, :].astype(f32)
+                out[q * 128 + j * 16 : q * 128 + (j + 1) * 16, :] = total.astype(out.dtype)
+        out[Z // 2 * 128 :, :] = tail
+
     tail = own[F:, :]
     for g in got:
         tail = tail + g[F:, :].astype(f32)
-    tail = gain_tail(tail[:8] + tail[8:])
-    for z in range(Z):
-        out[z, 128:, :] = tail
-
-
-def last_kernel(got, weight_out, gain_out):
-    total = got[0].astype(f32)
-    for z in range(1, Z):
-        total = total + got[z].astype(f32)
-    total = total * GRAD_SCALE
+    tail = tail[:8] + tail[8:]
+    put(send, 1 - bit, gain_tail(tail))
+    put(keep, bit, own_tail(tail))
+
+
+def z_kernel(count, own, got, keep, send):
+    bit = lax.rem(lax.axis_index("z") // (Z // count), 2)
+
+    def put(out, bit, tail):
+        for q in range(count // 2):
+            at = pl.ds(pl.multiple_of((2 * q + bit) * 128, 128), 128)
+            out[q * 128 : (q + 1) * 128, :] = (own[at, :] + got[at, :].astype(f32)).astype(out.dtype)
+        out[count // 2 * 128 :, :] = tail
+
+    tail = own[count * 128 :, :] + got[count * 128 :, :].astype(f32)
+    tail = tail[:8] + tail[8:]
+    put(send, 1 - bit, gain_tail(tail))
+    put(keep, bit, own_tail(tail))
+
+
+def last_kernel(own, got, weight_out, gain_out):
+    total = (own[...] + got[...].astype(f32)) * GRAD_SCALE
     tail = total[128:136] + total[136:]
     for j in range(F // 128):
         at = slice(j * 128, (j + 1) * 128)
@@ -264,6 +286,7 @@
 def body(activations, targets, routes, value_weights, norm_gains):
     peer = ("x", "z", "core")
     weights = value_weights[0]
+    flipped = weights.T
     order = routes[:, 0]
     given = order, activations.reshape(PIECES, MB, F), targets.reshape(PIECES, MB, C)
     sends = call(
@@ -289,38 +312,49 @@
         [pltpu.VMEM((8, 128), f32)],
         name="loss",
     )(exchange(partials, "tp"), arrived)
-    normed = call(normed_kernel, shape(ROWS, F), [VMEM] * 3, name="normed")(arrived, norm_gains, scales)
-    back, grads, gains = call(
+    normal = call(normal_kernel, shape(ROWS, F), [VMEM] * 2, name="normal")(arrived, scales)
+    got = exchange(grad_part, "tp")
+
+    half = (KV // CORES + EXTRA, F)
+    keep, send, grads = call(
+        share_kernel,
+        (shape(*half, dtype=f32), shape(*half), shape(KV // 256, ROWS, 256)),
+        [VMEM] * 4,
+        [pltpu.VMEM((8, F), f32)],
+        flops=2 * ROWS * F * KV,
+        name="share",
+    )(got, normal, norm_gains, flipped)
+    by_core = lax.ppermute(send, "core", [(0, 1), (1, 0)])
+    back = call(
         grad_kernel,
-        (shape(NP, MB, F + C), shape(ROWS, KV), shape(8, F, dtype=f32)),
-        [VMEM] * 6,
+        shape(NP, MB, F + C),
+        [VMEM] * 7,
         [pltpu.VMEM((ROWS, 128), f32)] * 2,
         flops=2 * ROWS * F * KV,
         size=8 << 20,
         name="grads",
-    )(exchange(grad_part, "tp"), arrived, norm_gains, weights, scales, value)
-    rows_back = exchange(back, peer)
-
-    half = (KV // CORES + EXTRA, F)
-    keep, send = call(
-        share_kernel,
-        (shape(*half, dtype=f32), shape(*half)),
-        [VMEM] * 3,
-        flops=2 * ROWS * F * KV,
-        name="share",
-    )(grads, normed, gains)
-    got = lax.ppermute(send, "core", [(0, 1), (1, 0)])
+    )(got, grads, arrived, norm_gains, flipped, scales, value)
+
     block = (F + EXTRA, 128)
     own, *sends = call(
         core_kernel, (shape(*block, dtype=f32),) + (shape(*block),) * (X - 1), [VMEM] * 2, name="sum_core"
-    )(keep, got)
-    got = [lax.ppermute(v, "x", [(i, (i + d + 1) % X) for i in range(X)]) for d, v in enumerate(sends)]
-    by_x = call(x_kernel, shape(Z, 128 + EXTRA, 128), [VMEM] * X, name="sum_x")(own, *got)
-    by_x, rows_back = lax.optimization_barrier((by_x, rows_back))
-    by_z = exchange(by_x, "z")
+    )(keep, by_core)
+    by_x = [lax.ppermute(v, "x", [(i, (i + d + 1) % X) for i in range(X)]) for d, v in enumerate(sends)]
+    back, by_x = lax.optimization_barrier((back, by_x))
+    rows_back = exchange(back, peer)
+
+    def halves(count):
+        return shape(count * 128 + EXTRA, 128, dtype=f32), shape(count * 128 + EXTRA, 128)
+
+    def swap(v, step):
+        return lax.ppermute(v, "z", [(i, i ^ step) for i in range(Z)])
+
+    keep, send = call(x_kernel, halves(4), [VMEM] * X, name="sum_x")(own, *by_x)
+    keep, send = call(functools.partial(z_kernel, 4), halves(2), [VMEM] * 2, name="sum_z1")(keep, swap(send, 1))
+    keep, send = call(functools.partial(z_kernel, 2), halves(1), [VMEM] * 2, name="sum_z2")(keep, swap(send, 2))
     weight_grad, gain_grad = call(
-        last_kernel, (shape(16, F, dtype=f32), shape(1, F, dtype=f32)), [VMEM], name="sum_z"
-    )(by_z)
+        last_kernel, (shape(16, F, dtype=f32), shape(1, F, dtype=f32)), [VMEM] * 2, name="sum_z4"
+    )(keep, swap(send, 4))
     grad_rows, values = call(
         unpack_kernel,
         (shape(PIECES, MB, F), shape(PIECES, MB, C)),

time: 184 us -> 211 us (1.15)
  waiting for transfers between devices: 26.7 us -> 65.2 us
  blocking collectives: 113 us -> 82.3 us
  starting transfers between devices: 27 us -> 36.2 us
  local copies, waits for them, and re-layouts: 0.02 us -> 9.12 us
    ppermute x1 -> x4, waiting for transfers between devices: 2.31 us -> 35.5 us  [the longest x3 33.2 us: swap(): return lax.ppermute(v, 'z', [(i, i ^ step) for i in range(Z)])]
    all_to_all x3 -> x2, blocking collectives: 113 us -> 82.3 us  [exchange(): return lax.all_to_all(v, axes, split_axis=0, concat_axis=0, tiled=True)]
    all_to_all x2, waiting for transfers between devices: 9.09 us -> 25.4 us  [exchange(): return lax.all_to_all(v, axes, split_axis=0, concat_axis=0, tiled=True)]
    ppermute x1 -> x4, starting transfers between devices: 2.36 us -> 14.3 us  [the longest x3 11.9 us: swap(): return lax.ppermute(v, 'z', [(i, i ^ step) for i in range(Z)])]
    ppermute x3, waiting for transfers between devices: 15.3 us -> 4.38 us  [body(): lax.ppermute(v, 'x', [(i, (i + d + 1) % X) for i in range(X)])]
    unnamed x6 -> x29, local copies, waits for them, and re-layouts: 0.02 us -> 9.12 us
    pallas_call x4 -> x6, Pallas kernels: 6.32 us -> 6.89 us  [the longest x1 3.27 us: body(): call(share_kernel, (shape(*half, dtype=f32), shape(*half), shape(KV // 25...]
  transfers between devices with their start and end apart: 6 -> 9, of which waited for: 4 -> 7; matrix products, arithmetic and copies ran while one was open for 0% -> 1% of each run, Pallas kernels for 3% -> 2%
where the time goes in v4:
time: 211 us; the launch traced here: 209 us
  blocking collectives  82.3 us (39%)
  waiting for transfers between devices  65.2 us (31%)
  starting transfers between devices  36.2 us (17%)
  Pallas kernels  14.8 us (7%)
  local copies, waits for them, and re-layouts  9.12 us (4%)
    all_to_all x2, blocking collectives, exchange(): return lax.all_to_all(v, axes, split_axis=0, concat_axis=0, tiled=True)  82.3 us
    ppermute x3, waiting for transfers between devices, swap(): return lax.ppermute(v, 'z', [(i, i ^ step) for i in range(Z)])  33.2 us
    all_to_all x2, waiting for transfers between devices, exchange(): return lax.all_to_all(v, axes, split_axis=0, concat_axis=0, tiled=True)  25.4 us
    all_to_all x2, starting transfers between devices, exchange(): return lax.all_to_all(v, axes, split_axis=0, concat_axis=0, tiled=True)  12.1 us
    ppermute x3, starting transfers between devices, swap(): return lax.ppermute(v, 'z', [(i, i ^ step) for i in range(Z)])  11.9 us
    ppermute x3, starting transfers between devices, body(): lax.ppermute(v, 'x', [(i, (i + d + 1) % X) for i in range(X)])  9.76 us
    unnamed x29, local copies, waits for them, and re-layouts  9.12 us
    ppermute x3, waiting for transfers between devices, body(): lax.ppermute(v, 'x', [(i, (i + d + 1) % X) for i in range(X)])  4.38 us
  transfers between devices with their start and end apart: 9, of which 7 were waited for; matrix products, arithmetic and copies ran while one was open for 1% of the time, Pallas kernels for 2%

profile of v4, /device:TPU:1, one launch (start us, length us, event | category | flops | bytes accessed | tf_op | source)
XLA Modules:
  0.0 208.5 jit_solution(8771308254447808010)
XLA Ops:
  0.6 1.8 pack.1
  2.5 0.0 copy-start
  2.5 0.0 copy-start.12
  2.5 46.1 %all_to_all.20.rows.goals = bf16[64,8,1152]{2,1,0:T(8,128)(2,1)S(1)} all-to-all(bf16[64,8,1152]{2,1,0:T(8,128)(2,1)S(1)} %pack.1), channel_id=1, replica_groups=mesh['x'=4,'z'=8,'core'=2,'tp'=8] {'x','z','core'}, dimensions={0} | all-to-all | bytes 2359296 | tf_op jit(solution)/shard_map/all_to_all | solution.py:283
  48.6 0.0 copy-done
  48.6 0.0 copy-done.12
  48.6 1.9 partial_values.1
  50.5 36.2 %all_to_all.21.got = bf16[8,528,128]{2,1,0:T(8,128)(2,1)S(1)} all-to-all(bf16[8,528,128]{2,1,0:T(8,128)(2,1)S(1)} %partial_values.1), channel_id=1, replica_groups=mesh['x'=4,'z'=8,'core'=2,'tp'=8] {'tp'}, dimensions={0} | all-to-all | bytes 2162688 | tf_op jit(solution)/shard_map/all_to_all | solution.py:283
  86.6 1.7 loss.1
  88.4 0.0 copy-start.10
  88.4 0.7 copy-done.10
  89.0 4.2 %all-to-all-start.2 = ((bf16[8,528,128]{2,1,0:T(8,128)(2,1)}), bf16[8,528,128]{2,1,0:T(8,128)(2,1)}, u32[]{:S(2)}, u32[]{:S(2)}) async-start(bf16[8,528,128]{2,1,0:T(8,128)(2,1)} %get-tuple-element.28), calls=%async_computation.2 | async-start | bytes 2162688 | tf_op jit(solution)/shard_map/all_to_all | solution.py:283
  93.3 2.9 %copy.9 = bf16[1,1024,1024]{1,2,0:T(8,128)(2,1)S(1)} copy(bf16[1,1024,1024]{2,1,0:T(8,128)(2,1)} %param.8) | data formatting | bytes 4194304 | tf_op args[3]
  96.2 0.7 normal.1
  96.9 0.0 copy-start.2
  96.9 1.0 copy-done.2
  97.9 25.4 %all-to-all-done.2.got = bf16[8,528,128]{2,1,0:T(8,128)(2,1)} async-done(((bf16[8,528,128]{2,1,0:T(8,128)(2,1)}), bf16[8,528,128]{2,1,0:T(8,128)(2,1)}, u32[]{:S(2)}, u32[]{:S(2)}) %all-to-all-start.2) | async-done | bytes 1081376 | tf_op jit(solution)/shard_map/all_to_all | solution.py:283
  123.2 0.0 copy-start.3
  123.2 1.2 copy-done.3
  124.4 3.3 %share.1 = (f32[528,1024]{1,0:T(8,128)S(1)}, bf16[528,1024]{1,0:T(8,128)(2,1)S(1)}, bf16[4,512,256]{2,1,0:T(8,128)(2,1)S(1)}) custom-call(bf16[8,528,128]{2,1,0:T(8,128)(2,1)} %all-to-all-done.2.got, bf16[512,1024]{1,0:T(8,128)(2,1)S(1)} %copy-done.3, f32[1,1024]{1,0:T(1,128)S(1)} %copy-done.12, bf16[1024,1024]{1,0:T(8,128)(2,1)S(1)} %bitcast.10), custom_call_target="tpu_custom_call" | custom-call | flops 1073741824 | bytes 4194304 | tf_op jit(solution)/shard_map/share/pallas_call | solution.py:319
  127.7 2.4 %collective-permute-start = (bf16[528,1024]{1,0:T(8,128)(2,1)S(1)}, bf16[528,1024]{1,0:T(8,128)(2,1)S(1)}, u32[]{:S(2)}, u32[]{:S(2)}) collective-permute-start(bf16[528,1024]{1,0:T(8,128)(2,1)S(1)} %get-tuple-element.33), channel_id=1, source_target_pairs={{0,8},{8,0},{1,9},{9,1},{2,10},{10,2},{3,11},{11,3},{4,12},{12,4},... | collective-permute-start | bytes 3244040 | tf_op jit(solution)/shard_map/ppermute | solution.py:327
  130.1 2.3 %collective-permute-done.got = bf16[528,1024]{1,0:T(8,128)(2,1)S(1)} collective-permute-done((bf16[528,1024]{1,0:T(8,128)(2,1)S(1)}, bf16[528,1024]{1,0:T(8,128)(2,1)S(1)}, u32[]{:S(2)}, u32[]{:S(2)}) %collective-permute-start) | collective-permute-done | bytes 1081376 | tf_op jit(solution)/shard_map/ppermute | solution.py:327
  132.5 0.0 copy-start.11
  132.5 0.3 sum_core.1
  132.7 0.0 copy-start.4
  132.7 3.5 %collective-permute-start.1 = (bf16[1040,128]{1,0:T(8,128)(2,1)S(1)}, bf16[1040,128]{1,0:T(8,128)(2,1)S(1)}, u32[]{:S(2)}, u32[]{:S(2)}) collective-permute-start(bf16[1040,128]{1,0:T(8,128)(2,1)S(1)} %get-tuple-element.34), channel_id=1, source_target_pairs={{0,128},{128,256},{256,384},{384,0},{1,129},{129,257},{257,385},{3... | collective-permute-start | bytes 798728 | tf_op jit(solution)/shard_map/ppermute | solution.py:342
  136.3 3.0 %collective-permute-start.2 = (bf16[1040,128]{1,0:T(8,128)(2,1)S(1)}, bf16[1040,128]{1,0:T(8,128)(2,1)S(1)}, u32[]{:S(2)}, u32[]{:S(2)}) collective-permute-start(bf16[1040,128]{1,0:T(8,128)(2,1)S(1)} %get-tuple-element.35), channel_id=1, source_target_pairs={{0,256},{128,384},{256,0},{384,128},{1,257},{129,385},{257,1},{385... | collective-permute-start | bytes 798728 | tf_op jit(solution)/shard_map/ppermute | solution.py:342
  139.3 3.2 %collective-permute-start.3 = (bf16[1040,128]{1,0:T(8,128)(2,1)S(1)}, bf16[1040,128]{1,0:T(8,128)(2,1)S(1)}, u32[]{:S(2)}, u32[]{:S(2)}) collective-permute-start(bf16[1040,128]{1,0:T(8,128)(2,1)S(1)} %get-tuple-element.36), channel_id=1, source_target_pairs={{0,384},{128,0},{256,128},{384,256},{1,385},{129,1},{257,129},{385... | collective-permute-start | bytes 798728 | tf_op jit(solution)/shard_map/ppermute | solution.py:342
  142.5 0.0 copy-done.11
  142.5 2.7 %grads.1 = bf16[64,8,1152]{2,1,0:T(8,128)(2,1)S(1)} custom-call(bf16[8,528,128]{2,1,0:T(8,128)(2,1)} %all-to-all-done.2.got, bf16[4,512,256]{2,1,0:T(8,128)(2,1)S(1)} %get-tuple-element.30.grads, bf16[64,8,1152]{2,1,0:T(8,128)(2,1)S(1)} %all_to_all.20.rows.goals, f32[1,1024]{1,0:T(1,128)S(1)} %copy-done.12, bf16[1024,1024]{1,0:T(8,128)(2,1)S(1)} %bitcast.11, ...), custom_call_target="tpu_custom_call" | custom-call | flops 1073741824 | bytes 8388608 | tf_op jit(solution)/shard_map/grads/pallas_call | solution.py:328
  145.2 0.0 copy-done.4
  145.2 0.0 copy-start.1
  145.2 1.0 copy-done.1
  146.2 0.0 collective-permute-done.1.refs_0_
  146.2 0.0 copy-start.5
  146.2 3.0 %collective-permute-done.2.refs_1_ = bf16[1040,128]{1,0:T(8,128)(2,1)S(1)} collective-permute-done((bf16[1040,128]{1,0:T(8,128)(2,1)S(1)}, bf16[1040,128]{1,0:T(8,128)(2,1)S(1)}, u32[]{:S(2)}, u32[]{:S(2)}) %collective-permute-start.2) | collective-permute-done | bytes 266272 | tf_op jit(solution)/shard_map/ppermute | solution.py:342
  149.2 0.0 copy-start.6
  149.2 0.7 copy-done.6
  149.9 1.4 collective-permute-done.3.refs_2_
  151.3 0.0 copy-start.8
  151.3 0.7 copy-done.8
  152.0 0.0 copy-start.7
  152.0 7.9 %all-to-all-start.3 = ((bf16[64,8,1152]{2,1,0:T(8,128)(2,1)}), bf16[64,8,1152]{2,1,0:T(8,128)(2,1)S(1)}, u32[]{:S(2)}, u32[]{:S(2)}) async-start(bf16[64,8,1152]{2,1,0:T(8,128)(2,1)} %copy-done.1), calls=%async_computation.3 | async-start | bytes 2359296 | tf_op jit(solution)/shard_map/all_to_all | solution.py:283
  159.9 0.0 copy-start.13
  160.0 0.0 copy-done.5
  160.0 0.0 copy-done.7
  160.0 0.0 copy-start.9
  160.0 0.9 copy-done.9
  160.9 0.2 sum_x.1
  161.1 3.3 %collective-permute-start.4 = (bf16[528,128]{1,0:T(8,128)(2,1)S(1)}, bf16[528,128]{1,0:T(8,128)(2,1)S(1)}, u32[]{:S(2)}, u32[]{:S(2)}) collective-permute-start(bf16[528,128]{1,0:T(8,128)(2,1)S(1)} %get-tuple-element.45), channel_id=1, source_target_pairs={{0,16},{16,0},{32,48},{48,32},{64,80},{80,64},{96,112},{112,96},{1... | collective-permute-start | bytes 405512 | tf_op jit(solution)/shard_map/ppermute | solution.py:350
  164.4 25.7 %collective-permute-done.4.got = bf16[528,128]{1,0:T(8,128)(2,1)S(1)} collective-permute-done((bf16[528,128]{1,0:T(8,128)(2,1)S(1)}, bf16[528,128]{1,0:T(8,128)(2,1)S(1)}, u32[]{:S(2)}, u32[]{:S(2)}) %collective-permute-start.4) | collective-permute-done | bytes 135200 | tf_op jit(solution)/shard_map/ppermute | solution.py:350
  190.2 4.0 %collective-permute-start.5 = (bf16[272,128]{1,0:T(8,128)(2,1)S(1)}, bf16[272,128]{1,0:T(8,128)(2,1)S(1)}, u32[]{:S(2)}, u32[]{:S(2)}) collective-permute-start(bf16[272,128]{1,0:T(8,128)(2,1)S(1)} %get-tuple-element.47), channel_id=1, source_target_pairs={{0,32},{16,48},{32,0},{48,16},{64,96},{80,112},{96,64},{112,80},{1... | collective-permute-start | bytes 208904 | tf_op jit(solution)/shard_map/ppermute | solution.py:350
  194.1 3.5 %collective-permute-done.5.got = bf16[272,128]{1,0:T(8,128)(2,1)S(1)} collective-permute-done((bf16[272,128]{1,0:T(8,128)(2,1)S(1)}, bf16[272,128]{1,0:T(8,128)(2,1)S(1)}, u32[]{:S(2)}, u32[]{:S(2)}) %collective-permute-start.5) | collective-permute-done | bytes 69664 | tf_op jit(solution)/shard_map/ppermute | solution.py:350
  197.7 4.7 %collective-permute-start.6 = (bf16[144,128]{1,0:T(8,128)(2,1)S(1)}, bf16[144,128]{1,0:T(8,128)(2,1)S(1)}, u32[]{:S(2)}, u32[]{:S(2)}) collective-permute-start(bf16[144,128]{1,0:T(8,128)(2,1)S(1)} %get-tuple-element.49), channel_id=1, source_target_pairs={{0,64},{16,80},{32,96},{48,112},{64,0},{80,16},{96,32},{112,48},{1... | collective-permute-start | bytes 110600 | tf_op jit(solution)/shard_map/ppermute | solution.py:350
  202.4 3.9 %collective-permute-done.6.got = bf16[144,128]{1,0:T(8,128)(2,1)S(1)} collective-permute-done((bf16[144,128]{1,0:T(8,128)(2,1)S(1)}, bf16[144,128]{1,0:T(8,128)(2,1)S(1)}, u32[]{:S(2)}, u32[]{:S(2)}) %collective-permute-start.6) | collective-permute-done | bytes 36896 | tf_op jit(solution)/shard_map/ppermute | solution.py:350
  206.3 0.6 sum_z4.1
  206.9 0.0 all-to-all-done.3.got
  206.9 0.0 copy-done.13
  206.9 1.6 unpack.1
  (2 shorter events, 0.1 us)
Async XLA Ops:
  2.5 46.2 %copy-start = (bf16[1,1024,1024]{2,1,0:T(8,128)(2,1)S(1)}, bf16[1,1024,1024]{2,1,0:T(8,128)(2,1)}, u32[]{:S(2)}) copy-start(bf16[1,1024,1024]{2,1,0:T(8,128)(2,1)} %param.8) | copy-start | bytes 6291460
  2.5 46.1 %copy-start.12 = (f32[1,1024]{1,0:T(1,128)S(1)}, f32[1,1024]{1,0:T(1,128)}, u32[]{:S(2)}) copy-start(f32[1,1024]{1,0:T(1,128)} %gain.5) | copy-start | bytes 12292
  88.4 0.7 copy-start.10
  89.0 34.2 %all-to-all-start.2 = ((bf16[8,528,128]{2,1,0:T(8,128)(2,1)}), bf16[8,528,128]{2,1,0:T(8,128)(2,1)}, u32[]{:S(2)}, u32[]{:S(2)}) async-start(bf16[8,528,128]{2,1,0:T(8,128)(2,1)} %get-tuple-element.28), calls=%async_computation.2 | async-start | bytes 2162688 | tf_op jit(solution)/shard_map/all_to_all | solution.py:283
  96.9 1.0 copy-start.2
  123.2 1.2 copy-start.3
  127.7 4.7 %collective-permute-start = (bf16[528,1024]{1,0:T(8,128)(2,1)S(1)}, bf16[528,1024]{1,0:T(8,128)(2,1)S(1)}, u32[]{:S(2)}, u32[]{:S(2)}) collective-permute-start(bf16[528,1024]{1,0:T(8,128)(2,1)S(1)} %get-tuple-element.33), channel_id=1, source_target_pairs={{0,8},{8,0},{1,9},{9,1},{2,10},{10,2},{3,11},{11,3},{4,12},{12,4},... | collective-permute-start | bytes 3244040 | tf_op jit(solution)/shard_map/ppermute | solution.py:327
  132.5 10.1 %copy-start.11 = (bf16[64,8,128]{2,1,0:T(8,128)(2,1)S(1)}, bf16[64,8,128]{2,1,0:T(8,128)(2,1)}, u32[]{:S(2)}) copy-start(bf16[64,8,128]{2,1,0:T(8,128)(2,1)} %copy-done.10) | copy-start | bytes 393220
  132.7 12.5 %copy-start.4 = (f32[1040,128]{1,0:T(8,128)}, f32[1040,128]{1,0:T(8,128)S(1)}, u32[]{:S(2)}) copy-start(f32[1040,128]{1,0:T(8,128)S(1)} %get-tuple-element.40.own) | copy-start | bytes 1597444
  132.7 13.5 %collective-permute-start.1 = (bf16[1040,128]{1,0:T(8,128)(2,1)S(1)}, bf16[1040,128]{1,0:T(8,128)(2,1)S(1)}, u32[]{:S(2)}, u32[]{:S(2)}) collective-permute-start(bf16[1040,128]{1,0:T(8,128)(2,1)S(1)} %get-tuple-element.34), channel_id=1, source_target_pairs={{0,128},{128,256},{256,384},{384,0},{1,129},{129,257},{257,385},{3... | collective-permute-start | bytes 798728 | tf_op jit(solution)/shard_map/ppermute | solution.py:342
  136.3 12.9 %collective-permute-start.2 = (bf16[1040,128]{1,0:T(8,128)(2,1)S(1)}, bf16[1040,128]{1,0:T(8,128)(2,1)S(1)}, u32[]{:S(2)}, u32[]{:S(2)}) collective-permute-start(bf16[1040,128]{1,0:T(8,128)(2,1)S(1)} %get-tuple-element.35), channel_id=1, source_target_pairs={{0,256},{128,384},{256,0},{384,128},{1,257},{129,385},{257,1},{385... | collective-permute-start | bytes 798728 | tf_op jit(solution)/shard_map/ppermute | solution.py:342
  139.3 12.0 %collective-permute-start.3 = (bf16[1040,128]{1,0:T(8,128)(2,1)S(1)}, bf16[1040,128]{1,0:T(8,128)(2,1)S(1)}, u32[]{:S(2)}, u32[]{:S(2)}) collective-permute-start(bf16[1040,128]{1,0:T(8,128)(2,1)S(1)} %get-tuple-element.36), channel_id=1, source_target_pairs={{0,384},{128,0},{256,128},{384,256},{1,385},{129,1},{257,129},{385... | collective-permute-start | bytes 798728 | tf_op jit(solution)/shard_map/ppermute | solution.py:342
  145.2 1.0 copy-start.1
  146.2 13.7 %copy-start.5 = (f32[1040,128]{1,0:T(8,128)S(1)}, f32[1040,128]{1,0:T(8,128)}, u32[]{:S(2)}) copy-start(f32[1040,128]{1,0:T(8,128)} %copy-done.4) | copy-start | bytes 1597444
  149.2 0.7 copy-start.6
  151.3 0.7 copy-start.8
  152.0 7.9 %copy-start.7 = (bf16[1040,128]{1,0:T(8,128)(2,1)S(1)}, bf16[1040,128]{1,0:T(8,128)(2,1)}, u32[]{:S(2)}) copy-start(bf16[1040,128]{1,0:T(8,128)(2,1)} %copy-done.6) | copy-start | bytes 798724
  152.0 54.9 %all-to-all-start.3 = ((bf16[64,8,1152]{2,1,0:T(8,128)(2,1)}), bf16[64,8,1152]{2,1,0:T(8,128)(2,1)S(1)}, u32[]{:S(2)}, u32[]{:S(2)}) async-start(bf16[64,8,1152]{2,1,0:T(8,128)(2,1)} %copy-done.1), calls=%async_computation.3 | async-start | bytes 2359296 | tf_op jit(solution)/shard_map/all_to_all | solution.py:283
  159.9 47.0 %copy-start.13 = (s32[32,1]{0,1:T(1,128)S(1)}, s32[32,1]{0,1:T(1,128)}, u32[]{:S(2)}) copy-start(s32[32,1]{0,1:T(1,128)} %param.7) | copy-start | bytes 388
  160.0 1.0 copy-start.9
  161.1 29.0 %collective-permute-start.4 = (bf16[528,128]{1,0:T(8,128)(2,1)S(1)}, bf16[528,128]{1,0:T(8,128)(2,1)S(1)}, u32[]{:S(2)}, u32[]{:S(2)}) collective-permute-start(bf16[528,128]{1,0:T(8,128)(2,1)S(1)} %get-tuple-element.45), channel_id=1, source_target_pairs={{0,16},{16,0},{32,48},{48,32},{64,80},{80,64},{96,112},{112,96},{1... | collective-permute-start | bytes 405512 | tf_op jit(solution)/shard_map/ppermute | solution.py:350
  190.2 7.5 %collective-permute-start.5 = (bf16[272,128]{1,0:T(8,128)(2,1)S(1)}, bf16[272,128]{1,0:T(8,128)(2,1)S(1)}, u32[]{:S(2)}, u32[]{:S(2)}) collective-permute-start(bf16[272,128]{1,0:T(8,128)(2,1)S(1)} %get-tuple-element.47), channel_id=1, source_target_pairs={{0,32},{16,48},{32,0},{48,16},{64,96},{80,112},{96,64},{112,80},{1... | collective-permute-start | bytes 208904 | tf_op jit(solution)/shard_map/ppermute | solution.py:350
  197.7 8.6 %collective-permute-start.6 = (bf16[144,128]{1,0:T(8,128)(2,1)S(1)}, bf16[144,128]{1,0:T(8,128)(2,1)S(1)}, u32[]{:S(2)}, u32[]{:S(2)}) collective-permute-start(bf16[144,128]{1,0:T(8,128)(2,1)S(1)} %get-tuple-element.49), channel_id=1, source_target_pairs={{0,64},{16,80},{32,96},{48,112},{64,0},{80,16},{96,32},{112,48},{1... | collective-permute-start | bytes 110600 | tf_op jit(solution)/shard_map/ppermute | solution.py:350

commit v5 on v3

--- a/solution.py
+++ b/solution.py
@@ -315,18 +315,18 @@
         core_kernel, (shape(*block, dtype=f32),) + (shape(*block),) * (X - 1), [VMEM] * 2, name="sum_core"
     )(keep, got)
     got = [lax.ppermute(v, "x", [(i, (i + d + 1) % X) for i in range(X)]) for d, v in enumerate(sends)]
-    by_x = call(x_kernel, shape(Z, 128 + EXTRA, 128), [VMEM] * X, name="sum_x")(own, *got)
-    by_x, rows_back = lax.optimization_barrier((by_x, rows_back))
-    by_z = exchange(by_x, "z")
-    weight_grad, gain_grad = call(
-        last_kernel, (shape(16, F, dtype=f32), shape(1, F, dtype=f32)), [VMEM], name="sum_z"
-    )(by_z)
     grad_rows, values = call(
         unpack_kernel,
         (shape(PIECES, MB, F), shape(PIECES, MB, C)),
         [SMEM, VMEM],
         name="unpack",
     )(order, rows_back)
+    got, grad_rows, values = lax.optimization_barrier((got, grad_rows, values))
+    by_x = call(x_kernel, shape(Z, 128 + EXTRA, 128), [VMEM] * X, name="sum_x")(own, *got)
+    by_z = exchange(by_x, "z")
+    weight_grad, gain_grad = call(
+        last_kernel, (shape(16, F, dtype=f32), shape(1, F, dtype=f32)), [VMEM], name="sum_z"
+    )(by_z)
     return (
         grad_rows.reshape(PIECES * MB, F),
         values.reshape(PIECES * MB, C),

time: 184 us -> 183 us (level)
  blocking collectives: 113 us -> 129 us
  waiting for transfers between devices: 26.7 us -> 16 us
  starting transfers between devices: 27 us -> 21.4 us
    all_to_all x3 -> x4, blocking collectives: 113 us -> 129 us  [exchange(): return lax.all_to_all(v, axes, split_axis=0, concat_axis=0, tiled=True)]
    ppermute x3, waiting for transfers between devices: 15.3 us -> 0.71 us  [body(): lax.ppermute(v, 'x', [(i, (i + d + 1) % X) for i in range(X)])]
    all_to_all x2 -> x1, starting transfers between devices: 13.9 us -> 8.35 us  [exchange(): return lax.all_to_all(v, axes, split_axis=0, concat_axis=0, tiled=True)]
    all_to_all x2 -> x1, waiting for transfers between devices: 9.09 us -> 13 us  [exchange(): return lax.all_to_all(v, axes, split_axis=0, concat_axis=0, tiled=True)]
  transfers between devices with their start and end apart: 6 -> 5, of which waited for: 4 -> 3; matrix products, arithmetic and copies ran while one was open for 0% -> 0% of each run, Pallas kernels for 3% -> 3%
where the time goes in v5:
time: 183 us; the launch traced here: 179 us
  blocking collectives  129 us (70%)
  starting transfers between devices  21.4 us (12%)
  waiting for transfers between devices  16 us (9%)
  Pallas kernels  12.5 us (7%)
    all_to_all x4, blocking collectives, exchange(): return lax.all_to_all(v, axes, split_axis=0, concat_axis=0, tiled=True)  129 us
    all_to_all x1, waiting for transfers between devices, exchange(): return lax.all_to_all(v, axes, split_axis=0, concat_axis=0, tiled=True)  13 us
    ppermute x3, starting transfers between devices, body(): lax.ppermute(v, 'x', [(i, (i + d + 1) % X) for i in range(X)])  10.7 us
    all_to_all x1, starting transfers between devices, exchange(): return lax.all_to_all(v, axes, split_axis=0, concat_axis=0, tiled=True)  8.35 us
  transfers between devices with their start and end apart: 5, of which 3 were waited for; matrix products, arithmetic and copies ran while one was open for 0% of the time, Pallas kernels for 3%

profile of v5, /device:TPU:1, one launch (start us, length us, event | category | flops | bytes accessed | tf_op | source)
XLA Modules:
  0.0 179.4 jit_solution(7653067958014985089)
XLA Ops:
  0.6 1.8 %pack.1 = bf16[64,8,1152]{2,1,0:T(8,128)(2,1)S(1)} custom-call(s32[32]{0:T(128)} %bitcast.9, bf16[32,8,1024]{2,1,0:T(8,128)(2,1)} %bitcast.11, bf16[32,8,128]{2,1,0:T(8,128)(2,1)} %bitcast.12), custom_call_target="tpu_custom_call" | custom-call | bytes 4194304 | tf_op jit(solution)/shard_map/pack/pallas_call | solution.py:269
  2.5 0.0 copy-start
  2.5 0.0 copy-start.1
  2.5 46.1 %all_to_all.25.rows.goals = bf16[64,8,1152]{2,1,0:T(8,128)(2,1)S(1)} all-to-all(bf16[64,8,1152]{2,1,0:T(8,128)(2,1)S(1)} %pack.1), channel_id=1, replica_groups=mesh['x'=4,'z'=8,'core'=2,'tp'=8] {'x','z','core'}, dimensions={0} | all-to-all | bytes 2359296 | tf_op jit(solution)/shard_map/all_to_all | solution.py:261
  48.6 0.0 copy-done
  48.6 0.0 copy-done.1
  48.6 1.9 %partial_values.1 = bf16[8,528,128]{2,1,0:T(8,128)(2,1)S(1)} custom-call(bf16[64,8,1152]{2,1,0:T(8,128)(2,1)S(1)} %all_to_all.25.rows.goals, f32[1,1024]{1,0:T(1,128)S(1)} %copy-done.1, bf16[1024,1024]{1,0:T(8,128)(2,1)S(1)} %bitcast.7), custom_call_target="tpu_custom_call" | custom-call | flops 1073741824 | bytes 4194304 | tf_op jit(solution)/shard_map/partial_values/pallas_call | solution.py:277
  50.5 36.2 %all_to_all.26.got = bf16[8,528,128]{2,1,0:T(8,128)(2,1)S(1)} all-to-all(bf16[8,528,128]{2,1,0:T(8,128)(2,1)S(1)} %partial_values.1), channel_id=1, replica_groups=mesh['x'=4,'z'=8,'core'=2,'tp'=8] {'tp'}, dimensions={0} | all-to-all | bytes 2162688 | tf_op jit(solution)/shard_map/all_to_all | solution.py:261
  86.7 0.8 loss.1
  87.4 30.5 %all_to_all.27.got = bf16[8,528,128]{2,1,0:T(8,128)(2,1)S(1)} all-to-all(bf16[8,528,128]{2,1,0:T(8,128)(2,1)S(1)} %get-tuple-element.25), channel_id=1, replica_groups=mesh['x'=4,'z'=8,'core'=2,'tp'=8] {'tp'}, dimensions={0} | all-to-all | bytes 2162688 | tf_op jit(solution)/shard_map/all_to_all | solution.py:261
  117.9 2.8 %grads.1 = (bf16[64,8,1152]{2,1,0:T(8,128)(2,1)}, bf16[512,1024]{1,0:T(8,128)(2,1)S(1)}, f32[8,1024]{1,0:T(8,128)S(1)}) custom-call(bf16[8,528,128]{2,1,0:T(8,128)(2,1)S(1)} %all_to_all.27.got, bf16[64,8,1152]{2,1,0:T(8,128)(2,1)S(1)} %all_to_all.25.rows.goals, f32[1,1024]{1,0:T(1,128)S(1)} %copy-done.1, bf16[1024,1024]{1,0:T(8,128)(2,1)S(1)} %bitcast.8, ...), custom_call_target="tpu_custom_call" | custom-call | flops 1073741824 | bytes 8388608 | tf_op jit(solution)/shard_map/grads/pallas_call | solution.py:293
  120.6 8.3 %all-to-all-start.3 = ((bf16[64,8,1152]{2,1,0:T(8,128)(2,1)}), bf16[64,8,1152]{2,1,0:T(8,128)(2,1)S(1)}, u32[]{:S(2)}, u32[]{:S(2)}) async-start(bf16[64,8,1152]{2,1,0:T(8,128)(2,1)} %get-tuple-element.35), calls=%async_computation.3 | async-start | bytes 2359296 | tf_op jit(solution)/shard_map/all_to_all | solution.py:261
  129.0 0.8 normed.1
  129.8 1.9 %share.1 = (f32[528,1024]{1,0:T(8,128)S(1)}, bf16[528,1024]{1,0:T(8,128)(2,1)S(1)}) custom-call(bf16[512,1024]{1,0:T(8,128)(2,1)S(1)} %get-tuple-element.28.grads, bf16[512,1024]{1,0:T(8,128)(2,1)S(1)} %normed.1, f32[8,1024]{1,0:T(8,128)S(1)} %get-tuple-element.29.gains), custom_call_target="tpu_custom_call" | custom-call | flops 1073741824 | bytes 4194304 | tf_op jit(solution)/shard_map/share/pallas_call | solution.py:305
  131.7 2.4 %collective-permute-start = (bf16[528,1024]{1,0:T(8,128)(2,1)S(1)}, bf16[528,1024]{1,0:T(8,128)(2,1)S(1)}, u32[]{:S(2)}, u32[]{:S(2)}) collective-permute-start(bf16[528,1024]{1,0:T(8,128)(2,1)S(1)} %get-tuple-element.31), channel_id=1, source_target_pairs={{0,8},{8,0},{1,9},{9,1},{2,10},{10,2},{3,11},{11,3},{4,12},{12,4},... | collective-permute-start | bytes 3244040 | tf_op jit(solution)/shard_map/ppermute | solution.py:312
  134.1 2.3 %collective-permute-done.got = bf16[528,1024]{1,0:T(8,128)(2,1)S(1)} collective-permute-done((bf16[528,1024]{1,0:T(8,128)(2,1)S(1)}, bf16[528,1024]{1,0:T(8,128)(2,1)S(1)}, u32[]{:S(2)}, u32[]{:S(2)}) %collective-permute-start) | collective-permute-done | bytes 1081376 | tf_op jit(solution)/shard_map/ppermute | solution.py:312
  136.4 0.0 copy-start.2
  136.4 0.2 sum_core.1
  136.6 3.2 %collective-permute-start.1 = (bf16[1040,128]{1,0:T(8,128)(2,1)S(1)}, bf16[1040,128]{1,0:T(8,128)(2,1)S(1)}, u32[]{:S(2)}, u32[]{:S(2)}) collective-permute-start(bf16[1040,128]{1,0:T(8,128)(2,1)S(1)} %get-tuple-element.32), channel_id=1, source_target_pairs={{0,128},{128,256},{256,384},{384,0},{1,129},{129,257},{257,385},{3... | collective-permute-start | bytes 798728 | tf_op jit(solution)/shard_map/ppermute | solution.py:317
  139.8 4.5 %collective-permute-start.2 = (bf16[1040,128]{1,0:T(8,128)(2,1)S(1)}, bf16[1040,128]{1,0:T(8,128)(2,1)S(1)}, u32[]{:S(2)}, u32[]{:S(2)}) collective-permute-start(bf16[1040,128]{1,0:T(8,128)(2,1)S(1)} %get-tuple-element.33), channel_id=1, source_target_pairs={{0,256},{128,384},{256,0},{384,128},{1,257},{129,385},{257,1},{385... | collective-permute-start | bytes 798728 | tf_op jit(solution)/shard_map/ppermute | solution.py:317
  144.4 3.0 %collective-permute-start.3 = (bf16[1040,128]{1,0:T(8,128)(2,1)S(1)}, bf16[1040,128]{1,0:T(8,128)(2,1)S(1)}, u32[]{:S(2)}, u32[]{:S(2)}) collective-permute-start(bf16[1040,128]{1,0:T(8,128)(2,1)S(1)} %get-tuple-element.34), channel_id=1, source_target_pairs={{0,384},{128,0},{256,128},{384,256},{1,385},{129,1},{257,129},{385... | collective-permute-start | bytes 798728 | tf_op jit(solution)/shard_map/ppermute | solution.py:317
  147.3 13.0 %all-to-all-done.3.got = bf16[64,8,1152]{2,1,0:T(8,128)(2,1)S(1)} async-done(((bf16[64,8,1152]{2,1,0:T(8,128)(2,1)}), bf16[64,8,1152]{2,1,0:T(8,128)(2,1)S(1)}, u32[]{:S(2)}, u32[]{:S(2)}) %all-to-all-start.3) | async-done | bytes 1179680 | tf_op jit(solution)/shard_map/all_to_all | solution.py:261
  160.4 0.0 copy-done.2
  160.4 1.6 unpack.1
  162.0 0.0 collective-permute-done.1.refs_0_
  162.0 0.7 collective-permute-done.2.refs_1_
  162.7 0.0 collective-permute-done.3.refs_2_
  162.7 0.1 sum_x.1
  162.8 15.9 %all_to_all.28.got = bf16[8,144,128]{2,1,0:T(8,128)(2,1)S(1)} all-to-all(bf16[8,144,128]{2,1,0:T(8,128)(2,1)S(1)} %sum_x.1), channel_id=1, replica_groups=mesh['x'=4,'z'=8,'core'=2,'tp'=8] {'z'}, dimensions={0} | all-to-all | bytes 589824 | tf_op jit(solution)/shard_map/all_to_all | solution.py:261
  178.7 0.7 sum_z.1
Async XLA Ops:
  2.5 46.2 %copy-start = (bf16[1,1024,1024]{2,1,0:T(8,128)(2,1)S(1)}, bf16[1,1024,1024]{2,1,0:T(8,128)(2,1)}, u32[]{:S(2)}) copy-start(bf16[1,1024,1024]{2,1,0:T(8,128)(2,1)} %param.8) | copy-start | bytes 6291460
  2.5 46.1 %copy-start.1 = (f32[1,1024]{1,0:T(1,128)S(1)}, f32[1,1024]{1,0:T(1,128)}, u32[]{:S(2)}) copy-start(f32[1,1024]{1,0:T(1,128)} %gain.5) | copy-start | bytes 12292
  120.6 39.7 %all-to-all-start.3 = ((bf16[64,8,1152]{2,1,0:T(8,128)(2,1)}), bf16[64,8,1152]{2,1,0:T(8,128)(2,1)S(1)}, u32[]{:S(2)}, u32[]{:S(2)}) async-start(bf16[64,8,1152]{2,1,0:T(8,128)(2,1)} %get-tuple-element.35), calls=%async_computation.3 | async-start | bytes 2359296 | tf_op jit(solution)/shard_map/all_to_all | solution.py:261
  131.7 4.7 %collective-permute-start = (bf16[528,1024]{1,0:T(8,128)(2,1)S(1)}, bf16[528,1024]{1,0:T(8,128)(2,1)S(1)}, u32[]{:S(2)}, u32[]{:S(2)}) collective-permute-start(bf16[528,1024]{1,0:T(8,128)(2,1)S(1)} %get-tuple-element.31), channel_id=1, source_target_pairs={{0,8},{8,0},{1,9},{9,1},{2,10},{10,2},{3,11},{11,3},{4,12},{12,4},... | collective-permute-start | bytes 3244040 | tf_op jit(solution)/shard_map/ppermute | solution.py:312
  136.4 24.0 %copy-start.2 = (s32[32,1]{0,1:T(1,128)S(1)}, s32[32,1]{0,1:T(1,128)}, u32[]{:S(2)}) copy-start(s32[32,1]{0,1:T(1,128)} %param.7) | copy-start | bytes 388
  136.6 25.3 %collective-permute-start.1 = (bf16[1040,128]{1,0:T(8,128)(2,1)S(1)}, bf16[1040,128]{1,0:T(8,128)(2,1)S(1)}, u32[]{:S(2)}, u32[]{:S(2)}) collective-permute-start(bf16[1040,128]{1,0:T(8,128)(2,1)S(1)} %get-tuple-element.32), channel_id=1, source_target_pairs={{0,128},{128,256},{256,384},{384,0},{1,129},{129,257},{257,385},{3... | collective-permute-start | bytes 798728 | tf_op jit(solution)/shard_map/ppermute | solution.py:317
  139.8 22.8 %collective-permute-start.2 = (bf16[1040,128]{1,0:T(8,128)(2,1)S(1)}, bf16[1040,128]{1,0:T(8,128)(2,1)S(1)}, u32[]{:S(2)}, u32[]{:S(2)}) collective-permute-start(bf16[1040,128]{1,0:T(8,128)(2,1)S(1)} %get-tuple-element.33), channel_id=1, source_target_pairs={{0,256},{128,384},{256,0},{384,128},{1,257},{129,385},{257,1},{385... | collective-permute-start | bytes 798728 | tf_op jit(solution)/shard_map/ppermute | solution.py:317
  144.4 18.3 %collective-permute-start.3 = (bf16[1040,128]{1,0:T(8,128)(2,1)S(1)}, bf16[1040,128]{1,0:T(8,128)(2,1)S(1)}, u32[]{:S(2)}, u32[]{:S(2)}) collective-permute-start(bf16[1040,128]{1,0:T(8,128)(2,1)S(1)} %get-tuple-element.34), channel_id=1, source_target_pairs={{0,384},{128,0},{256,128},{384,256},{1,385},{129,1},{257,129},{385... | collective-permute-start | bytes 798728 | tf_op jit(solution)/shard_map/ppermute | solution.py:317

commit v6 on v5

--- a/solution.py
+++ b/solution.py
@@ -79,17 +79,14 @@
 
 
 def value_kernel(rows, gain, weights, out, gained, squares):
-    def tile(i, _):
-        x = rows[pl.ds(i * 16, 16), :, :F].astype(f32).reshape(TILE, F)
+    for i in range(NTILES):
+        x = rows[i * 16 : (i + 1) * 16, :, :F].astype(f32).reshape(TILE, F)
         sq = x * x
         folded = sq[:, :128]
         for j in range(1, F // 128):
             folded = folded + sq[:, j * 128 : (j + 1) * 128]
-        squares[pl.ds(i, 1), :] = to_lanes(folded)
-        gained[pl.ds(pl.multiple_of(i * TILE, TILE), TILE), :] = (x * gain[...]).astype(bf16)
-        return 0
-
-    lax.fori_loop(0, NTILES, tile, 0)
+        squares[i : i + 1, :] = to_lanes(folded)
+        gained[i * TILE : (i + 1) * TILE, :] = (x * gain[...]).astype(bf16)
     for i in range(KV // 256):
         partial = jnp.dot(gained[...], weights[:, i * 256 : (i + 1) * 256], preferred_element_type=f32).astype(bf16)
         out[2 * i, :ROWS, :] = partial[:, :C]
@@ -108,35 +105,23 @@
     scales[0:4, :] = lax.rsqrt(total / D + epsilon)
     scales[4:8, :] = jnp.zeros((4, 128), f32)
 
-    def tile(i, _):
-        here = pl.ds(pl.multiple_of(i * TILE, TILE), TILE)
+    for i in range(NTILES):
+        here = slice(i * TILE, (i + 1) * TILE)
         total = got[0, here, :].astype(f32)
         for t in range(1, NT):
             total = total + got[t, here, :].astype(f32)
-        value = total * to_rows(scales[pl.ds(i, 1), :])
-        value_out[pl.ds(i * 16, 16)] = value.reshape(16, MB, C).astype(bf16)
-        goal = goals[pl.ds(i * 16, 16), :, F:].astype(f32).reshape(TILE, C)
+        value = total * to_rows(scales[i : i + 1, :])
+        value_out[i * 16 : (i + 1) * 16] = value.reshape(16, MB, C).astype(bf16)
+        goal = goals[i * 16 : (i + 1) * 16, :, F:].astype(f32).reshape(TILE, C)
         grad = (value - goal).astype(bf16)
         for t in range(NT):
             send[t, here, :] = grad
-        dots[pl.ds(i, 1), :] = to_lanes(grad.astype(f32) * value)
-        return 0
-
-    lax.fori_loop(0, NTILES, tile, 0)
+        dots[i : i + 1, :] = to_lanes(grad.astype(f32) * value)
+
     high, mid, low = parts(dots[0:4, :])
     tail = jnp.concatenate([high, mid, low, jnp.zeros_like(high)], axis=0).astype(bf16)
     for t in range(NT):
         send[t, ROWS:, :] = tail
-
-
-def normed_kernel(rows, gain, scales, normed):
-    def tile(i, _):
-        scale = to_rows(scales[pl.ds(i, 1), :])[:, :1]
-        normal = rows[pl.ds(i * 16, 16), :, :F].astype(f32).reshape(TILE, F) * scale
-        normed[pl.ds(pl.multiple_of(i * TILE, TILE), TILE), :] = (normal * gain[...]).astype(bf16)
-        return 0
-
-    lax.fori_loop(0, NTILES, tile, 0)
 
 
 def grad_kernel(got, rows, gain, weights, scales, value, back, grads, gains, scale_of, dot_of):
@@ -158,32 +143,27 @@
         grad_normed = lax.dot_general(
             grads[...], weights[at, :], (((1,), (1,)), ((), ())), preferred_element_type=f32
         )
-        scaled = grad_normed * scale_of[:, :1]
+        scaled = grad_normed * jnp.concatenate([scale_of[...]] * 2, axis=1)
         x = rows[:, :, at].astype(f32).reshape(ROWS, 256)
-        row_grad = scaled * gain[:, at] - x * dot_of[:, :1]
+        row_grad = scaled * gain[:, at] - x * jnp.concatenate([dot_of[...]] * 2, axis=1)
         back[:, :, at] = row_grad.reshape(NP, MB, 256).astype(bf16)
         gains[:, at] = jnp.sum((scaled * x).reshape(ROWS // 8, 8, 256), axis=0)
 
 
-def share_kernel(grads, normed, gains, keep, send):
+def share_kernel(grads, scales, gained, gains, keep, send):
     first = lax.axis_index("core") == 0
-
-    def block(i, _):
-        mine = lax.dot_general(
-            grads[:, pl.ds(pl.multiple_of(i * 256, 256), 256)],
-            normed[...],
-            (((0,), (0,)), ((), ())),
-            preferred_element_type=f32,
-        )
+    scale = jnp.concatenate([to_rows(scales[i : i + 1, :]) for i in range(NTILES)], axis=0)
+    scale = jnp.concatenate([scale, scale], axis=1)
+    for i in range(KV // 256):
+        scaled = (grads[:, i * 256 : (i + 1) * 256].astype(f32) * scale).astype(bf16)
+        mine = lax.dot_general(scaled, gained[...], (((0,), (0,)), ((), ())), preferred_element_type=f32)
         for j in range(8):
-            at = pl.ds(pl.multiple_of(i * 128 + j * 16, 16), 16)
+            at = slice(i * 128 + j * 16, i * 128 + (j + 1) * 16)
             even = mine[j * 32 : j * 32 + 16, :]
             odd = mine[j * 32 + 16 : j * 32 + 32, :]
             keep[at, :] = jnp.where(first, even, odd)
             send[at, :] = jnp.where(first, odd, even).astype(bf16)
-        return 0
-
-    lax.fori_loop(0, KV // 256, block, 0)
+
     total = jnp.sum(gains[...], axis=0, keepdims=True)
     keep[KV // 2 :, :] = jnp.concatenate([total, jnp.zeros((EXTRA - 1, F), f32)], axis=0)
     high, mid, low = parts(total)
@@ -274,11 +254,11 @@
         name="pack",
     )(*[pltpu.with_memory_space_constraint(v, pltpu.HBM) for v in given])
     arrived = exchange(sends, peer)
-    partials = call(
+    partials, gained = call(
         value_kernel,
-        shape(NT, ROWS + EXTRA, C),
+        (shape(NT, ROWS + EXTRA, C), shape(ROWS, F)),
         [VMEM] * 3,
-        [pltpu.VMEM((ROWS, F), bf16), pltpu.VMEM((8, 128), f32)],
+        [pltpu.VMEM((8, 128), f32)],
         flops=2 * ROWS * F * KV,
         name="partial_values",
     )(arrived, norm_gains, weights)
@@ -289,7 +269,6 @@
         [pltpu.VMEM((8, 128), f32)],
         name="loss",
     )(exchange(partials, "tp"), arrived)
-    normed = call(normed_kernel, shape(ROWS, F), [VMEM] * 3, name="normed")(arrived, norm_gains, scales)
     back, grads, gains = call(
         grad_kernel,
         (shape(NP, MB, F + C), shape(ROWS, KV), shape(8, F, dtype=f32)),
@@ -305,10 +284,10 @@
     keep, send = call(
         share_kernel,
         (shape(*half, dtype=f32), shape(*half)),
-        [VMEM] * 3,
+        [VMEM] * 4,
         flops=2 * ROWS * F * KV,
         name="share",
-    )(grads, normed, gains)
+    )(grads, scales, gained, gains)
     got = lax.ppermute(send, "core", [(0, 1), (1, 0)])
     block = (F + EXTRA, 128)
     own, *sends = call(

time: 183 us -> 181 us (0.989)
  Pallas kernels: 12.5 us -> 10.2 us
    pallas_call x3 -> x2, Pallas kernels: 4.58 us -> 2.8 us  [the longest x1 1.52 us: body(): call(share_kernel, (shape(*half, dtype=f32), shape(*half)), [VMEM] * 4, f...]
  transfers between devices with their start and end apart: 5 -> 5, of which waited for: 3 -> 2; matrix products, arithmetic and copies ran while one was open for 0% -> 0% of each run, Pallas kernels for 3% -> 2%
where the time goes in v6:
time: 181 us; the launch traced here: 178 us
  blocking collectives  129 us (71%)
  starting transfers between devices  21.4 us (12%)
  waiting for transfers between devices  16.5 us (9%)
  Pallas kernels  10.2 us (6%)
    all_to_all x4, blocking collectives, exchange(): return lax.all_to_all(v, axes, split_axis=0, concat_axis=0, tiled=True)  129 us
    all_to_all x1, waiting for transfers between devices, exchange(): return lax.all_to_all(v, axes, split_axis=0, concat_axis=0, tiled=True)  14.2 us
    ppermute x3, starting transfers between devices, body(): lax.ppermute(v, 'x', [(i, (i + d + 1) % X) for i in range(X)])  10.7 us
    all_to_all x1, starting transfers between devices, exchange(): return lax.all_to_all(v, axes, split_axis=0, concat_axis=0, tiled=True)  8.36 us
  transfers between devices with their start and end apart: 5, of which 2 were waited for; matrix products, arithmetic and copies ran while one was open for 0% of the time, Pallas kernels for 2%

profile of v6, /device:TPU:1, one launch (start us, length us, event | category | flops | bytes accessed | tf_op | source)
XLA Modules:
  0.0 178.1 jit_solution(11042810928336985313)
XLA Ops:
  0.6 1.8 %pack.1 = bf16[64,8,1152]{2,1,0:T(8,128)(2,1)S(1)} custom-call(s32[32]{0:T(128)} %bitcast.9, bf16[32,8,1024]{2,1,0:T(8,128)(2,1)} %bitcast.11, bf16[32,8,128]{2,1,0:T(8,128)(2,1)} %bitcast.12), custom_call_target="tpu_custom_call" | custom-call | bytes 4194304 | tf_op jit(solution)/shard_map/pack/pallas_call | solution.py:249
  2.5 0.0 copy-start
  2.5 0.0 copy-start.1
  2.5 46.1 %all_to_all.25.rows.goals = bf16[64,8,1152]{2,1,0:T(8,128)(2,1)S(1)} all-to-all(bf16[64,8,1152]{2,1,0:T(8,128)(2,1)S(1)} %pack.1), channel_id=1, replica_groups=mesh['x'=4,'z'=8,'core'=2,'tp'=8] {'x','z','core'}, dimensions={0} | all-to-all | bytes 2359296 | tf_op jit(solution)/shard_map/all_to_all | solution.py:241
  48.6 0.0 copy-done
  48.6 0.0 copy-done.1
  48.6 1.3 partial_values.1
  49.9 36.2 %all_to_all.26.got = bf16[8,528,128]{2,1,0:T(8,128)(2,1)S(1)} all-to-all(bf16[8,528,128]{2,1,0:T(8,128)(2,1)S(1)} %get-tuple-element.27), channel_id=1, replica_groups=mesh['x'=4,'z'=8,'core'=2,'tp'=8] {'tp'}, dimensions={0} | all-to-all | bytes 2162688 | tf_op jit(solution)/shard_map/all_to_all | solution.py:241
  86.1 0.3 loss.1
  86.4 30.5 %all_to_all.27.got = bf16[8,528,128]{2,1,0:T(8,128)(2,1)S(1)} all-to-all(bf16[8,528,128]{2,1,0:T(8,128)(2,1)S(1)} %get-tuple-element.28), channel_id=1, replica_groups=mesh['x'=4,'z'=8,'core'=2,'tp'=8] {'tp'}, dimensions={0} | all-to-all | bytes 2162688 | tf_op jit(solution)/shard_map/all_to_all | solution.py:241
  116.8 2.7 %grads.1 = (bf16[64,8,1152]{2,1,0:T(8,128)(2,1)}, bf16[512,1024]{1,0:T(8,128)(2,1)S(1)}, f32[8,1024]{1,0:T(8,128)S(1)}) custom-call(bf16[8,528,128]{2,1,0:T(8,128)(2,1)S(1)} %all_to_all.27.got, bf16[64,8,1152]{2,1,0:T(8,128)(2,1)S(1)} %all_to_all.25.rows.goals, f32[1,1024]{1,0:T(1,128)S(1)} %copy-done.1, bf16[1024,1024]{1,0:T(8,128)(2,1)S(1)} %bitcast.8, ...), custom_call_target="tpu_custom_call" | custom-call | flops 1073741824 | bytes 8388608 | tf_op jit(solution)/shard_map/grads/pallas_call | solution.py:272
  119.5 8.4 %all-to-all-start.3 = ((bf16[64,8,1152]{2,1,0:T(8,128)(2,1)}), bf16[64,8,1152]{2,1,0:T(8,128)(2,1)S(1)}, u32[]{:S(2)}, u32[]{:S(2)}) async-start(bf16[64,8,1152]{2,1,0:T(8,128)(2,1)} %get-tuple-element.39), calls=%async_computation.3 | async-start | bytes 2359296 | tf_op jit(solution)/shard_map/all_to_all | solution.py:241
  127.9 1.5 share.1
  129.4 2.4 %collective-permute-start = (bf16[528,1024]{1,0:T(8,128)(2,1)S(1)}, bf16[528,1024]{1,0:T(8,128)(2,1)S(1)}, u32[]{:S(2)}, u32[]{:S(2)}) collective-permute-start(bf16[528,1024]{1,0:T(8,128)(2,1)S(1)} %get-tuple-element.35), channel_id=1, source_target_pairs={{0,8},{8,0},{1,9},{9,1},{2,10},{10,2},{3,11},{11,3},{4,12},{12,4},... | collective-permute-start | bytes 3244040 | tf_op jit(solution)/shard_map/ppermute | solution.py:291
  131.8 2.3 %collective-permute-done.got = bf16[528,1024]{1,0:T(8,128)(2,1)S(1)} collective-permute-done((bf16[528,1024]{1,0:T(8,128)(2,1)S(1)}, bf16[528,1024]{1,0:T(8,128)(2,1)S(1)}, u32[]{:S(2)}, u32[]{:S(2)}) %collective-permute-start) | collective-permute-done | bytes 1081376 | tf_op jit(solution)/shard_map/ppermute | solution.py:291
  134.1 0.0 copy-start.2
  134.1 0.3 sum_core.1
  134.3 3.2 %collective-permute-start.1 = (bf16[1040,128]{1,0:T(8,128)(2,1)S(1)}, bf16[1040,128]{1,0:T(8,128)(2,1)S(1)}, u32[]{:S(2)}, u32[]{:S(2)}) collective-permute-start(bf16[1040,128]{1,0:T(8,128)(2,1)S(1)} %get-tuple-element.36), channel_id=1, source_target_pairs={{0,128},{128,256},{256,384},{384,0},{1,129},{129,257},{257,385},{3... | collective-permute-start | bytes 798728 | tf_op jit(solution)/shard_map/ppermute | solution.py:296
  137.6 4.5 %collective-permute-start.2 = (bf16[1040,128]{1,0:T(8,128)(2,1)S(1)}, bf16[1040,128]{1,0:T(8,128)(2,1)S(1)}, u32[]{:S(2)}, u32[]{:S(2)}) collective-permute-start(bf16[1040,128]{1,0:T(8,128)(2,1)S(1)} %get-tuple-element.37), channel_id=1, source_target_pairs={{0,256},{128,384},{256,0},{384,128},{1,257},{129,385},{257,1},{385... | collective-permute-start | bytes 798728 | tf_op jit(solution)/shard_map/ppermute | solution.py:296
  142.1 3.0 %collective-permute-start.3 = (bf16[1040,128]{1,0:T(8,128)(2,1)S(1)}, bf16[1040,128]{1,0:T(8,128)(2,1)S(1)}, u32[]{:S(2)}, u32[]{:S(2)}) collective-permute-start(bf16[1040,128]{1,0:T(8,128)(2,1)S(1)} %get-tuple-element.38), channel_id=1, source_target_pairs={{0,384},{128,0},{256,128},{384,256},{1,385},{129,1},{257,129},{385... | collective-permute-start | bytes 798728 | tf_op jit(solution)/shard_map/ppermute | solution.py:296
  145.1 14.2 %all-to-all-done.3.got = bf16[64,8,1152]{2,1,0:T(8,128)(2,1)S(1)} async-done(((bf16[64,8,1152]{2,1,0:T(8,128)(2,1)}), bf16[64,8,1152]{2,1,0:T(8,128)(2,1)S(1)}, u32[]{:S(2)}, u32[]{:S(2)}) %all-to-all-start.3) | async-done | bytes 1179680 | tf_op jit(solution)/shard_map/all_to_all | solution.py:241
  159.2 0.0 copy-done.2
  159.2 1.6 unpack.1
  160.8 0.0 collective-permute-done.1.refs_0_
  160.8 0.0 collective-permute-done.2.refs_1_
  160.8 0.0 collective-permute-done.3.refs_2_
  160.8 0.1 sum_x.1
  161.0 16.5 %all_to_all.28.got = bf16[8,144,128]{2,1,0:T(8,128)(2,1)S(1)} all-to-all(bf16[8,144,128]{2,1,0:T(8,128)(2,1)S(1)} %sum_x.1), channel_id=1, replica_groups=mesh['x'=4,'z'=8,'core'=2,'tp'=8] {'z'}, dimensions={0} | all-to-all | bytes 589824 | tf_op jit(solution)/shard_map/all_to_all | solution.py:241
  177.5 0.7 sum_z.1
Async XLA Ops:
  2.5 46.2 %copy-start = (bf16[1,1024,1024]{2,1,0:T(8,128)(2,1)S(1)}, bf16[1,1024,1024]{2,1,0:T(8,128)(2,1)}, u32[]{:S(2)}) copy-start(bf16[1,1024,1024]{2,1,0:T(8,128)(2,1)} %param.8) | copy-start | bytes 6291460
  2.5 46.1 %copy-start.1 = (f32[1,1024]{1,0:T(1,128)S(1)}, f32[1,1024]{1,0:T(1,128)}, u32[]{:S(2)}) copy-start(f32[1,1024]{1,0:T(1,128)} %gain.3) | copy-start | bytes 12292
  119.5 39.7 %all-to-all-start.3 = ((bf16[64,8,1152]{2,1,0:T(8,128)(2,1)}), bf16[64,8,1152]{2,1,0:T(8,128)(2,1)S(1)}, u32[]{:S(2)}, u32[]{:S(2)}) async-start(bf16[64,8,1152]{2,1,0:T(8,128)(2,1)} %get-tuple-element.39), calls=%async_computation.3 | async-start | bytes 2359296 | tf_op jit(solution)/shard_map/all_to_all | solution.py:241
  129.4 4.7 %collective-permute-start = (bf16[528,1024]{1,0:T(8,128)(2,1)S(1)}, bf16[528,1024]{1,0:T(8,128)(2,1)S(1)}, u32[]{:S(2)}, u32[]{:S(2)}) collective-permute-start(bf16[528,1024]{1,0:T(8,128)(2,1)S(1)} %get-tuple-element.35), channel_id=1, source_target_pairs={{0,8},{8,0},{1,9},{9,1},{2,10},{10,2},{3,11},{11,3},{4,12},{12,4},... | collective-permute-start | bytes 3244040 | tf_op jit(solution)/shard_map/ppermute | solution.py:291
  134.1 25.2 %copy-start.2 = (s32[32,1]{0,1:T(1,128)S(1)}, s32[32,1]{0,1:T(1,128)}, u32[]{:S(2)}) copy-start(s32[32,1]{0,1:T(1,128)} %param.7) | copy-start | bytes 388
  134.3 26.5 %collective-permute-start.1 = (bf16[1040,128]{1,0:T(8,128)(2,1)S(1)}, bf16[1040,128]{1,0:T(8,128)(2,1)S(1)}, u32[]{:S(2)}, u32[]{:S(2)}) collective-permute-start(bf16[1040,128]{1,0:T(8,128)(2,1)S(1)} %get-tuple-element.36), channel_id=1, source_target_pairs={{0,128},{128,256},{256,384},{384,0},{1,129},{129,257},{257,385},{3... | collective-permute-start | bytes 798728 | tf_op jit(solution)/shard_map/ppermute | solution.py:296
  137.6 23.3 %collective-permute-start.2 = (bf16[1040,128]{1,0:T(8,128)(2,1)S(1)}, bf16[1040,128]{1,0:T(8,128)(2,1)S(1)}, u32[]{:S(2)}, u32[]{:S(2)}) collective-permute-start(bf16[1040,128]{1,0:T(8,128)(2,1)S(1)} %get-tuple-element.37), channel_id=1, source_target_pairs={{0,256},{128,384},{256,0},{384,128},{1,257},{129,385},{257,1},{385... | collective-permute-start | bytes 798728 | tf_op jit(solution)/shard_map/ppermute | solution.py:296
  142.1 18.8 %collective-permute-start.3 = (bf16[1040,128]{1,0:T(8,128)(2,1)S(1)}, bf16[1040,128]{1,0:T(8,128)(2,1)S(1)}, u32[]{:S(2)}, u32[]{:S(2)}) collective-permute-start(bf16[1040,128]{1,0:T(8,128)(2,1)S(1)} %get-tuple-element.38), channel_id=1, source_target_pairs={{0,384},{128,0},{256,128},{384,256},{1,385},{129,1},{257,129},{385... | collective-permute-start | bytes 798728 | tf_op jit(solution)/shard_map/ppermute | solution.py:296

commit v7 on v6

--- a/solution.py
+++ b/solution.py
@@ -28,12 +28,12 @@
 SMEM = pl.BlockSpec(memory_space=pltpu.SMEM)
 
 
-def call(kernel, outs, in_specs, scratch=(), flops=0, size=4 << 20, name=None):
+def call(kernel, outs, in_specs, scratch=(), out_specs=None, flops=0, size=4 << 20, name=None):
     return pl.pallas_call(
         kernel,
         out_shape=outs,
         in_specs=in_specs,
-        out_specs=jax.tree.map(lambda _: VMEM, outs),
+        out_specs=jax.tree.map(lambda _: VMEM, outs) if out_specs is None else out_specs,
         scratch_shapes=scratch,
         compiler_params=pltpu.CompilerParams(vmem_limit_bytes=40 << 20),
         cost_estimate=pl.CostEstimate(flops=flops, bytes_accessed=size, transcendentals=0),
@@ -56,26 +56,30 @@
     return jnp.broadcast_to(lanes, (TILE, TILE)).T
 
 
-def pack_kernel(routes, acts, goals, out, order, route_sem, row_sem, goal_sem):
-    fetch = pltpu.make_async_copy(routes, order, route_sem)
-    fetch.start()
+def pack_kernel(routes, acts, goals, out, order, rows, columns, route_sem, row_sem, goal_sem):
+    copies = [
+        pltpu.make_async_copy(routes, order, route_sem),
+        pltpu.make_async_copy(acts, rows, row_sem),
+        pltpu.make_async_copy(goals, columns, goal_sem),
+    ]
+    for copy in copies:
+        copy.start()
 
     def clear(d, _):
         out[pl.ds(d * 4, 4)] = jnp.zeros((4, MB, F + C), bf16)
         return 0
 
     lax.fori_loop(0, NP // 4, clear, 0)
-    fetch.wait()
-
-    def send(m, _):
+    for copy in copies:
+        copy.wait()
+
+    def put(m, _):
         d = order[m]
-        pltpu.make_async_copy(acts.at[m], out.at[d, :, pl.ds(0, F)], row_sem).start()
-        pltpu.make_async_copy(goals.at[m], out.at[d, :, pl.ds(F, C)], goal_sem).start()
+        out[d, :, :F] = rows[m]
+        out[d, :, F:] = columns[m]
         return 0
 
-    lax.fori_loop(0, PIECES, send, 0)
-    pltpu.make_async_copy(acts, out.at[pl.ds(0, PIECES), :, pl.ds(0, F)], row_sem).wait()
-    pltpu.make_async_copy(goals, out.at[pl.ds(0, PIECES), :, pl.ds(F, C)], goal_sem).wait()
+    lax.fori_loop(0, PIECES, put, 0, unroll=4)
 
 
 def value_kernel(rows, gain, weights, out, gained, squares):
@@ -124,30 +128,43 @@
         send[t, ROWS:, :] = tail
 
 
-def grad_kernel(got, rows, gain, weights, scales, value, back, grads, gains, scale_of, dot_of):
+def grad_kernel(got, rows, gain, weights, scales, value, back, grads, gains, made, sems):
     tail = got[0, ROWS:, :].astype(f32)
     for t in range(1, NT):
         tail = tail + got[t, ROWS:, :].astype(f32)
     dots = (tail[0:4] + tail[4:8] + tail[8:12]) / D
-    for i in range(NTILES):
-        here = slice(i * TILE, (i + 1) * TILE)
-        scale = scales[i : i + 1, :]
-        scale_of[here, :] = to_rows(scale)
-        dot_of[here, :] = to_rows(scale * scale * dots[i : i + 1, :])
-    for t in range(NT):
-        grads[:, t * C : (t + 1) * C] = got[t, :ROWS, :]
-    back[:, :, F:] = value[...]
-
+    copies = []
+    sums = [0.0] * (F // 256)
+    for half in range(2):
+        here = slice(half * ROWS // 2, (half + 1) * ROWS // 2)
+        slots = slice(half * NP // 2, (half + 1) * NP // 2)
+        for t in range(NT):
+            grads[here, t * C : (t + 1) * C] = got[t, here, :]
+        tiles = range(half * NTILES // 2, (half + 1) * NTILES // 2)
+        scale = [scales[i : i + 1, :] for i in tiles]
+        dot = [v * v * dots[i : i + 1, :] for i, v in zip(tiles, scale)]
+        scale = jnp.concatenate([to_rows(v) for v in scale], axis=0)
+        scale = jnp.concatenate([scale, scale], axis=1)
+        dot = jnp.concatenate([to_rows(v) for v in dot], axis=0)
+        dot = jnp.concatenate([dot, dot], axis=1)
+        made[slots, :, F:] = value[slots]
+        for i in range(F // 256):
+            at = slice(i * 256, (i + 1) * 256)
+            grad_normed = lax.dot_general(
+                grads[here, :], weights[at, :], (((1,), (1,)), ((), ())), preferred_element_type=f32
+            )
+            scaled = grad_normed * scale
+            x = rows[slots, :, at].astype(f32).reshape(ROWS // 2, 256)
+            row_grad = scaled * gain[:, at] - x * dot
+            made[slots, :, at] = row_grad.reshape(NP // 2, MB, 256).astype(bf16)
+            sums[i] += jnp.sum((scaled * x).reshape(ROWS // 16, 8, 256), axis=0)
+        where = pl.ds(half * NP // 2, NP // 2)
+        copies.append(pltpu.make_async_copy(made.at[where], back.at[where], sems.at[half]))
+        copies[-1].start()
     for i in range(F // 256):
-        at = slice(i * 256, (i + 1) * 256)
-        grad_normed = lax.dot_general(
-            grads[...], weights[at, :], (((1,), (1,)), ((), ())), preferred_element_type=f32
-        )
-        scaled = grad_normed * jnp.concatenate([scale_of[...]] * 2, axis=1)
-        x = rows[:, :, at].astype(f32).reshape(ROWS, 256)
-        row_grad = scaled * gain[:, at] - x * jnp.concatenate([dot_of[...]] * 2, axis=1)
-        back[:, :, at] = row_grad.reshape(NP, MB, 256).astype(bf16)
-        gains[:, at] = jnp.sum((scaled * x).reshape(ROWS // 8, 8, 256), axis=0)
+        gains[:, i * 256 : (i + 1) * 256] = sums[i]
+    for copy in copies:
+        copy.wait()
 
 
 def share_kernel(grads, scales, gained, gains, keep, send):
@@ -250,7 +267,12 @@
         pack_kernel,
         shape(NP, MB, F + C),
         [HBM] * 3,
-        [pltpu.SMEM((PIECES,), jnp.int32)] + [pltpu.SemaphoreType.DMA] * 3,
+        [
+            pltpu.SMEM((PIECES,), jnp.int32),
+            pltpu.VMEM((PIECES, MB, F), bf16),
+            pltpu.VMEM((PIECES, MB, C), bf16),
+        ]
+        + [pltpu.SemaphoreType.DMA] * 3,
         name="pack",
     )(*[pltpu.with_memory_space_constraint(v, pltpu.HBM) for v in given])
     arrived = exchange(sends, peer)
@@ -273,7 +295,8 @@
         grad_kernel,
         (shape(NP, MB, F + C), shape(ROWS, KV), shape(8, F, dtype=f32)),
         [VMEM] * 6,
-        [pltpu.VMEM((ROWS, 128), f32)] * 2,
+        [pltpu.VMEM((NP, MB, F + C), bf16), pltpu.SemaphoreType.DMA((2,))],
+        out_specs=(HBM, VMEM, VMEM),
         flops=2 * ROWS * F * KV,
         size=8 << 20,
         name="grads",

time: 181 us -> 181 us (level)
  no operation moved by 1% of the time
where the time goes in v7:
time: 181 us; the launch traced here: 177 us
  blocking collectives  129 us (71%)
  starting transfers between devices  21.4 us (12%)
  waiting for transfers between devices  16.5 us (9%)
  Pallas kernels  9.5 us (5%)
    all_to_all x4, blocking collectives, exchange(): return lax.all_to_all(v, axes, split_axis=0, concat_axis=0, tiled=True)  129 us
    all_to_all x1, waiting for transfers between devices, exchange(): return lax.all_to_all(v, axes, split_axis=0, concat_axis=0, tiled=True)  14.2 us
    ppermute x3, starting transfers between devices, body(): lax.ppermute(v, 'x', [(i, (i + d + 1) % X) for i in range(X)])  10.7 us
    all_to_all x1, starting transfers between devices, exchange(): return lax.all_to_all(v, axes, split_axis=0, concat_axis=0, tiled=True)  8.37 us
  transfers between devices with their start and end apart: 5, of which 2 were waited for; matrix products, arithmetic and copies ran while one was open for 0% of the time, Pallas kernels for 2%

profile of v7, /device:TPU:1, one launch (start us, length us, event | category | flops | bytes accessed | tf_op | source)
XLA Modules:
  0.0 177.4 jit_solution(14384043201184791714)
XLA Ops:
  0.6 1.2 pack.1
  1.8 0.0 copy-start
  1.8 0.0 copy-start.1
  1.8 46.1 %all_to_all.25.rows.goals = bf16[64,8,1152]{2,1,0:T(8,128)(2,1)S(1)} all-to-all(bf16[64,8,1152]{2,1,0:T(8,128)(2,1)S(1)} %pack.1), channel_id=1, replica_groups=mesh['x'=4,'z'=8,'core'=2,'tp'=8] {'x','z','core'}, dimensions={0} | all-to-all | bytes 2359296 | tf_op jit(solution)/shard_map/all_to_all | solution.py:258
  48.0 0.0 copy-done
  48.0 0.0 copy-done.1
  48.0 1.3 partial_values.1
  49.3 36.1 %all_to_all.26.got = bf16[8,528,128]{2,1,0:T(8,128)(2,1)S(1)} all-to-all(bf16[8,528,128]{2,1,0:T(8,128)(2,1)S(1)} %get-tuple-element.27), channel_id=1, replica_groups=mesh['x'=4,'z'=8,'core'=2,'tp'=8] {'tp'}, dimensions={0} | all-to-all | bytes 2162688 | tf_op jit(solution)/shard_map/all_to_all | solution.py:258
  85.4 0.3 loss.1
  85.7 30.5 %all_to_all.27.got = bf16[8,528,128]{2,1,0:T(8,128)(2,1)S(1)} all-to-all(bf16[8,528,128]{2,1,0:T(8,128)(2,1)S(1)} %get-tuple-element.28), channel_id=1, replica_groups=mesh['x'=4,'z'=8,'core'=2,'tp'=8] {'tp'}, dimensions={0} | all-to-all | bytes 2162688 | tf_op jit(solution)/shard_map/all_to_all | solution.py:258
  116.2 2.6 %grads.1 = (bf16[64,8,1152]{2,1,0:T(8,128)(2,1)}, bf16[512,1024]{1,0:T(8,128)(2,1)S(1)}, f32[8,1024]{1,0:T(8,128)S(1)}) custom-call(bf16[8,528,128]{2,1,0:T(8,128)(2,1)S(1)} %all_to_all.27.got, bf16[64,8,1152]{2,1,0:T(8,128)(2,1)S(1)} %all_to_all.25.rows.goals, f32[1,1024]{1,0:T(1,128)S(1)} %copy-done.1, bf16[1024,1024]{1,0:T(8,128)(2,1)S(1)} %bitcast.8, ...), custom_call_target="tpu_custom_call" | custom-call | flops 1073741824 | bytes 8388608 | tf_op jit(solution)/shard_map/grads/pallas_call | solution.py:294
  118.7 8.4 %all-to-all-start.3 = ((bf16[64,8,1152]{2,1,0:T(8,128)(2,1)}), bf16[64,8,1152]{2,1,0:T(8,128)(2,1)S(1)}, u32[]{:S(2)}, u32[]{:S(2)}) async-start(bf16[64,8,1152]{2,1,0:T(8,128)(2,1)} %get-tuple-element.39), calls=%async_computation.3 | async-start | bytes 2359296 | tf_op jit(solution)/shard_map/all_to_all | solution.py:258
  127.1 1.5 share.1
  128.7 2.4 %collective-permute-start = (bf16[528,1024]{1,0:T(8,128)(2,1)S(1)}, bf16[528,1024]{1,0:T(8,128)(2,1)S(1)}, u32[]{:S(2)}, u32[]{:S(2)}) collective-permute-start(bf16[528,1024]{1,0:T(8,128)(2,1)S(1)} %get-tuple-element.35), channel_id=1, source_target_pairs={{0,8},{8,0},{1,9},{9,1},{2,10},{10,2},{3,11},{11,3},{4,12},{12,4},... | collective-permute-start | bytes 3244040 | tf_op jit(solution)/shard_map/ppermute | solution.py:314
  131.0 2.3 %collective-permute-done.got = bf16[528,1024]{1,0:T(8,128)(2,1)S(1)} collective-permute-done((bf16[528,1024]{1,0:T(8,128)(2,1)S(1)}, bf16[528,1024]{1,0:T(8,128)(2,1)S(1)}, u32[]{:S(2)}, u32[]{:S(2)}) %collective-permute-start) | collective-permute-done | bytes 1081376 | tf_op jit(solution)/shard_map/ppermute | solution.py:314
  133.3 0.0 copy-start.2
  133.3 0.3 sum_core.1
  133.6 3.2 %collective-permute-start.1 = (bf16[1040,128]{1,0:T(8,128)(2,1)S(1)}, bf16[1040,128]{1,0:T(8,128)(2,1)S(1)}, u32[]{:S(2)}, u32[]{:S(2)}) collective-permute-start(bf16[1040,128]{1,0:T(8,128)(2,1)S(1)} %get-tuple-element.36), channel_id=1, source_target_pairs={{0,128},{128,256},{256,384},{384,0},{1,129},{129,257},{257,385},{3... | collective-permute-start | bytes 798728 | tf_op jit(solution)/shard_map/ppermute | solution.py:319
  136.8 4.5 %collective-permute-start.2 = (bf16[1040,128]{1,0:T(8,128)(2,1)S(1)}, bf16[1040,128]{1,0:T(8,128)(2,1)S(1)}, u32[]{:S(2)}, u32[]{:S(2)}) collective-permute-start(bf16[1040,128]{1,0:T(8,128)(2,1)S(1)} %get-tuple-element.37), channel_id=1, source_target_pairs={{0,256},{128,384},{256,0},{384,128},{1,257},{129,385},{257,1},{385... | collective-permute-start | bytes 798728 | tf_op jit(solution)/shard_map/ppermute | solution.py:319
  141.3 3.0 %collective-permute-start.3 = (bf16[1040,128]{1,0:T(8,128)(2,1)S(1)}, bf16[1040,128]{1,0:T(8,128)(2,1)S(1)}, u32[]{:S(2)}, u32[]{:S(2)}) collective-permute-start(bf16[1040,128]{1,0:T(8,128)(2,1)S(1)} %get-tuple-element.38), channel_id=1, source_target_pairs={{0,384},{128,0},{256,128},{384,256},{1,385},{129,1},{257,129},{385... | collective-permute-start | bytes 798728 | tf_op jit(solution)/shard_map/ppermute | solution.py:319
  144.3 14.2 %all-to-all-done.3.got = bf16[64,8,1152]{2,1,0:T(8,128)(2,1)S(1)} async-done(((bf16[64,8,1152]{2,1,0:T(8,128)(2,1)}), bf16[64,8,1152]{2,1,0:T(8,128)(2,1)S(1)}, u32[]{:S(2)}, u32[]{:S(2)}) %all-to-all-start.3) | async-done | bytes 1179680 | tf_op jit(solution)/shard_map/all_to_all | solution.py:258
  158.5 0.0 copy-done.2
  158.5 1.6 unpack.1
  160.1 0.0 collective-permute-done.1.refs_0_
  160.1 0.0 collective-permute-done.2.refs_1_
  160.1 0.0 collective-permute-done.3.refs_2_
  160.1 0.1 sum_x.1
  160.2 16.5 %all_to_all.28.got = bf16[8,144,128]{2,1,0:T(8,128)(2,1)S(1)} all-to-all(bf16[8,144,128]{2,1,0:T(8,128)(2,1)S(1)} %sum_x.1), channel_id=1, replica_groups=mesh['x'=4,'z'=8,'core'=2,'tp'=8] {'z'}, dimensions={0} | all-to-all | bytes 589824 | tf_op jit(solution)/shard_map/all_to_all | solution.py:258
  176.7 0.7 sum_z.1
Async XLA Ops:
  1.8 46.2 %copy-start = (bf16[1,1024,1024]{2,1,0:T(8,128)(2,1)S(1)}, bf16[1,1024,1024]{2,1,0:T(8,128)(2,1)}, u32[]{:S(2)}) copy-start(bf16[1,1024,1024]{2,1,0:T(8,128)(2,1)} %param.8) | copy-start | bytes 6291460
  1.8 46.1 %copy-start.1 = (f32[1,1024]{1,0:T(1,128)S(1)}, f32[1,1024]{1,0:T(1,128)}, u32[]{:S(2)}) copy-start(f32[1,1024]{1,0:T(1,128)} %gain.3) | copy-start | bytes 12292
  118.7 39.7 %all-to-all-start.3 = ((bf16[64,8,1152]{2,1,0:T(8,128)(2,1)}), bf16[64,8,1152]{2,1,0:T(8,128)(2,1)S(1)}, u32[]{:S(2)}, u32[]{:S(2)}) async-start(bf16[64,8,1152]{2,1,0:T(8,128)(2,1)} %get-tuple-element.39), calls=%async_computation.3 | async-start | bytes 2359296 | tf_op jit(solution)/shard_map/all_to_all | solution.py:258
  128.7 4.7 %collective-permute-start = (bf16[528,1024]{1,0:T(8,128)(2,1)S(1)}, bf16[528,1024]{1,0:T(8,128)(2,1)S(1)}, u32[]{:S(2)}, u32[]{:S(2)}) collective-permute-start(bf16[528,1024]{1,0:T(8,128)(2,1)S(1)} %get-tuple-element.35), channel_id=1, source_target_pairs={{0,8},{8,0},{1,9},{9,1},{2,10},{10,2},{3,11},{11,3},{4,12},{12,4},... | collective-permute-start | bytes 3244040 | tf_op jit(solution)/shard_map/ppermute | solution.py:314
  133.3 25.1 %copy-start.2 = (s32[32,1]{0,1:T(1,128)S(1)}, s32[32,1]{0,1:T(1,128)}, u32[]{:S(2)}) copy-start(s32[32,1]{0,1:T(1,128)} %param.7) | copy-start | bytes 388
  133.6 26.5 %collective-permute-start.1 = (bf16[1040,128]{1,0:T(8,128)(2,1)S(1)}, bf16[1040,128]{1,0:T(8,128)(2,1)S(1)}, u32[]{:S(2)}, u32[]{:S(2)}) collective-permute-start(bf16[1040,128]{1,0:T(8,128)(2,1)S(1)} %get-tuple-element.36), channel_id=1, source_target_pairs={{0,128},{128,256},{256,384},{384,0},{1,129},{129,257},{257,385},{3... | collective-permute-start | bytes 798728 | tf_op jit(solution)/shard_map/ppermute | solution.py:319
  136.8 23.3 %collective-permute-start.2 = (bf16[1040,128]{1,0:T(8,128)(2,1)S(1)}, bf16[1040,128]{1,0:T(8,128)(2,1)S(1)}, u32[]{:S(2)}, u32[]{:S(2)}) collective-permute-start(bf16[1040,128]{1,0:T(8,128)(2,1)S(1)} %get-tuple-element.37), channel_id=1, source_target_pairs={{0,256},{128,384},{256,0},{384,128},{1,257},{129,385},{257,1},{385... | collective-permute-start | bytes 798728 | tf_op jit(solution)/shard_map/ppermute | solution.py:319
  141.3 18.8 %collective-permute-start.3 = (bf16[1040,128]{1,0:T(8,128)(2,1)S(1)}, bf16[1040,128]{1,0:T(8,128)(2,1)S(1)}, u32[]{:S(2)}, u32[]{:S(2)}) collective-permute-start(bf16[1040,128]{1,0:T(8,128)(2,1)S(1)} %get-tuple-element.38), channel_id=1, source_target_pairs={{0,384},{128,0},{256,128},{384,256},{1,385},{129,1},{257,129},{385... | collective-permute-start | bytes 798728 | tf_op jit(solution)/shard_map/ppermute | solution.py:319

commit v8 on v7

--- a/solution.py
+++ b/solution.py
@@ -14,6 +14,7 @@
 NP = 64
 NT = 8
 X, Z, CORES = 4, 8, 2
+X_STEPS = (2, 1, 3)
 ROWS = NP * MB
 TILE = 128
 NTILES = ROWS // TILE
@@ -206,8 +207,8 @@
             out[j * 128 : (j + 1) * 128, :] = total[:, j * 128 : (j + 1) * 128].astype(out.dtype)
         out[F:, :] = tail
 
-    for d, send in enumerate(sends):
-        put(send, d + 1, gain_tail(tail))
+    for d, send in zip(X_STEPS, sends):
+        put(send, d, gain_tail(tail))
     put(own, 0, jnp.concatenate([tail, jnp.zeros_like(tail)], axis=0))
 
 
@@ -316,7 +317,7 @@
     own, *sends = call(
         core_kernel, (shape(*block, dtype=f32),) + (shape(*block),) * (X - 1), [VMEM] * 2, name="sum_core"
     )(keep, got)
-    got = [lax.ppermute(v, "x", [(i, (i + d + 1) % X) for i in range(X)]) for d, v in enumerate(sends)]
+    got = [lax.ppermute(v, "x", [(i, (i + d) % X) for i in range(X)]) for d, v in zip(X_STEPS, sends)]
     grad_rows, values = call(
         unpack_kernel,
         (shape(PIECES, MB, F), shape(PIECES, MB, C)),

time: 181 us -> 179 us (0.989)
  no operation moved by 1% of the time
where the time goes in v8:
time: 179 us; the launch traced here: 177 us
  blocking collectives  129 us (72%)
  starting transfers between devices  22 us (12%)
  waiting for transfers between devices  15.9 us (9%)
  Pallas kernels  9.5 us (5%)
    all_to_all x4, blocking collectives, exchange(): return lax.all_to_all(v, axes, split_axis=0, concat_axis=0, tiled=True)  129 us
    all_to_all x1, waiting for transfers between devices, exchange(): return lax.all_to_all(v, axes, split_axis=0, concat_axis=0, tiled=True)  13.6 us
    ppermute x3, starting transfers between devices, body(): lax.ppermute(v, 'x', [(i, (i + d) % X) for i in range(X)])  11.3 us
    all_to_all x1, starting transfers between devices, exchange(): return lax.all_to_all(v, axes, split_axis=0, concat_axis=0, tiled=True)  8.37 us
  transfers between devices with their start and end apart: 5, of which 2 were waited for; matrix products, arithmetic and copies ran while one was open for 0% of the time, Pallas kernels for 2%

profile of v8, /device:TPU:1, one launch (start us, length us, event | category | flops | bytes accessed | tf_op | source)
XLA Modules:
  0.0 176.7 jit_solution(15262028573039363719)
XLA Ops:
  0.6 1.2 pack.1
  1.8 0.0 copy-start
  1.8 0.0 copy-start.1
  1.8 46.1 %all_to_all.25.rows.goals = bf16[64,8,1152]{2,1,0:T(8,128)(2,1)S(1)} all-to-all(bf16[64,8,1152]{2,1,0:T(8,128)(2,1)S(1)} %pack.1), channel_id=1, replica_groups=mesh['x'=4,'z'=8,'core'=2,'tp'=8] {'x','z','core'}, dimensions={0} | all-to-all | bytes 2359296 | tf_op jit(solution)/shard_map/all_to_all | solution.py:259
  48.0 0.0 copy-done
  48.0 0.0 copy-done.1
  48.0 1.3 partial_values.1
  49.3 36.1 %all_to_all.26.got = bf16[8,528,128]{2,1,0:T(8,128)(2,1)S(1)} all-to-all(bf16[8,528,128]{2,1,0:T(8,128)(2,1)S(1)} %get-tuple-element.27), channel_id=1, replica_groups=mesh['x'=4,'z'=8,'core'=2,'tp'=8] {'tp'}, dimensions={0} | all-to-all | bytes 2162688 | tf_op jit(solution)/shard_map/all_to_all | solution.py:259
  85.4 0.3 loss.1
  85.7 30.5 %all_to_all.27.got = bf16[8,528,128]{2,1,0:T(8,128)(2,1)S(1)} all-to-all(bf16[8,528,128]{2,1,0:T(8,128)(2,1)S(1)} %get-tuple-element.28), channel_id=1, replica_groups=mesh['x'=4,'z'=8,'core'=2,'tp'=8] {'tp'}, dimensions={0} | all-to-all | bytes 2162688 | tf_op jit(solution)/shard_map/all_to_all | solution.py:259
  116.2 2.6 %grads.1 = (bf16[64,8,1152]{2,1,0:T(8,128)(2,1)}, bf16[512,1024]{1,0:T(8,128)(2,1)S(1)}, f32[8,1024]{1,0:T(8,128)S(1)}) custom-call(bf16[8,528,128]{2,1,0:T(8,128)(2,1)S(1)} %all_to_all.27.got, bf16[64,8,1152]{2,1,0:T(8,128)(2,1)S(1)} %all_to_all.25.rows.goals, f32[1,1024]{1,0:T(1,128)S(1)} %copy-done.1, bf16[1024,1024]{1,0:T(8,128)(2,1)S(1)} %bitcast.8, ...), custom_call_target="tpu_custom_call" | custom-call | flops 1073741824 | bytes 8388608 | tf_op jit(solution)/shard_map/grads/pallas_call | solution.py:295
  118.7 8.4 %all-to-all-start.3 = ((bf16[64,8,1152]{2,1,0:T(8,128)(2,1)}), bf16[64,8,1152]{2,1,0:T(8,128)(2,1)S(1)}, u32[]{:S(2)}, u32[]{:S(2)}) async-start(bf16[64,8,1152]{2,1,0:T(8,128)(2,1)} %get-tuple-element.39), calls=%async_computation.3 | async-start | bytes 2359296 | tf_op jit(solution)/shard_map/all_to_all | solution.py:259
  127.1 1.5 share.1
  128.7 2.4 %collective-permute-start = (bf16[528,1024]{1,0:T(8,128)(2,1)S(1)}, bf16[528,1024]{1,0:T(8,128)(2,1)S(1)}, u32[]{:S(2)}, u32[]{:S(2)}) collective-permute-start(bf16[528,1024]{1,0:T(8,128)(2,1)S(1)} %get-tuple-element.35), channel_id=1, source_target_pairs={{0,8},{8,0},{1,9},{9,1},{2,10},{10,2},{3,11},{11,3},{4,12},{12,4},... | collective-permute-start | bytes 3244040 | tf_op jit(solution)/shard_map/ppermute | solution.py:315
  131.0 2.3 %collective-permute-done.got = bf16[528,1024]{1,0:T(8,128)(2,1)S(1)} collective-permute-done((bf16[528,1024]{1,0:T(8,128)(2,1)S(1)}, bf16[528,1024]{1,0:T(8,128)(2,1)S(1)}, u32[]{:S(2)}, u32[]{:S(2)}) %collective-permute-start) | collective-permute-done | bytes 1081376 | tf_op jit(solution)/shard_map/ppermute | solution.py:315
  133.3 0.0 copy-start.2
  133.3 0.3 sum_core.1
  133.6 4.8 %collective-permute-start.1 = (bf16[1040,128]{1,0:T(8,128)(2,1)S(1)}, bf16[1040,128]{1,0:T(8,128)(2,1)S(1)}, u32[]{:S(2)}, u32[]{:S(2)}) collective-permute-start(bf16[1040,128]{1,0:T(8,128)(2,1)S(1)} %get-tuple-element.36), channel_id=1, source_target_pairs={{0,256},{128,384},{256,0},{384,128},{1,257},{129,385},{257,1},{385... | collective-permute-start | bytes 798728 | tf_op jit(solution)/shard_map/ppermute | solution.py:320
  138.4 2.3 %collective-permute-start.2 = (bf16[1040,128]{1,0:T(8,128)(2,1)S(1)}, bf16[1040,128]{1,0:T(8,128)(2,1)S(1)}, u32[]{:S(2)}, u32[]{:S(2)}) collective-permute-start(bf16[1040,128]{1,0:T(8,128)(2,1)S(1)} %get-tuple-element.37), channel_id=1, source_target_pairs={{0,128},{128,256},{256,384},{384,0},{1,129},{129,257},{257,385},{3... | collective-permute-start | bytes 798728 | tf_op jit(solution)/shard_map/ppermute | solution.py:320
  140.7 4.2 %collective-permute-start.3 = (bf16[1040,128]{1,0:T(8,128)(2,1)S(1)}, bf16[1040,128]{1,0:T(8,128)(2,1)S(1)}, u32[]{:S(2)}, u32[]{:S(2)}) collective-permute-start(bf16[1040,128]{1,0:T(8,128)(2,1)S(1)} %get-tuple-element.38), channel_id=1, source_target_pairs={{0,384},{128,0},{256,128},{384,256},{1,385},{129,1},{257,129},{385... | collective-permute-start | bytes 798728 | tf_op jit(solution)/shard_map/ppermute | solution.py:320
  144.9 13.6 %all-to-all-done.3.got = bf16[64,8,1152]{2,1,0:T(8,128)(2,1)S(1)} async-done(((bf16[64,8,1152]{2,1,0:T(8,128)(2,1)}), bf16[64,8,1152]{2,1,0:T(8,128)(2,1)S(1)}, u32[]{:S(2)}, u32[]{:S(2)}) %all-to-all-start.3) | async-done | bytes 1179680 | tf_op jit(solution)/shard_map/all_to_all | solution.py:259
  158.5 0.0 copy-done.2
  158.5 1.6 unpack.1
  160.1 0.0 collective-permute-done.1.refs_0_
  160.1 0.0 collective-permute-done.2.refs_1_
  160.1 0.0 collective-permute-done.3.refs_2_
  160.1 0.1 sum_x.1
  160.2 15.8 %all_to_all.28.got = bf16[8,144,128]{2,1,0:T(8,128)(2,1)S(1)} all-to-all(bf16[8,144,128]{2,1,0:T(8,128)(2,1)S(1)} %sum_x.1), channel_id=1, replica_groups=mesh['x'=4,'z'=8,'core'=2,'tp'=8] {'z'}, dimensions={0} | all-to-all | bytes 589824 | tf_op jit(solution)/shard_map/all_to_all | solution.py:259
  176.0 0.7 sum_z.1
Async XLA Ops:
  1.8 46.2 %copy-start = (bf16[1,1024,1024]{2,1,0:T(8,128)(2,1)S(1)}, bf16[1,1024,1024]{2,1,0:T(8,128)(2,1)}, u32[]{:S(2)}) copy-start(bf16[1,1024,1024]{2,1,0:T(8,128)(2,1)} %param.8) | copy-start | bytes 6291460
  1.8 46.1 %copy-start.1 = (f32[1,1024]{1,0:T(1,128)S(1)}, f32[1,1024]{1,0:T(1,128)}, u32[]{:S(2)}) copy-start(f32[1,1024]{1,0:T(1,128)} %gain.3) | copy-start | bytes 12292
  118.7 39.7 %all-to-all-start.3 = ((bf16[64,8,1152]{2,1,0:T(8,128)(2,1)}), bf16[64,8,1152]{2,1,0:T(8,128)(2,1)S(1)}, u32[]{:S(2)}, u32[]{:S(2)}) async-start(bf16[64,8,1152]{2,1,0:T(8,128)(2,1)} %get-tuple-element.39), calls=%async_computation.3 | async-start | bytes 2359296 | tf_op jit(solution)/shard_map/all_to_all | solution.py:259
  128.7 4.7 %collective-permute-start = (bf16[528,1024]{1,0:T(8,128)(2,1)S(1)}, bf16[528,1024]{1,0:T(8,128)(2,1)S(1)}, u32[]{:S(2)}, u32[]{:S(2)}) collective-permute-start(bf16[528,1024]{1,0:T(8,128)(2,1)S(1)} %get-tuple-element.35), channel_id=1, source_target_pairs={{0,8},{8,0},{1,9},{9,1},{2,10},{10,2},{3,11},{11,3},{4,12},{12,4},... | collective-permute-start | bytes 3244040 | tf_op jit(solution)/shard_map/ppermute | solution.py:315
  133.3 25.1 %copy-start.2 = (s32[32,1]{0,1:T(1,128)S(1)}, s32[32,1]{0,1:T(1,128)}, u32[]{:S(2)}) copy-start(s32[32,1]{0,1:T(1,128)} %param.7) | copy-start | bytes 388
  133.6 26.5 %collective-permute-start.1 = (bf16[1040,128]{1,0:T(8,128)(2,1)S(1)}, bf16[1040,128]{1,0:T(8,128)(2,1)S(1)}, u32[]{:S(2)}, u32[]{:S(2)}) collective-permute-start(bf16[1040,128]{1,0:T(8,128)(2,1)S(1)} %get-tuple-element.36), channel_id=1, source_target_pairs={{0,256},{128,384},{256,0},{384,128},{1,257},{129,385},{257,1},{385... | collective-permute-start | bytes 798728 | tf_op jit(solution)/shard_map/ppermute | solution.py:320
  138.4 21.7 %collective-permute-start.2 = (bf16[1040,128]{1,0:T(8,128)(2,1)S(1)}, bf16[1040,128]{1,0:T(8,128)(2,1)S(1)}, u32[]{:S(2)}, u32[]{:S(2)}) collective-permute-start(bf16[1040,128]{1,0:T(8,128)(2,1)S(1)} %get-tuple-element.37), channel_id=1, source_target_pairs={{0,128},{128,256},{256,384},{384,0},{1,129},{129,257},{257,385},{3... | collective-permute-start | bytes 798728 | tf_op jit(solution)/shard_map/ppermute | solution.py:320
  140.7 19.4 %collective-permute-start.3 = (bf16[1040,128]{1,0:T(8,128)(2,1)S(1)}, bf16[1040,128]{1,0:T(8,128)(2,1)S(1)}, u32[]{:S(2)}, u32[]{:S(2)}) collective-permute-start(bf16[1040,128]{1,0:T(8,128)(2,1)S(1)} %get-tuple-element.38), channel_id=1, source_target_pairs={{0,384},{128,0},{256,128},{384,256},{1,385},{129,1},{257,129},{385... | collective-permute-start | bytes 798728 | tf_op jit(solution)/shard_map/ppermute | solution.py:320

commit v9 on v8

--- a/solution.py
+++ b/solution.py
@@ -201,7 +201,7 @@
     tail = jnp.concatenate([tail[:, j * 128 : (j + 1) * 128] for j in range(F // 128)], axis=0)
 
     def put(out, d, tail):
-        there = pl.ds(pl.multiple_of(lax.rem(me + d, X) * 128, 128), 128)
+        there = pl.ds(pl.multiple_of((me ^ d) * 128, 128), 128)
         total = keep[there, :] + got[there, :].astype(f32)
         for j in range(F // 128):
             out[j * 128 : (j + 1) * 128, :] = total[:, j * 128 : (j + 1) * 128].astype(out.dtype)
@@ -317,7 +317,7 @@
     own, *sends = call(
         core_kernel, (shape(*block, dtype=f32),) + (shape(*block),) * (X - 1), [VMEM] * 2, name="sum_core"
     )(keep, got)
-    got = [lax.ppermute(v, "x", [(i, (i + d) % X) for i in range(X)]) for d, v in zip(X_STEPS, sends)]
+    got = [lax.ppermute(v, "x", [(i, i ^ d) for i in range(X)]) for d, v in zip(X_STEPS, sends)]
     grad_rows, values = call(
         unpack_kernel,
         (shape(PIECES, MB, F), shape(PIECES, MB, C)),

time: 179 us -> 179 us (level)
  waiting for transfers between devices: 15.9 us -> 17.8 us
  starting transfers between devices: 22 us -> 20.2 us
    all_to_all x1, waiting for transfers between devices: 13.6 us -> 15.4 us  [exchange(): return lax.all_to_all(v, axes, split_axis=0, concat_axis=0, tiled=True)]
    ppermute x3, starting transfers between devices: 11.3 us -> 9.43 us  [body(): lax.ppermute(v, 'x', [(i, i ^ d) for i in range(X)])]
where the time goes in v9:
time: 179 us; the launch traced here: 177 us
  blocking collectives  129 us (72%)
  starting transfers between devices  20.2 us (11%)
  waiting for transfers between devices  17.8 us (10%)
  Pallas kernels  9.49 us (5%)
    all_to_all x4, blocking collectives, exchange(): return lax.all_to_all(v, axes, split_axis=0, concat_axis=0, tiled=True)  129 us
    all_to_all x1, waiting for transfers between devices, exchange(): return lax.all_to_all(v, axes, split_axis=0, concat_axis=0, tiled=True)  15.4 us
    ppermute x3, starting transfers between devices, body(): lax.ppermute(v, 'x', [(i, i ^ d) for i in range(X)])  9.43 us
    all_to_all x1, starting transfers between devices, exchange(): return lax.all_to_all(v, axes, split_axis=0, concat_axis=0, tiled=True)  8.37 us
  transfers between devices with their start and end apart: 5, of which 2 were waited for; matrix products, arithmetic and copies ran while one was open for 0% of the time, Pallas kernels for 2%

profile of v9, /device:TPU:1, one launch (start us, length us, event | category | flops | bytes accessed | tf_op | source)
XLA Modules:
  0.0 176.7 jit_solution(17250138393850180102)
XLA Ops:
  0.6 1.2 pack.1
  1.8 0.0 copy-start
  1.8 0.0 copy-start.1
  1.8 46.1 %all_to_all.25.rows.goals = bf16[64,8,1152]{2,1,0:T(8,128)(2,1)S(1)} all-to-all(bf16[64,8,1152]{2,1,0:T(8,128)(2,1)S(1)} %pack.1), channel_id=1, replica_groups=mesh['x'=4,'z'=8,'core'=2,'tp'=8] {'x','z','core'}, dimensions={0} | all-to-all | bytes 2359296 | tf_op jit(solution)/shard_map/all_to_all | solution.py:259
  48.0 0.0 copy-done
  48.0 0.0 copy-done.1
  48.0 1.3 partial_values.1
  49.3 36.1 %all_to_all.26.got = bf16[8,528,128]{2,1,0:T(8,128)(2,1)S(1)} all-to-all(bf16[8,528,128]{2,1,0:T(8,128)(2,1)S(1)} %get-tuple-element.27), channel_id=1, replica_groups=mesh['x'=4,'z'=8,'core'=2,'tp'=8] {'tp'}, dimensions={0} | all-to-all | bytes 2162688 | tf_op jit(solution)/shard_map/all_to_all | solution.py:259
  85.4 0.3 loss.1
  85.7 30.5 %all_to_all.27.got = bf16[8,528,128]{2,1,0:T(8,128)(2,1)S(1)} all-to-all(bf16[8,528,128]{2,1,0:T(8,128)(2,1)S(1)} %get-tuple-element.28), channel_id=1, replica_groups=mesh['x'=4,'z'=8,'core'=2,'tp'=8] {'tp'}, dimensions={0} | all-to-all | bytes 2162688 | tf_op jit(solution)/shard_map/all_to_all | solution.py:259
  116.2 2.6 %grads.1 = (bf16[64,8,1152]{2,1,0:T(8,128)(2,1)}, bf16[512,1024]{1,0:T(8,128)(2,1)S(1)}, f32[8,1024]{1,0:T(8,128)S(1)}) custom-call(bf16[8,528,128]{2,1,0:T(8,128)(2,1)S(1)} %all_to_all.27.got, bf16[64,8,1152]{2,1,0:T(8,128)(2,1)S(1)} %all_to_all.25.rows.goals, f32[1,1024]{1,0:T(1,128)S(1)} %copy-done.1, bf16[1024,1024]{1,0:T(8,128)(2,1)S(1)} %bitcast.8, ...), custom_call_target="tpu_custom_call" | custom-call | flops 1073741824 | bytes 8388608 | tf_op jit(solution)/shard_map/grads/pallas_call | solution.py:295
  118.7 8.4 %all-to-all-start.3 = ((bf16[64,8,1152]{2,1,0:T(8,128)(2,1)}), bf16[64,8,1152]{2,1,0:T(8,128)(2,1)S(1)}, u32[]{:S(2)}, u32[]{:S(2)}) async-start(bf16[64,8,1152]{2,1,0:T(8,128)(2,1)} %get-tuple-element.39), calls=%async_computation.3 | async-start | bytes 2359296 | tf_op jit(solution)/shard_map/all_to_all | solution.py:259
  127.1 1.5 share.1
  128.7 2.4 %collective-permute-start = (bf16[528,1024]{1,0:T(8,128)(2,1)S(1)}, bf16[528,1024]{1,0:T(8,128)(2,1)S(1)}, u32[]{:S(2)}, u32[]{:S(2)}) collective-permute-start(bf16[528,1024]{1,0:T(8,128)(2,1)S(1)} %get-tuple-element.35), channel_id=1, source_target_pairs={{0,8},{8,0},{1,9},{9,1},{2,10},{10,2},{3,11},{11,3},{4,12},{12,4},... | collective-permute-start | bytes 3244040 | tf_op jit(solution)/shard_map/ppermute | solution.py:315
  131.0 2.3 %collective-permute-done.got = bf16[528,1024]{1,0:T(8,128)(2,1)S(1)} collective-permute-done((bf16[528,1024]{1,0:T(8,128)(2,1)S(1)}, bf16[528,1024]{1,0:T(8,128)(2,1)S(1)}, u32[]{:S(2)}, u32[]{:S(2)}) %collective-permute-start) | collective-permute-done | bytes 1081376 | tf_op jit(solution)/shard_map/ppermute | solution.py:315
  133.3 0.0 copy-start.2
  133.3 0.3 sum_core.1
  133.6 4.8 %collective-permute-start.1 = (bf16[1040,128]{1,0:T(8,128)(2,1)S(1)}, bf16[1040,128]{1,0:T(8,128)(2,1)S(1)}, u32[]{:S(2)}, u32[]{:S(2)}) collective-permute-start(bf16[1040,128]{1,0:T(8,128)(2,1)S(1)} %get-tuple-element.36), channel_id=1, source_target_pairs={{0,256},{128,384},{256,0},{384,128},{1,257},{129,385},{257,1},{385... | collective-permute-start | bytes 798728 | tf_op jit(solution)/shard_map/ppermute | solution.py:320
  138.4 2.3 %collective-permute-start.2 = (bf16[1040,128]{1,0:T(8,128)(2,1)S(1)}, bf16[1040,128]{1,0:T(8,128)(2,1)S(1)}, u32[]{:S(2)}, u32[]{:S(2)}) collective-permute-start(bf16[1040,128]{1,0:T(8,128)(2,1)S(1)} %get-tuple-element.37), channel_id=1, source_target_pairs={{0,128},{128,0},{256,384},{384,256},{1,129},{129,1},{257,385},{385... | collective-permute-start | bytes 798728 | tf_op jit(solution)/shard_map/ppermute | solution.py:320
  140.7 2.3 %collective-permute-start.3 = (bf16[1040,128]{1,0:T(8,128)(2,1)S(1)}, bf16[1040,128]{1,0:T(8,128)(2,1)S(1)}, u32[]{:S(2)}, u32[]{:S(2)}) collective-permute-start(bf16[1040,128]{1,0:T(8,128)(2,1)S(1)} %get-tuple-element.38), channel_id=1, source_target_pairs={{0,384},{128,256},{256,128},{384,0},{1,385},{129,257},{257,129},{3... | collective-permute-start | bytes 798728 | tf_op jit(solution)/shard_map/ppermute | solution.py:320
  143.1 15.4 %all-to-all-done.3.got = bf16[64,8,1152]{2,1,0:T(8,128)(2,1)S(1)} async-done(((bf16[64,8,1152]{2,1,0:T(8,128)(2,1)}), bf16[64,8,1152]{2,1,0:T(8,128)(2,1)S(1)}, u32[]{:S(2)}, u32[]{:S(2)}) %all-to-all-start.3) | async-done | bytes 1179680 | tf_op jit(solution)/shard_map/all_to_all | solution.py:259
  158.5 0.0 copy-done.2
  158.5 1.6 unpack.1
  160.1 0.0 collective-permute-done.1.refs_0_
  160.1 0.0 collective-permute-done.2.refs_1_
  160.1 0.0 collective-permute-done.3.refs_2_
  160.1 0.1 sum_x.1
  160.2 15.8 %all_to_all.28.got = bf16[8,144,128]{2,1,0:T(8,128)(2,1)S(1)} all-to-all(bf16[8,144,128]{2,1,0:T(8,128)(2,1)S(1)} %sum_x.1), channel_id=1, replica_groups=mesh['x'=4,'z'=8,'core'=2,'tp'=8] {'z'}, dimensions={0} | all-to-all | bytes 589824 | tf_op jit(solution)/shard_map/all_to_all | solution.py:259
  176.0 0.7 sum_z.1
Async XLA Ops:
  1.8 46.2 %copy-start = (bf16[1,1024,1024]{2,1,0:T(8,128)(2,1)S(1)}, bf16[1,1024,1024]{2,1,0:T(8,128)(2,1)}, u32[]{:S(2)}) copy-start(bf16[1,1024,1024]{2,1,0:T(8,128)(2,1)} %param.8) | copy-start | bytes 6291460
  1.8 46.1 %copy-start.1 = (f32[1,1024]{1,0:T(1,128)S(1)}, f32[1,1024]{1,0:T(1,128)}, u32[]{:S(2)}) copy-start(f32[1,1024]{1,0:T(1,128)} %gain.3) | copy-start | bytes 12292
  118.7 39.7 %all-to-all-start.3 = ((bf16[64,8,1152]{2,1,0:T(8,128)(2,1)}), bf16[64,8,1152]{2,1,0:T(8,128)(2,1)S(1)}, u32[]{:S(2)}, u32[]{:S(2)}) async-start(bf16[64,8,1152]{2,1,0:T(8,128)(2,1)} %get-tuple-element.39), calls=%async_computation.3 | async-start | bytes 2359296 | tf_op jit(solution)/shard_map/all_to_all | solution.py:259
  128.7 4.7 %collective-permute-start = (bf16[528,1024]{1,0:T(8,128)(2,1)S(1)}, bf16[528,1024]{1,0:T(8,128)(2,1)S(1)}, u32[]{:S(2)}, u32[]{:S(2)}) collective-permute-start(bf16[528,1024]{1,0:T(8,128)(2,1)S(1)} %get-tuple-element.35), channel_id=1, source_target_pairs={{0,8},{8,0},{1,9},{9,1},{2,10},{10,2},{3,11},{11,3},{4,12},{12,4},... | collective-permute-start | bytes 3244040 | tf_op jit(solution)/shard_map/ppermute | solution.py:315
  133.3 25.1 %copy-start.2 = (s32[32,1]{0,1:T(1,128)S(1)}, s32[32,1]{0,1:T(1,128)}, u32[]{:S(2)}) copy-start(s32[32,1]{0,1:T(1,128)} %param.7) | copy-start | bytes 388
  133.6 26.5 %collective-permute-start.1 = (bf16[1040,128]{1,0:T(8,128)(2,1)S(1)}, bf16[1040,128]{1,0:T(8,128)(2,1)S(1)}, u32[]{:S(2)}, u32[]{:S(2)}) collective-permute-start(bf16[1040,128]{1,0:T(8,128)(2,1)S(1)} %get-tuple-element.36), channel_id=1, source_target_pairs={{0,256},{128,384},{256,0},{384,128},{1,257},{129,385},{257,1},{385... | collective-permute-start | bytes 798728 | tf_op jit(solution)/shard_map/ppermute | solution.py:320
  138.4 21.7 %collective-permute-start.2 = (bf16[1040,128]{1,0:T(8,128)(2,1)S(1)}, bf16[1040,128]{1,0:T(8,128)(2,1)S(1)}, u32[]{:S(2)}, u32[]{:S(2)}) collective-permute-start(bf16[1040,128]{1,0:T(8,128)(2,1)S(1)} %get-tuple-element.37), channel_id=1, source_target_pairs={{0,128},{128,0},{256,384},{384,256},{1,129},{129,1},{257,385},{385... | collective-permute-start | bytes 798728 | tf_op jit(solution)/shard_map/ppermute | solution.py:320
  140.7 19.4 %collective-permute-start.3 = (bf16[1040,128]{1,0:T(8,128)(2,1)S(1)}, bf16[1040,128]{1,0:T(8,128)(2,1)S(1)}, u32[]{:S(2)}, u32[]{:S(2)}) collective-permute-start(bf16[1040,128]{1,0:T(8,128)(2,1)S(1)} %get-tuple-element.38), channel_id=1, source_target_pairs={{0,384},{128,256},{256,128},{384,0},{1,385},{129,257},{257,129},{3... | collective-permute-start | bytes 798728 | tf_op jit(solution)/shard_map/ppermute | solution.py:320

commit v10 on v8

--- a/solution.py
+++ b/solution.py
@@ -318,18 +318,18 @@
         core_kernel, (shape(*block, dtype=f32),) + (shape(*block),) * (X - 1), [VMEM] * 2, name="sum_core"
     )(keep, got)
     got = [lax.ppermute(v, "x", [(i, (i + d) % X) for i in range(X)]) for d, v in zip(X_STEPS, sends)]
+    by_x = call(x_kernel, shape(Z, 128 + EXTRA, 128), [VMEM] * X, name="sum_x")(own, *got)
+    by_x, rows_back = lax.optimization_barrier((by_x, rows_back))
+    by_z = exchange(by_x, "z")
+    weight_grad, gain_grad = call(
+        last_kernel, (shape(16, F, dtype=f32), shape(1, F, dtype=f32)), [VMEM], name="sum_z"
+    )(by_z)
     grad_rows, values = call(
         unpack_kernel,
         (shape(PIECES, MB, F), shape(PIECES, MB, C)),
         [SMEM, VMEM],
         name="unpack",
     )(order, rows_back)
-    got, grad_rows, values = lax.optimization_barrier((got, grad_rows, values))
-    by_x = call(x_kernel, shape(Z, 128 + EXTRA, 128), [VMEM] * X, name="sum_x")(own, *got)
-    by_z = exchange(by_x, "z")
-    weight_grad, gain_grad = call(
-        last_kernel, (shape(16, F, dtype=f32), shape(1, F, dtype=f32)), [VMEM], name="sum_z"
-    )(by_z)
     return (
         grad_rows.reshape(PIECES * MB, F),
         values.reshape(PIECES * MB, C),

time: 179 us -> 180 us (level)
  blocking collectives: 129 us -> 113 us
  waiting for transfers between devices: 15.9 us -> 26.4 us
  starting transfers between devices: 22 us -> 27.7 us
    all_to_all x4 -> x3, blocking collectives: 129 us -> 113 us  [exchange(): return lax.all_to_all(v, axes, split_axis=0, concat_axis=0, tiled=True)]
    ppermute x3, waiting for transfers between devices: 0.01 us -> 14.8 us  [body(): lax.ppermute(v, 'x', [(i, (i + d) % X) for i in range(X)])]
    all_to_all x1 -> x2, starting transfers between devices: 8.37 us -> 14 us  [exchange(): return lax.all_to_all(v, axes, split_axis=0, concat_axis=0, tiled=True)]
    all_to_all x1 -> x2, waiting for transfers between devices: 13.6 us -> 9.35 us  [exchange(): return lax.all_to_all(v, axes, split_axis=0, concat_axis=0, tiled=True)]
  transfers between devices with their start and end apart: 5 -> 6, of which waited for: 2 -> 4; matrix products, arithmetic and copies ran while one was open for 0% -> 0% of each run, Pallas kernels for 2% -> 2%
where the time goes in v10:
time: 180 us; the launch traced here: 178 us
  blocking collectives  113 us (63%)
  starting transfers between devices  27.7 us (15%)
  waiting for transfers between devices  26.4 us (15%)
  Pallas kernels  10.2 us (6%)
    all_to_all x3, blocking collectives, exchange(): return lax.all_to_all(v, axes, split_axis=0, concat_axis=0, tiled=True)  113 us
    ppermute x3, waiting for transfers between devices, body(): lax.ppermute(v, 'x', [(i, (i + d) % X) for i in range(X)])  14.8 us
    all_to_all x2, starting transfers between devices, exchange(): return lax.all_to_all(v, axes, split_axis=0, concat_axis=0, tiled=True)  14 us
    ppermute x3, starting transfers between devices, body(): lax.ppermute(v, 'x', [(i, (i + d) % X) for i in range(X)])  11.3 us
    all_to_all x2, waiting for transfers between devices, exchange(): return lax.all_to_all(v, axes, split_axis=0, concat_axis=0, tiled=True)  9.35 us
  transfers between devices with their start and end apart: 6, of which 4 were waited for; matrix products, arithmetic and copies ran while one was open for 0% of the time, Pallas kernels for 2%

profile of v10, /device:TPU:1, one launch (start us, length us, event | category | flops | bytes accessed | tf_op | source)
XLA Modules:
  0.0 177.9 jit_solution(8417419373681089706)
XLA Ops:
  0.6 1.2 pack.1
  1.8 0.0 copy-start
  1.8 0.0 copy-start.1
  1.8 46.1 %all_to_all.25.rows.goals = bf16[64,8,1152]{2,1,0:T(8,128)(2,1)S(1)} all-to-all(bf16[64,8,1152]{2,1,0:T(8,128)(2,1)S(1)} %pack.1), channel_id=1, replica_groups=mesh['x'=4,'z'=8,'core'=2,'tp'=8] {'x','z','core'}, dimensions={0} | all-to-all | bytes 2359296 | tf_op jit(solution)/shard_map/all_to_all | solution.py:259
  48.0 0.0 copy-done
  48.0 0.0 copy-done.1
  48.0 1.3 partial_values.1
  49.3 36.1 %all_to_all.26.got = bf16[8,528,128]{2,1,0:T(8,128)(2,1)S(1)} all-to-all(bf16[8,528,128]{2,1,0:T(8,128)(2,1)S(1)} %get-tuple-element.24), channel_id=1, replica_groups=mesh['x'=4,'z'=8,'core'=2,'tp'=8] {'tp'}, dimensions={0} | all-to-all | bytes 2162688 | tf_op jit(solution)/shard_map/all_to_all | solution.py:259
  85.4 0.3 loss.1
  85.7 30.5 %all_to_all.27.got = bf16[8,528,128]{2,1,0:T(8,128)(2,1)S(1)} all-to-all(bf16[8,528,128]{2,1,0:T(8,128)(2,1)S(1)} %get-tuple-element.25), channel_id=1, replica_groups=mesh['x'=4,'z'=8,'core'=2,'tp'=8] {'tp'}, dimensions={0} | all-to-all | bytes 2162688 | tf_op jit(solution)/shard_map/all_to_all | solution.py:259
  116.2 2.6 %grads.1 = (bf16[64,8,1152]{2,1,0:T(8,128)(2,1)}, bf16[512,1024]{1,0:T(8,128)(2,1)S(1)}, f32[8,1024]{1,0:T(8,128)S(1)}) custom-call(bf16[8,528,128]{2,1,0:T(8,128)(2,1)S(1)} %all_to_all.27.got, bf16[64,8,1152]{2,1,0:T(8,128)(2,1)S(1)} %all_to_all.25.rows.goals, f32[1,1024]{1,0:T(1,128)S(1)} %copy-done.1, bf16[1024,1024]{1,0:T(8,128)(2,1)S(1)} %bitcast.8, ...), custom_call_target="tpu_custom_call" | custom-call | flops 1073741824 | bytes 8388608 | tf_op jit(solution)/shard_map/grads/pallas_call | solution.py:295
  118.7 8.4 %all-to-all-start.3 = ((bf16[64,8,1152]{2,1,0:T(8,128)(2,1)}), bf16[64,8,1152]{2,1,0:T(8,128)(2,1)S(1)}, u32[]{:S(2)}, u32[]{:S(2)}) async-start(bf16[64,8,1152]{2,1,0:T(8,128)(2,1)} %get-tuple-element.37), calls=%async_computation.3 | async-start | bytes 2359296 | tf_op jit(solution)/shard_map/all_to_all | solution.py:259
  127.1 1.5 share.1
  128.7 2.4 %collective-permute-start = (bf16[528,1024]{1,0:T(8,128)(2,1)S(1)}, bf16[528,1024]{1,0:T(8,128)(2,1)S(1)}, u32[]{:S(2)}, u32[]{:S(2)}) collective-permute-start(bf16[528,1024]{1,0:T(8,128)(2,1)S(1)} %get-tuple-element.32), channel_id=1, source_target_pairs={{0,8},{8,0},{1,9},{9,1},{2,10},{10,2},{3,11},{11,3},{4,12},{12,4},... | collective-permute-start | bytes 3244040 | tf_op jit(solution)/shard_map/ppermute | solution.py:315
  131.0 2.3 %collective-permute-done.got = bf16[528,1024]{1,0:T(8,128)(2,1)S(1)} collective-permute-done((bf16[528,1024]{1,0:T(8,128)(2,1)S(1)}, bf16[528,1024]{1,0:T(8,128)(2,1)S(1)}, u32[]{:S(2)}, u32[]{:S(2)}) %collective-permute-start) | collective-permute-done | bytes 1081376 | tf_op jit(solution)/shard_map/ppermute | solution.py:315
  133.3 0.3 sum_core.1
  133.6 0.0 copy-start.2
  133.6 4.8 %collective-permute-start.1 = (bf16[1040,128]{1,0:T(8,128)(2,1)S(1)}, bf16[1040,128]{1,0:T(8,128)(2,1)S(1)}, u32[]{:S(2)}, u32[]{:S(2)}) collective-permute-start(bf16[1040,128]{1,0:T(8,128)(2,1)S(1)} %get-tuple-element.34), channel_id=1, source_target_pairs={{0,256},{128,384},{256,0},{384,128},{1,257},{129,385},{257,1},{385... | collective-permute-start | bytes 798728 | tf_op jit(solution)/shard_map/ppermute | solution.py:320
  138.4 2.3 %collective-permute-start.2 = (bf16[1040,128]{1,0:T(8,128)(2,1)S(1)}, bf16[1040,128]{1,0:T(8,128)(2,1)S(1)}, u32[]{:S(2)}, u32[]{:S(2)}) collective-permute-start(bf16[1040,128]{1,0:T(8,128)(2,1)S(1)} %get-tuple-element.35), channel_id=1, source_target_pairs={{0,128},{128,256},{256,384},{384,0},{1,129},{129,257},{257,385},{3... | collective-permute-start | bytes 798728 | tf_op jit(solution)/shard_map/ppermute | solution.py:320
  140.8 4.2 %collective-permute-start.3 = (bf16[1040,128]{1,0:T(8,128)(2,1)S(1)}, bf16[1040,128]{1,0:T(8,128)(2,1)S(1)}, u32[]{:S(2)}, u32[]{:S(2)}) collective-permute-start(bf16[1040,128]{1,0:T(8,128)(2,1)S(1)} %get-tuple-element.36), channel_id=1, source_target_pairs={{0,384},{128,0},{256,128},{384,256},{1,385},{129,1},{257,129},{385... | collective-permute-start | bytes 798728 | tf_op jit(solution)/shard_map/ppermute | solution.py:320
  144.9 4.9 %collective-permute-done.1.refs_0_ = bf16[1040,128]{1,0:T(8,128)(2,1)S(1)} collective-permute-done((bf16[1040,128]{1,0:T(8,128)(2,1)S(1)}, bf16[1040,128]{1,0:T(8,128)(2,1)S(1)}, u32[]{:S(2)}, u32[]{:S(2)}) %collective-permute-start.1) | collective-permute-done | bytes 266272 | tf_op jit(solution)/shard_map/ppermute | solution.py:320
  149.9 9.8 %collective-permute-done.2.refs_1_ = bf16[1040,128]{1,0:T(8,128)(2,1)S(1)} collective-permute-done((bf16[1040,128]{1,0:T(8,128)(2,1)S(1)}, bf16[1040,128]{1,0:T(8,128)(2,1)S(1)}, u32[]{:S(2)}, u32[]{:S(2)}) %collective-permute-start.2) | collective-permute-done | bytes 266272 | tf_op jit(solution)/shard_map/ppermute | solution.py:320
  159.7 0.0 collective-permute-done.3.refs_2_
  159.7 0.9 sum_x.1
  160.6 0.0 all-to-all-done.3.got
  160.6 5.6 %all-to-all-start.4 = ((bf16[8,144,128]{2,1,0:T(8,128)(2,1)}), bf16[8,144,128]{2,1,0:T(8,128)(2,1)S(1)}, u32[]{:S(2)}, u32[]{:S(2)}) async-start(bf16[8,144,128]{2,1,0:T(8,128)(2,1)} %sum_x.1), calls=%async_computation.4 | async-start | bytes 589824 | tf_op jit(solution)/shard_map/all_to_all | solution.py:259
  166.2 0.0 copy-done.2
  166.2 1.6 unpack.1
  167.8 9.3 %all-to-all-done.4.got = bf16[8,144,128]{2,1,0:T(8,128)(2,1)S(1)} async-done(((bf16[8,144,128]{2,1,0:T(8,128)(2,1)}), bf16[8,144,128]{2,1,0:T(8,128)(2,1)S(1)}, u32[]{:S(2)}, u32[]{:S(2)}) %all-to-all-start.4) | async-done | bytes 294944 | tf_op jit(solution)/shard_map/all_to_all | solution.py:259
  177.2 0.7 sum_z.1
Async XLA Ops:
  1.8 46.2 %copy-start = (bf16[1,1024,1024]{2,1,0:T(8,128)(2,1)S(1)}, bf16[1,1024,1024]{2,1,0:T(8,128)(2,1)}, u32[]{:S(2)}) copy-start(bf16[1,1024,1024]{2,1,0:T(8,128)(2,1)} %param.8) | copy-start | bytes 6291460
  1.8 46.1 %copy-start.1 = (f32[1,1024]{1,0:T(1,128)S(1)}, f32[1,1024]{1,0:T(1,128)}, u32[]{:S(2)}) copy-start(f32[1,1024]{1,0:T(1,128)} %gain.3) | copy-start | bytes 12292
  118.7 41.8 %all-to-all-start.3 = ((bf16[64,8,1152]{2,1,0:T(8,128)(2,1)}), bf16[64,8,1152]{2,1,0:T(8,128)(2,1)S(1)}, u32[]{:S(2)}, u32[]{:S(2)}) async-start(bf16[64,8,1152]{2,1,0:T(8,128)(2,1)} %get-tuple-element.37), calls=%async_computation.3 | async-start | bytes 2359296 | tf_op jit(solution)/shard_map/all_to_all | solution.py:259
  128.7 4.7 %collective-permute-start = (bf16[528,1024]{1,0:T(8,128)(2,1)S(1)}, bf16[528,1024]{1,0:T(8,128)(2,1)S(1)}, u32[]{:S(2)}, u32[]{:S(2)}) collective-permute-start(bf16[528,1024]{1,0:T(8,128)(2,1)S(1)} %get-tuple-element.32), channel_id=1, source_target_pairs={{0,8},{8,0},{1,9},{9,1},{2,10},{10,2},{3,11},{11,3},{4,12},{12,4},... | collective-permute-start | bytes 3244040 | tf_op jit(solution)/shard_map/ppermute | solution.py:315
  133.6 32.6 %copy-start.2 = (s32[32,1]{0,1:T(1,128)S(1)}, s32[32,1]{0,1:T(1,128)}, u32[]{:S(2)}) copy-start(s32[32,1]{0,1:T(1,128)} %param.7) | copy-start | bytes 388
  133.6 16.3 %collective-permute-start.1 = (bf16[1040,128]{1,0:T(8,128)(2,1)S(1)}, bf16[1040,128]{1,0:T(8,128)(2,1)S(1)}, u32[]{:S(2)}, u32[]{:S(2)}) collective-permute-start(bf16[1040,128]{1,0:T(8,128)(2,1)S(1)} %get-tuple-element.34), channel_id=1, source_target_pairs={{0,256},{128,384},{256,0},{384,128},{1,257},{129,385},{257,1},{385... | collective-permute-start | bytes 798728 | tf_op jit(solution)/shard_map/ppermute | solution.py:320
  138.4 21.3 %collective-permute-start.2 = (bf16[1040,128]{1,0:T(8,128)(2,1)S(1)}, bf16[1040,128]{1,0:T(8,128)(2,1)S(1)}, u32[]{:S(2)}, u32[]{:S(2)}) collective-permute-start(bf16[1040,128]{1,0:T(8,128)(2,1)S(1)} %get-tuple-element.35), channel_id=1, source_target_pairs={{0,128},{128,256},{256,384},{384,0},{1,129},{129,257},{257,385},{3... | collective-permute-start | bytes 798728 | tf_op jit(solution)/shard_map/ppermute | solution.py:320
  140.8 19.0 %collective-permute-start.3 = (bf16[1040,128]{1,0:T(8,128)(2,1)S(1)}, bf16[1040,128]{1,0:T(8,128)(2,1)S(1)}, u32[]{:S(2)}, u32[]{:S(2)}) collective-permute-start(bf16[1040,128]{1,0:T(8,128)(2,1)S(1)} %get-tuple-element.36), channel_id=1, source_target_pairs={{0,384},{128,0},{256,128},{384,256},{1,385},{129,1},{257,129},{385... | collective-permute-start | bytes 798728 | tf_op jit(solution)/shard_map/ppermute | solution.py:320
  160.6 16.6 %all-to-all-start.4 = ((bf16[8,144,128]{2,1,0:T(8,128)(2,1)}), bf16[8,144,128]{2,1,0:T(8,128)(2,1)S(1)}, u32[]{:S(2)}, u32[]{:S(2)}) async-start(bf16[8,144,128]{2,1,0:T(8,128)(2,1)} %sum_x.1), calls=%async_computation.4 | async-start | bytes 589824 | tf_op jit(solution)/shard_map/all_to_all | solution.py:259

commit v11 on v8

--- a/solution.py
+++ b/solution.py
@@ -19,6 +19,7 @@
 TILE = 128
 NTILES = ROWS // TILE
 EXTRA = 16
+SUMS = 8
 GRAD_SCALE = (ROWS // 2 * NP) ** (-0.5)
 
 epsilon = 1e-05
@@ -47,6 +48,11 @@
     rest = v - high
     mid = rest.astype(bf16).astype(f32)
     return high, mid, rest - mid
+
+
+def halves(v):
+    high = v.astype(bf16).astype(f32)
+    return high, v - high
 
 
 def to_lanes(square):
@@ -96,8 +102,8 @@
         partial = jnp.dot(gained[...], weights[:, i * 256 : (i + 1) * 256], preferred_element_type=f32).astype(bf16)
         out[2 * i, :ROWS, :] = partial[:, :C]
         out[2 * i + 1, :ROWS, :] = partial[:, C:]
-    high, mid, low = parts(squares[0:4, :])
-    tail = jnp.concatenate([high, mid, low, jnp.zeros_like(high)], axis=0).astype(bf16)
+    high, rest = halves(squares[0:4, :])
+    tail = jnp.concatenate([high, rest], axis=0).astype(bf16)
     for t in range(NT):
         out[t, ROWS:, :] = tail
 
@@ -106,7 +112,7 @@
     tail = got[0, ROWS:, :].astype(f32)
     for t in range(1, NT):
         tail = tail + got[t, ROWS:, :].astype(f32)
-    total = tail[0:4] + tail[4:8] + tail[8:12]
+    total = tail[0:4] + tail[4:8]
     scales[0:4, :] = lax.rsqrt(total / D + epsilon)
     scales[4:8, :] = jnp.zeros((4, 128), f32)
 
@@ -123,8 +129,8 @@
             send[t, here, :] = grad
         dots[i : i + 1, :] = to_lanes(grad.astype(f32) * value)
 
-    high, mid, low = parts(dots[0:4, :])
-    tail = jnp.concatenate([high, mid, low, jnp.zeros_like(high)], axis=0).astype(bf16)
+    high, rest = halves(dots[0:4, :])
+    tail = jnp.concatenate([high, rest], axis=0).astype(bf16)
     for t in range(NT):
         send[t, ROWS:, :] = tail
 
@@ -133,7 +139,7 @@
     tail = got[0, ROWS:, :].astype(f32)
     for t in range(1, NT):
         tail = tail + got[t, ROWS:, :].astype(f32)
-    dots = (tail[0:4] + tail[4:8] + tail[8:12]) / D
+    dots = (tail[0:4] + tail[4:8]) / D
     copies = []
     sums = [0.0] * (F // 256)
     for half in range(2):
@@ -279,7 +285,7 @@
     arrived = exchange(sends, peer)
     partials, gained = call(
         value_kernel,
-        (shape(NT, ROWS + EXTRA, C), shape(ROWS, F)),
+        (shape(NT, ROWS + SUMS, C), shape(ROWS, F)),
         [VMEM] * 3,
         [pltpu.VMEM((8, 128), f32)],
         flops=2 * ROWS * F * KV,
@@ -287,7 +293,7 @@
     )(arrived, norm_gains, weights)
     value, grad_part, scales = call(
         loss_kernel,
-        (shape(NP, MB, C), shape(NT, ROWS + EXTRA, C), shape(8, 128, dtype=f32)),
+        (shape(NP, MB, C), shape(NT, ROWS + SUMS, C), shape(8, 128, dtype=f32)),
         [VMEM] * 2,
         [pltpu.VMEM((8, 128), f32)],
         name="loss",

time: 179 us -> 178 us (level)
  no operation moved by 1% of the time
where the time goes in v11:
time: 178 us; the launch traced here: 176 us
  blocking collectives  129 us (72%)
  starting transfers between devices  20.3 us (11%)
  waiting for transfers between devices  15.9 us (9%)
  Pallas kernels  9.51 us (5%)
    all_to_all x4, blocking collectives, exchange(): return lax.all_to_all(v, axes, split_axis=0, concat_axis=0, tiled=True)  129 us
    all_to_all x1, waiting for transfers between devices, exchange(): return lax.all_to_all(v, axes, split_axis=0, concat_axis=0, tiled=True)  13.6 us
    ppermute x3, starting transfers between devices, body(): lax.ppermute(v, 'x', [(i, (i + d) % X) for i in range(X)])  11.3 us
    all_to_all x1, starting transfers between devices, exchange(): return lax.all_to_all(v, axes, split_axis=0, concat_axis=0, tiled=True)  6.65 us
  transfers between devices with their start and end apart: 5, of which 2 were waited for; matrix products, arithmetic and copies ran while one was open for 0% of the time, Pallas kernels for 2%

profile of v11, /device:TPU:1, one launch (start us, length us, event | category | flops | bytes accessed | tf_op | source)
XLA Modules:
  0.0 175.8 jit_solution(11496087331113486308)
XLA Ops:
  0.6 1.2 pack.1
  1.8 0.0 copy-start
  1.8 0.0 copy-start.1
  1.8 46.1 %all_to_all.25.rows.goals = bf16[64,8,1152]{2,1,0:T(8,128)(2,1)S(1)} all-to-all(bf16[64,8,1152]{2,1,0:T(8,128)(2,1)S(1)} %pack.1), channel_id=1, replica_groups=mesh['x'=4,'z'=8,'core'=2,'tp'=8] {'x','z','core'}, dimensions={0} | all-to-all | bytes 2359296 | tf_op jit(solution)/shard_map/all_to_all | solution.py:265
  48.0 0.0 copy-done
  48.0 0.0 copy-done.1
  48.0 1.3 partial_values.1
  49.3 36.1 %all_to_all.26.got = bf16[8,520,128]{2,1,0:T(8,128)(2,1)S(1)} all-to-all(bf16[8,520,128]{2,1,0:T(8,128)(2,1)S(1)} %get-tuple-element.27), channel_id=1, replica_groups=mesh['x'=4,'z'=8,'core'=2,'tp'=8] {'tp'}, dimensions={0} | all-to-all | bytes 2129920 | tf_op jit(solution)/shard_map/all_to_all | solution.py:265
  85.4 0.3 loss.1
  85.7 31.4 %all_to_all.27.got = bf16[8,520,128]{2,1,0:T(8,128)(2,1)S(1)} all-to-all(bf16[8,520,128]{2,1,0:T(8,128)(2,1)S(1)} %get-tuple-element.28), channel_id=1, replica_groups=mesh['x'=4,'z'=8,'core'=2,'tp'=8] {'tp'}, dimensions={0} | all-to-all | bytes 2129920 | tf_op jit(solution)/shard_map/all_to_all | solution.py:265
  117.0 2.6 %grads.1 = (bf16[64,8,1152]{2,1,0:T(8,128)(2,1)}, bf16[512,1024]{1,0:T(8,128)(2,1)S(1)}, f32[8,1024]{1,0:T(8,128)S(1)}) custom-call(bf16[8,520,128]{2,1,0:T(8,128)(2,1)S(1)} %all_to_all.27.got, bf16[64,8,1152]{2,1,0:T(8,128)(2,1)S(1)} %all_to_all.25.rows.goals, f32[1,1024]{1,0:T(1,128)S(1)} %copy-done.1, bf16[1024,1024]{1,0:T(8,128)(2,1)S(1)} %bitcast.8, ...), custom_call_target="tpu_custom_call" | custom-call | flops 1073741824 | bytes 8388608 | tf_op jit(solution)/shard_map/grads/pallas_call | solution.py:301
  119.6 6.6 %all-to-all-start.3 = ((bf16[64,8,1152]{2,1,0:T(8,128)(2,1)}), bf16[64,8,1152]{2,1,0:T(8,128)(2,1)S(1)}, u32[]{:S(2)}, u32[]{:S(2)}) async-start(bf16[64,8,1152]{2,1,0:T(8,128)(2,1)} %get-tuple-element.39), calls=%async_computation.3 | async-start | bytes 2359296 | tf_op jit(solution)/shard_map/all_to_all | solution.py:265
  126.2 1.5 share.1
  127.8 2.4 %collective-permute-start = (bf16[528,1024]{1,0:T(8,128)(2,1)S(1)}, bf16[528,1024]{1,0:T(8,128)(2,1)S(1)}, u32[]{:S(2)}, u32[]{:S(2)}) collective-permute-start(bf16[528,1024]{1,0:T(8,128)(2,1)S(1)} %get-tuple-element.35), channel_id=1, source_target_pairs={{0,8},{8,0},{1,9},{9,1},{2,10},{10,2},{3,11},{11,3},{4,12},{12,4},... | collective-permute-start | bytes 3244040 | tf_op jit(solution)/shard_map/ppermute | solution.py:321
  130.1 2.3 %collective-permute-done.got = bf16[528,1024]{1,0:T(8,128)(2,1)S(1)} collective-permute-done((bf16[528,1024]{1,0:T(8,128)(2,1)S(1)}, bf16[528,1024]{1,0:T(8,128)(2,1)S(1)}, u32[]{:S(2)}, u32[]{:S(2)}) %collective-permute-start) | collective-permute-done | bytes 1081376 | tf_op jit(solution)/shard_map/ppermute | solution.py:321
  132.5 0.0 copy-start.2
  132.5 0.3 sum_core.1
  132.7 4.8 %collective-permute-start.1 = (bf16[1040,128]{1,0:T(8,128)(2,1)S(1)}, bf16[1040,128]{1,0:T(8,128)(2,1)S(1)}, u32[]{:S(2)}, u32[]{:S(2)}) collective-permute-start(bf16[1040,128]{1,0:T(8,128)(2,1)S(1)} %get-tuple-element.36), channel_id=1, source_target_pairs={{0,256},{128,384},{256,0},{384,128},{1,257},{129,385},{257,1},{385... | collective-permute-start | bytes 798728 | tf_op jit(solution)/shard_map/ppermute | solution.py:326
  137.5 2.3 %collective-permute-start.2 = (bf16[1040,128]{1,0:T(8,128)(2,1)S(1)}, bf16[1040,128]{1,0:T(8,128)(2,1)S(1)}, u32[]{:S(2)}, u32[]{:S(2)}) collective-permute-start(bf16[1040,128]{1,0:T(8,128)(2,1)S(1)} %get-tuple-element.37), channel_id=1, source_target_pairs={{0,128},{128,256},{256,384},{384,0},{1,129},{129,257},{257,385},{3... | collective-permute-start | bytes 798728 | tf_op jit(solution)/shard_map/ppermute | solution.py:326
  139.8 4.2 %collective-permute-start.3 = (bf16[1040,128]{1,0:T(8,128)(2,1)S(1)}, bf16[1040,128]{1,0:T(8,128)(2,1)S(1)}, u32[]{:S(2)}, u32[]{:S(2)}) collective-permute-start(bf16[1040,128]{1,0:T(8,128)(2,1)S(1)} %get-tuple-element.38), channel_id=1, source_target_pairs={{0,384},{128,0},{256,128},{384,256},{1,385},{129,1},{257,129},{385... | collective-permute-start | bytes 798728 | tf_op jit(solution)/shard_map/ppermute | solution.py:326
  144.0 13.6 %all-to-all-done.3.got = bf16[64,8,1152]{2,1,0:T(8,128)(2,1)S(1)} async-done(((bf16[64,8,1152]{2,1,0:T(8,128)(2,1)}), bf16[64,8,1152]{2,1,0:T(8,128)(2,1)S(1)}, u32[]{:S(2)}, u32[]{:S(2)}) %all-to-all-start.3) | async-done | bytes 1179680 | tf_op jit(solution)/shard_map/all_to_all | solution.py:265
  157.6 0.0 copy-done.2
  157.6 1.6 unpack.1
  159.2 0.0 collective-permute-done.1.refs_0_
  159.2 0.0 collective-permute-done.2.refs_1_
  159.2 0.0 collective-permute-done.3.refs_2_
  159.2 0.1 sum_x.1
  159.4 15.8 %all_to_all.28.got = bf16[8,144,128]{2,1,0:T(8,128)(2,1)S(1)} all-to-all(bf16[8,144,128]{2,1,0:T(8,128)(2,1)S(1)} %sum_x.1), channel_id=1, replica_groups=mesh['x'=4,'z'=8,'core'=2,'tp'=8] {'z'}, dimensions={0} | all-to-all | bytes 589824 | tf_op jit(solution)/shard_map/all_to_all | solution.py:265
  175.2 0.7 sum_z.1
Async XLA Ops:
  1.8 46.2 %copy-start = (bf16[1,1024,1024]{2,1,0:T(8,128)(2,1)S(1)}, bf16[1,1024,1024]{2,1,0:T(8,128)(2,1)}, u32[]{:S(2)}) copy-start(bf16[1,1024,1024]{2,1,0:T(8,128)(2,1)} %param.8) | copy-start | bytes 6291460
  1.8 46.1 %copy-start.1 = (f32[1,1024]{1,0:T(1,128)S(1)}, f32[1,1024]{1,0:T(1,128)}, u32[]{:S(2)}) copy-start(f32[1,1024]{1,0:T(1,128)} %gain.3) | copy-start | bytes 12292
  119.6 38.0 %all-to-all-start.3 = ((bf16[64,8,1152]{2,1,0:T(8,128)(2,1)}), bf16[64,8,1152]{2,1,0:T(8,128)(2,1)S(1)}, u32[]{:S(2)}, u32[]{:S(2)}) async-start(bf16[64,8,1152]{2,1,0:T(8,128)(2,1)} %get-tuple-element.39), calls=%async_computation.3 | async-start | bytes 2359296 | tf_op jit(solution)/shard_map/all_to_all | solution.py:265
  127.8 4.7 %collective-permute-start = (bf16[528,1024]{1,0:T(8,128)(2,1)S(1)}, bf16[528,1024]{1,0:T(8,128)(2,1)S(1)}, u32[]{:S(2)}, u32[]{:S(2)}) collective-permute-start(bf16[528,1024]{1,0:T(8,128)(2,1)S(1)} %get-tuple-element.35), channel_id=1, source_target_pairs={{0,8},{8,0},{1,9},{9,1},{2,10},{10,2},{3,11},{11,3},{4,12},{12,4},... | collective-permute-start | bytes 3244040 | tf_op jit(solution)/shard_map/ppermute | solution.py:321
  132.5 25.1 %copy-start.2 = (s32[32,1]{0,1:T(1,128)S(1)}, s32[32,1]{0,1:T(1,128)}, u32[]{:S(2)}) copy-start(s32[32,1]{0,1:T(1,128)} %param.7) | copy-start | bytes 388
  132.7 26.5 %collective-permute-start.1 = (bf16[1040,128]{1,0:T(8,128)(2,1)S(1)}, bf16[1040,128]{1,0:T(8,128)(2,1)S(1)}, u32[]{:S(2)}, u32[]{:S(2)}) collective-permute-start(bf16[1040,128]{1,0:T(8,128)(2,1)S(1)} %get-tuple-element.36), channel_id=1, source_target_pairs={{0,256},{128,384},{256,0},{384,128},{1,257},{129,385},{257,1},{385... | collective-permute-start | bytes 798728 | tf_op jit(solution)/shard_map/ppermute | solution.py:326
  137.5 21.7 %collective-permute-start.2 = (bf16[1040,128]{1,0:T(8,128)(2,1)S(1)}, bf16[1040,128]{1,0:T(8,128)(2,1)S(1)}, u32[]{:S(2)}, u32[]{:S(2)}) collective-permute-start(bf16[1040,128]{1,0:T(8,128)(2,1)S(1)} %get-tuple-element.37), channel_id=1, source_target_pairs={{0,128},{128,256},{256,384},{384,0},{1,129},{129,257},{257,385},{3... | collective-permute-start | bytes 798728 | tf_op jit(solution)/shard_map/ppermute | solution.py:326
  139.8 19.4 %collective-permute-start.3 = (bf16[1040,128]{1,0:T(8,128)(2,1)S(1)}, bf16[1040,128]{1,0:T(8,128)(2,1)S(1)}, u32[]{:S(2)}, u32[]{:S(2)}) collective-permute-start(bf16[1040,128]{1,0:T(8,128)(2,1)S(1)} %get-tuple-element.38), channel_id=1, source_target_pairs={{0,384},{128,0},{256,128},{384,256},{1,385},{129,1},{257,129},{385... | collective-permute-start | bytes 798728 | tf_op jit(solution)/shard_map/ppermute | solution.py:326

commit v12 on v11

--- a/solution.py
+++ b/solution.py
@@ -230,7 +230,7 @@
     tail = own[F:, :]
     for g in got:
         tail = tail + g[F:, :].astype(f32)
-    tail = gain_tail(tail[:8] + tail[8:])
+    tail = (tail[:8] + tail[8:]).astype(bf16)
     for z in range(Z):
         out[z, 128:, :] = tail
 
@@ -240,7 +240,7 @@
     for z in range(1, Z):
         total = total + got[z].astype(f32)
     total = total * GRAD_SCALE
-    tail = total[128:136] + total[136:]
+    tail = total[128:]
     for j in range(F // 128):
         at = slice(j * 128, (j + 1) * 128)
         weight_out[:, at] = total[j * 16 : (j + 1) * 16]
@@ -331,7 +331,7 @@
         name="unpack",
     )(order, rows_back)
     got, grad_rows, values = lax.optimization_barrier((got, grad_rows, values))
-    by_x = call(x_kernel, shape(Z, 128 + EXTRA, 128), [VMEM] * X, name="sum_x")(own, *got)
+    by_x = call(x_kernel, shape(Z, 128 + 8, 128), [VMEM] * X, name="sum_x")(own, *got)
     by_z = exchange(by_x, "z")
     weight_grad, gain_grad = call(
         last_kernel, (shape(16, F, dtype=f32), shape(1, F, dtype=f32)), [VMEM], name="sum_z"

time: 178 us -> 178 us (level)
  no operation moved by 1% of the time
where the time goes in v12:
time: 178 us; the launch traced here: 176 us
  blocking collectives  129 us (72%)
  starting transfers between devices  20.3 us (11%)
  waiting for transfers between devices  15.9 us (9%)
  Pallas kernels  9.51 us (5%)
    all_to_all x4, blocking collectives, exchange(): return lax.all_to_all(v, axes, split_axis=0, concat_axis=0, tiled=True)  129 us
    all_to_all x1, waiting for transfers between devices, exchange(): return lax.all_to_all(v, axes, split_axis=0, concat_axis=0, tiled=True)  13.6 us
    ppermute x3, starting transfers between devices, body(): lax.ppermute(v, 'x', [(i, (i + d) % X) for i in range(X)])  11.3 us
    all_to_all x1, starting transfers between devices, exchange(): return lax.all_to_all(v, axes, split_axis=0, concat_axis=0, tiled=True)  6.65 us
  transfers between devices with their start and end apart: 5, of which 2 were waited for; matrix products, arithmetic and copies ran while one was open for 0% of the time, Pallas kernels for 2%

profile of v12, /device:TPU:1, one launch (start us, length us, event | category | flops | bytes accessed | tf_op | source)
XLA Modules:
  0.0 175.6 jit_solution(4055154719083817211)
XLA Ops:
  0.6 1.2 pack.1
  1.8 0.0 copy-start
  1.8 0.0 copy-start.1
  1.8 46.1 %all_to_all.25.rows.goals = bf16[64,8,1152]{2,1,0:T(8,128)(2,1)S(1)} all-to-all(bf16[64,8,1152]{2,1,0:T(8,128)(2,1)S(1)} %pack.1), channel_id=1, replica_groups=mesh['x'=4,'z'=8,'core'=2,'tp'=8] {'x','z','core'}, dimensions={0} | all-to-all | bytes 2359296 | tf_op jit(solution)/shard_map/all_to_all | solution.py:265
  48.0 0.0 copy-done
  48.0 0.0 copy-done.1
  48.0 1.3 partial_values.1
  49.3 36.1 %all_to_all.26.got = bf16[8,520,128]{2,1,0:T(8,128)(2,1)S(1)} all-to-all(bf16[8,520,128]{2,1,0:T(8,128)(2,1)S(1)} %get-tuple-element.27), channel_id=1, replica_groups=mesh['x'=4,'z'=8,'core'=2,'tp'=8] {'tp'}, dimensions={0} | all-to-all | bytes 2129920 | tf_op jit(solution)/shard_map/all_to_all | solution.py:265
  85.4 0.3 loss.1
  85.7 31.4 %all_to_all.27.got = bf16[8,520,128]{2,1,0:T(8,128)(2,1)S(1)} all-to-all(bf16[8,520,128]{2,1,0:T(8,128)(2,1)S(1)} %get-tuple-element.28), channel_id=1, replica_groups=mesh['x'=4,'z'=8,'core'=2,'tp'=8] {'tp'}, dimensions={0} | all-to-all | bytes 2129920 | tf_op jit(solution)/shard_map/all_to_all | solution.py:265
  117.0 2.6 %grads.1 = (bf16[64,8,1152]{2,1,0:T(8,128)(2,1)}, bf16[512,1024]{1,0:T(8,128)(2,1)S(1)}, f32[8,1024]{1,0:T(8,128)S(1)}) custom-call(bf16[8,520,128]{2,1,0:T(8,128)(2,1)S(1)} %all_to_all.27.got, bf16[64,8,1152]{2,1,0:T(8,128)(2,1)S(1)} %all_to_all.25.rows.goals, f32[1,1024]{1,0:T(1,128)S(1)} %copy-done.1, bf16[1024,1024]{1,0:T(8,128)(2,1)S(1)} %bitcast.8, ...), custom_call_target="tpu_custom_call" | custom-call | flops 1073741824 | bytes 8388608 | tf_op jit(solution)/shard_map/grads/pallas_call | solution.py:301
  119.6 6.6 %all-to-all-start.3 = ((bf16[64,8,1152]{2,1,0:T(8,128)(2,1)}), bf16[64,8,1152]{2,1,0:T(8,128)(2,1)S(1)}, u32[]{:S(2)}, u32[]{:S(2)}) async-start(bf16[64,8,1152]{2,1,0:T(8,128)(2,1)} %get-tuple-element.39), calls=%async_computation.3 | async-start | bytes 2359296 | tf_op jit(solution)/shard_map/all_to_all | solution.py:265
  126.2 1.5 share.1
  127.8 2.4 %collective-permute-start = (bf16[528,1024]{1,0:T(8,128)(2,1)S(1)}, bf16[528,1024]{1,0:T(8,128)(2,1)S(1)}, u32[]{:S(2)}, u32[]{:S(2)}) collective-permute-start(bf16[528,1024]{1,0:T(8,128)(2,1)S(1)} %get-tuple-element.35), channel_id=1, source_target_pairs={{0,8},{8,0},{1,9},{9,1},{2,10},{10,2},{3,11},{11,3},{4,12},{12,4},... | collective-permute-start | bytes 3244040 | tf_op jit(solution)/shard_map/ppermute | solution.py:321
  130.1 2.3 %collective-permute-done.got = bf16[528,1024]{1,0:T(8,128)(2,1)S(1)} collective-permute-done((bf16[528,1024]{1,0:T(8,128)(2,1)S(1)}, bf16[528,1024]{1,0:T(8,128)(2,1)S(1)}, u32[]{:S(2)}, u32[]{:S(2)}) %collective-permute-start) | collective-permute-done | bytes 1081376 | tf_op jit(solution)/shard_map/ppermute | solution.py:321
  132.5 0.0 copy-start.2
  132.5 0.3 sum_core.1
  132.7 4.8 %collective-permute-start.1 = (bf16[1040,128]{1,0:T(8,128)(2,1)S(1)}, bf16[1040,128]{1,0:T(8,128)(2,1)S(1)}, u32[]{:S(2)}, u32[]{:S(2)}) collective-permute-start(bf16[1040,128]{1,0:T(8,128)(2,1)S(1)} %get-tuple-element.36), channel_id=1, source_target_pairs={{0,256},{128,384},{256,0},{384,128},{1,257},{129,385},{257,1},{385... | collective-permute-start | bytes 798728 | tf_op jit(solution)/shard_map/ppermute | solution.py:326
  137.5 2.3 %collective-permute-start.2 = (bf16[1040,128]{1,0:T(8,128)(2,1)S(1)}, bf16[1040,128]{1,0:T(8,128)(2,1)S(1)}, u32[]{:S(2)}, u32[]{:S(2)}) collective-permute-start(bf16[1040,128]{1,0:T(8,128)(2,1)S(1)} %get-tuple-element.37), channel_id=1, source_target_pairs={{0,128},{128,256},{256,384},{384,0},{1,129},{129,257},{257,385},{3... | collective-permute-start | bytes 798728 | tf_op jit(solution)/shard_map/ppermute | solution.py:326
  139.8 4.2 %collective-permute-start.3 = (bf16[1040,128]{1,0:T(8,128)(2,1)S(1)}, bf16[1040,128]{1,0:T(8,128)(2,1)S(1)}, u32[]{:S(2)}, u32[]{:S(2)}) collective-permute-start(bf16[1040,128]{1,0:T(8,128)(2,1)S(1)} %get-tuple-element.38), channel_id=1, source_target_pairs={{0,384},{128,0},{256,128},{384,256},{1,385},{129,1},{257,129},{385... | collective-permute-start | bytes 798728 | tf_op jit(solution)/shard_map/ppermute | solution.py:326
  144.0 13.6 %all-to-all-done.3.got = bf16[64,8,1152]{2,1,0:T(8,128)(2,1)S(1)} async-done(((bf16[64,8,1152]{2,1,0:T(8,128)(2,1)}), bf16[64,8,1152]{2,1,0:T(8,128)(2,1)S(1)}, u32[]{:S(2)}, u32[]{:S(2)}) %all-to-all-start.3) | async-done | bytes 1179680 | tf_op jit(solution)/shard_map/all_to_all | solution.py:265
  157.6 0.0 copy-done.2
  157.6 1.6 unpack.1
  159.2 0.0 collective-permute-done.1.refs_0_
  159.2 0.0 collective-permute-done.2.refs_1_
  159.2 0.0 collective-permute-done.3.refs_2_
  159.2 0.1 sum_x.1
  159.4 15.6 %all_to_all.28.got = bf16[8,136,128]{2,1,0:T(8,128)(2,1)S(1)} all-to-all(bf16[8,136,128]{2,1,0:T(8,128)(2,1)S(1)} %sum_x.1), channel_id=1, replica_groups=mesh['x'=4,'z'=8,'core'=2,'tp'=8] {'z'}, dimensions={0} | all-to-all | bytes 557056 | tf_op jit(solution)/shard_map/all_to_all | solution.py:265
  174.9 0.7 sum_z.1
Async XLA Ops:
  1.8 46.2 %copy-start = (bf16[1,1024,1024]{2,1,0:T(8,128)(2,1)S(1)}, bf16[1,1024,1024]{2,1,0:T(8,128)(2,1)}, u32[]{:S(2)}) copy-start(bf16[1,1024,1024]{2,1,0:T(8,128)(2,1)} %param.8) | copy-start | bytes 6291460
  1.8 46.1 %copy-start.1 = (f32[1,1024]{1,0:T(1,128)S(1)}, f32[1,1024]{1,0:T(1,128)}, u32[]{:S(2)}) copy-start(f32[1,1024]{1,0:T(1,128)} %gain.3) | copy-start | bytes 12292
  119.6 38.0 %all-to-all-start.3 = ((bf16[64,8,1152]{2,1,0:T(8,128)(2,1)}), bf16[64,8,1152]{2,1,0:T(8,128)(2,1)S(1)}, u32[]{:S(2)}, u32[]{:S(2)}) async-start(bf16[64,8,1152]{2,1,0:T(8,128)(2,1)} %get-tuple-element.39), calls=%async_computation.3 | async-start | bytes 2359296 | tf_op jit(solution)/shard_map/all_to_all | solution.py:265
  127.8 4.7 %collective-permute-start = (bf16[528,1024]{1,0:T(8,128)(2,1)S(1)}, bf16[528,1024]{1,0:T(8,128)(2,1)S(1)}, u32[]{:S(2)}, u32[]{:S(2)}) collective-permute-start(bf16[528,1024]{1,0:T(8,128)(2,1)S(1)} %get-tuple-element.35), channel_id=1, source_target_pairs={{0,8},{8,0},{1,9},{9,1},{2,10},{10,2},{3,11},{11,3},{4,12},{12,4},... | collective-permute-start | bytes 3244040 | tf_op jit(solution)/shard_map/ppermute | solution.py:321
  132.5 25.1 %copy-start.2 = (s32[32,1]{0,1:T(1,128)S(1)}, s32[32,1]{0,1:T(1,128)}, u32[]{:S(2)}) copy-start(s32[32,1]{0,1:T(1,128)} %param.7) | copy-start | bytes 388
  132.7 26.5 %collective-permute-start.1 = (bf16[1040,128]{1,0:T(8,128)(2,1)S(1)}, bf16[1040,128]{1,0:T(8,128)(2,1)S(1)}, u32[]{:S(2)}, u32[]{:S(2)}) collective-permute-start(bf16[1040,128]{1,0:T(8,128)(2,1)S(1)} %get-tuple-element.36), channel_id=1, source_target_pairs={{0,256},{128,384},{256,0},{384,128},{1,257},{129,385},{257,1},{385... | collective-permute-start | bytes 798728 | tf_op jit(solution)/shard_map/ppermute | solution.py:326
  137.5 21.7 %collective-permute-start.2 = (bf16[1040,128]{1,0:T(8,128)(2,1)S(1)}, bf16[1040,128]{1,0:T(8,128)(2,1)S(1)}, u32[]{:S(2)}, u32[]{:S(2)}) collective-permute-start(bf16[1040,128]{1,0:T(8,128)(2,1)S(1)} %get-tuple-element.37), channel_id=1, source_target_pairs={{0,128},{128,256},{256,384},{384,0},{1,129},{129,257},{257,385},{3... | collective-permute-start | bytes 798728 | tf_op jit(solution)/shard_map/ppermute | solution.py:326
  139.8 19.4 %collective-permute-start.3 = (bf16[1040,128]{1,0:T(8,128)(2,1)S(1)}, bf16[1040,128]{1,0:T(8,128)(2,1)S(1)}, u32[]{:S(2)}, u32[]{:S(2)}) collective-permute-start(bf16[1040,128]{1,0:T(8,128)(2,1)S(1)} %get-tuple-element.38), channel_id=1, source_target_pairs={{0,384},{128,0},{256,128},{384,256},{1,385},{129,1},{257,129},{385... | collective-permute-start | bytes 798728 | tf_op jit(solution)/shard_map/ppermute | solution.py:326

commit v13 on v12

--- a/solution.py
+++ b/solution.py
@@ -86,7 +86,7 @@
         out[d, :, F:] = columns[m]
         return 0
 
-    lax.fori_loop(0, PIECES, put, 0, unroll=4)
+    lax.fori_loop(0, PIECES, put, 0, unroll=8)
 
 
 def value_kernel(rows, gain, weights, out, gained, squares):
@@ -254,7 +254,7 @@
         values[m] = got[d, :, F:]
         return 0
 
-    lax.fori_loop(0, PIECES, take, 0)
+    lax.fori_loop(0, PIECES, take, 0, unroll=8)
 
 
 def shape(*dims, dtype=bf16):

time: 178 us -> 178 us (level)
  no operation moved by 1% of the time
where the time goes in v13:
time: 178 us; the launch traced here: 176 us
  blocking collectives  129 us (72%)
  starting transfers between devices  20.3 us (11%)
  waiting for transfers between devices  15.9 us (9%)
  Pallas kernels  9.3 us (5%)
    all_to_all x4, blocking collectives, exchange(): return lax.all_to_all(v, axes, split_axis=0, concat_axis=0, tiled=True)  129 us
    all_to_all x1, waiting for transfers between devices, exchange(): return lax.all_to_all(v, axes, split_axis=0, concat_axis=0, tiled=True)  13.6 us
    ppermute x3, starting transfers between devices, body(): lax.ppermute(v, 'x', [(i, (i + d) % X) for i in range(X)])  11.3 us
    all_to_all x1, starting transfers between devices, exchange(): return lax.all_to_all(v, axes, split_axis=0, concat_axis=0, tiled=True)  6.64 us
  transfers between devices with their start and end apart: 5, of which 2 were waited for; matrix products, arithmetic and copies ran while one was open for 0% of the time, Pallas kernels for 2%

profile of v13, /device:TPU:1, one launch (start us, length us, event | category | flops | bytes accessed | tf_op | source)
XLA Modules:
  0.0 175.6 jit_solution(17394863813179849768)
XLA Ops:
  0.6 1.1 pack.1
  1.8 0.0 copy-start
  1.8 0.0 copy-start.1
  1.8 46.1 %all_to_all.25.rows.goals = bf16[64,8,1152]{2,1,0:T(8,128)(2,1)S(1)} all-to-all(bf16[64,8,1152]{2,1,0:T(8,128)(2,1)S(1)} %pack.1), channel_id=1, replica_groups=mesh['x'=4,'z'=8,'core'=2,'tp'=8] {'x','z','core'}, dimensions={0} | all-to-all | bytes 2359296 | tf_op jit(solution)/shard_map/all_to_all | solution.py:265
  47.9 0.0 copy-done
  47.9 0.0 copy-done.1
  47.9 1.3 partial_values.1
  49.2 36.1 %all_to_all.26.got = bf16[8,520,128]{2,1,0:T(8,128)(2,1)S(1)} all-to-all(bf16[8,520,128]{2,1,0:T(8,128)(2,1)S(1)} %get-tuple-element.27), channel_id=1, replica_groups=mesh['x'=4,'z'=8,'core'=2,'tp'=8] {'tp'}, dimensions={0} | all-to-all | bytes 2129920 | tf_op jit(solution)/shard_map/all_to_all | solution.py:265
  85.4 0.3 loss.1
  85.7 31.4 %all_to_all.27.got = bf16[8,520,128]{2,1,0:T(8,128)(2,1)S(1)} all-to-all(bf16[8,520,128]{2,1,0:T(8,128)(2,1)S(1)} %get-tuple-element.28), channel_id=1, replica_groups=mesh['x'=4,'z'=8,'core'=2,'tp'=8] {'tp'}, dimensions={0} | all-to-all | bytes 2129920 | tf_op jit(solution)/shard_map/all_to_all | solution.py:265
  117.0 2.6 %grads.1 = (bf16[64,8,1152]{2,1,0:T(8,128)(2,1)}, bf16[512,1024]{1,0:T(8,128)(2,1)S(1)}, f32[8,1024]{1,0:T(8,128)S(1)}) custom-call(bf16[8,520,128]{2,1,0:T(8,128)(2,1)S(1)} %all_to_all.27.got, bf16[64,8,1152]{2,1,0:T(8,128)(2,1)S(1)} %all_to_all.25.rows.goals, f32[1,1024]{1,0:T(1,128)S(1)} %copy-done.1, bf16[1024,1024]{1,0:T(8,128)(2,1)S(1)} %bitcast.8, ...), custom_call_target="tpu_custom_call" | custom-call | flops 1073741824 | bytes 8388608 | tf_op jit(solution)/shard_map/grads/pallas_call | solution.py:301
  119.6 6.6 %all-to-all-start.3 = ((bf16[64,8,1152]{2,1,0:T(8,128)(2,1)}), bf16[64,8,1152]{2,1,0:T(8,128)(2,1)S(1)}, u32[]{:S(2)}, u32[]{:S(2)}) async-start(bf16[64,8,1152]{2,1,0:T(8,128)(2,1)} %get-tuple-element.39), calls=%async_computation.3 | async-start | bytes 2359296 | tf_op jit(solution)/shard_map/all_to_all | solution.py:265
  126.2 1.5 share.1
  127.8 2.4 %collective-permute-start = (bf16[528,1024]{1,0:T(8,128)(2,1)S(1)}, bf16[528,1024]{1,0:T(8,128)(2,1)S(1)}, u32[]{:S(2)}, u32[]{:S(2)}) collective-permute-start(bf16[528,1024]{1,0:T(8,128)(2,1)S(1)} %get-tuple-element.35), channel_id=1, source_target_pairs={{0,8},{8,0},{1,9},{9,1},{2,10},{10,2},{3,11},{11,3},{4,12},{12,4},... | collective-permute-start | bytes 3244040 | tf_op jit(solution)/shard_map/ppermute | solution.py:321
  130.1 2.3 %collective-permute-done.got = bf16[528,1024]{1,0:T(8,128)(2,1)S(1)} collective-permute-done((bf16[528,1024]{1,0:T(8,128)(2,1)S(1)}, bf16[528,1024]{1,0:T(8,128)(2,1)S(1)}, u32[]{:S(2)}, u32[]{:S(2)}) %collective-permute-start) | collective-permute-done | bytes 1081376 | tf_op jit(solution)/shard_map/ppermute | solution.py:321
  132.4 0.0 copy-start.2
  132.4 0.3 sum_core.1
  132.7 4.8 %collective-permute-start.1 = (bf16[1040,128]{1,0:T(8,128)(2,1)S(1)}, bf16[1040,128]{1,0:T(8,128)(2,1)S(1)}, u32[]{:S(2)}, u32[]{:S(2)}) collective-permute-start(bf16[1040,128]{1,0:T(8,128)(2,1)S(1)} %get-tuple-element.36), channel_id=1, source_target_pairs={{0,256},{128,384},{256,0},{384,128},{1,257},{129,385},{257,1},{385... | collective-permute-start | bytes 798728 | tf_op jit(solution)/shard_map/ppermute | solution.py:326
  137.5 2.3 %collective-permute-start.2 = (bf16[1040,128]{1,0:T(8,128)(2,1)S(1)}, bf16[1040,128]{1,0:T(8,128)(2,1)S(1)}, u32[]{:S(2)}, u32[]{:S(2)}) collective-permute-start(bf16[1040,128]{1,0:T(8,128)(2,1)S(1)} %get-tuple-element.37), channel_id=1, source_target_pairs={{0,128},{128,256},{256,384},{384,0},{1,129},{129,257},{257,385},{3... | collective-permute-start | bytes 798728 | tf_op jit(solution)/shard_map/ppermute | solution.py:326
  139.8 4.2 %collective-permute-start.3 = (bf16[1040,128]{1,0:T(8,128)(2,1)S(1)}, bf16[1040,128]{1,0:T(8,128)(2,1)S(1)}, u32[]{:S(2)}, u32[]{:S(2)}) collective-permute-start(bf16[1040,128]{1,0:T(8,128)(2,1)S(1)} %get-tuple-element.38), channel_id=1, source_target_pairs={{0,384},{128,0},{256,128},{384,256},{1,385},{129,1},{257,129},{385... | collective-permute-start | bytes 798728 | tf_op jit(solution)/shard_map/ppermute | solution.py:326
  144.0 13.6 %all-to-all-done.3.got = bf16[64,8,1152]{2,1,0:T(8,128)(2,1)S(1)} async-done(((bf16[64,8,1152]{2,1,0:T(8,128)(2,1)}), bf16[64,8,1152]{2,1,0:T(8,128)(2,1)S(1)}, u32[]{:S(2)}, u32[]{:S(2)}) %all-to-all-start.3) | async-done | bytes 1179680 | tf_op jit(solution)/shard_map/all_to_all | solution.py:265
  157.6 0.0 copy-done.2
  157.6 1.4 unpack.1
  159.0 0.0 collective-permute-done.1.refs_0_
  159.0 0.0 collective-permute-done.2.refs_1_
  159.0 0.0 collective-permute-done.3.refs_2_
  159.0 0.1 sum_x.1
  159.2 15.7 %all_to_all.28.got = bf16[8,136,128]{2,1,0:T(8,128)(2,1)S(1)} all-to-all(bf16[8,136,128]{2,1,0:T(8,128)(2,1)S(1)} %sum_x.1), channel_id=1, replica_groups=mesh['x'=4,'z'=8,'core'=2,'tp'=8] {'z'}, dimensions={0} | all-to-all | bytes 557056 | tf_op jit(solution)/shard_map/all_to_all | solution.py:265
  174.9 0.7 sum_z.1
Async XLA Ops:
  1.8 46.2 %copy-start = (bf16[1,1024,1024]{2,1,0:T(8,128)(2,1)S(1)}, bf16[1,1024,1024]{2,1,0:T(8,128)(2,1)}, u32[]{:S(2)}) copy-start(bf16[1,1024,1024]{2,1,0:T(8,128)(2,1)} %param.8) | copy-start | bytes 6291460
  1.8 46.1 %copy-start.1 = (f32[1,1024]{1,0:T(1,128)S(1)}, f32[1,1024]{1,0:T(1,128)}, u32[]{:S(2)}) copy-start(f32[1,1024]{1,0:T(1,128)} %gain.3) | copy-start | bytes 12292
  119.6 38.0 %all-to-all-start.3 = ((bf16[64,8,1152]{2,1,0:T(8,128)(2,1)}), bf16[64,8,1152]{2,1,0:T(8,128)(2,1)S(1)}, u32[]{:S(2)}, u32[]{:S(2)}) async-start(bf16[64,8,1152]{2,1,0:T(8,128)(2,1)} %get-tuple-element.39), calls=%async_computation.3 | async-start | bytes 2359296 | tf_op jit(solution)/shard_map/all_to_all | solution.py:265
  127.8 4.7 %collective-permute-start = (bf16[528,1024]{1,0:T(8,128)(2,1)S(1)}, bf16[528,1024]{1,0:T(8,128)(2,1)S(1)}, u32[]{:S(2)}, u32[]{:S(2)}) collective-permute-start(bf16[528,1024]{1,0:T(8,128)(2,1)S(1)} %get-tuple-element.35), channel_id=1, source_target_pairs={{0,8},{8,0},{1,9},{9,1},{2,10},{10,2},{3,11},{11,3},{4,12},{12,4},... | collective-permute-start | bytes 3244040 | tf_op jit(solution)/shard_map/ppermute | solution.py:321
  132.4 25.2 %copy-start.2 = (s32[32,1]{0,1:T(1,128)S(1)}, s32[32,1]{0,1:T(1,128)}, u32[]{:S(2)}) copy-start(s32[32,1]{0,1:T(1,128)} %param.7) | copy-start | bytes 388
  132.7 26.3 %collective-permute-start.1 = (bf16[1040,128]{1,0:T(8,128)(2,1)S(1)}, bf16[1040,128]{1,0:T(8,128)(2,1)S(1)}, u32[]{:S(2)}, u32[]{:S(2)}) collective-permute-start(bf16[1040,128]{1,0:T(8,128)(2,1)S(1)} %get-tuple-element.36), channel_id=1, source_target_pairs={{0,256},{128,384},{256,0},{384,128},{1,257},{129,385},{257,1},{385... | collective-permute-start | bytes 798728 | tf_op jit(solution)/shard_map/ppermute | solution.py:326
  137.5 21.5 %collective-permute-start.2 = (bf16[1040,128]{1,0:T(8,128)(2,1)S(1)}, bf16[1040,128]{1,0:T(8,128)(2,1)S(1)}, u32[]{:S(2)}, u32[]{:S(2)}) collective-permute-start(bf16[1040,128]{1,0:T(8,128)(2,1)S(1)} %get-tuple-element.37), channel_id=1, source_target_pairs={{0,128},{128,256},{256,384},{384,0},{1,129},{129,257},{257,385},{3... | collective-permute-start | bytes 798728 | tf_op jit(solution)/shard_map/ppermute | solution.py:326
  139.8 19.2 %collective-permute-start.3 = (bf16[1040,128]{1,0:T(8,128)(2,1)S(1)}, bf16[1040,128]{1,0:T(8,128)(2,1)S(1)}, u32[]{:S(2)}, u32[]{:S(2)}) collective-permute-start(bf16[1040,128]{1,0:T(8,128)(2,1)S(1)} %get-tuple-element.38), channel_id=1, source_target_pairs={{0,384},{128,0},{256,128},{384,256},{1,385},{129,1},{257,129},{385... | collective-permute-start | bytes 798728 | tf_op jit(solution)/shard_map/ppermute | solution.py:326

commit v14 on v12

--- a/solution.py
+++ b/solution.py
@@ -14,7 +14,7 @@
 NP = 64
 NT = 8
 X, Z, CORES = 4, 8, 2
-X_STEPS = (2, 1, 3)
+X_STEPS = (2, 3, 1)
 ROWS = NP * MB
 TILE = 128
 NTILES = ROWS // TILE

time: 178 us -> 178 us (level)
  no operation moved by 1% of the time
where the time goes in v14:
time: 178 us; the launch traced here: 176 us
  blocking collectives  129 us (72%)
  starting transfers between devices  19.1 us (11%)
  waiting for transfers between devices  17.1 us (10%)
  Pallas kernels  9.51 us (5%)
    all_to_all x4, blocking collectives, exchange(): return lax.all_to_all(v, axes, split_axis=0, concat_axis=0, tiled=True)  129 us
    all_to_all x1, waiting for transfers between devices, exchange(): return lax.all_to_all(v, axes, split_axis=0, concat_axis=0, tiled=True)  14.8 us
    ppermute x3, starting transfers between devices, body(): lax.ppermute(v, 'x', [(i, (i + d) % X) for i in range(X)])  10.1 us
    all_to_all x1, starting transfers between devices, exchange(): return lax.all_to_all(v, axes, split_axis=0, concat_axis=0, tiled=True)  6.65 us
  transfers between devices with their start and end apart: 5, of which 2 were waited for; matrix products, arithmetic and copies ran while one was open for 0% of the time, Pallas kernels for 2%

profile of v14, /device:TPU:1, one launch (start us, length us, event | category | flops | bytes accessed | tf_op | source)
XLA Modules:
  0.0 175.6 jit_solution(8167498200145770924)
XLA Ops:
  0.6 1.2 pack.1
  1.8 0.0 copy-start
  1.8 0.0 copy-start.1
  1.8 46.1 %all_to_all.25.rows.goals = bf16[64,8,1152]{2,1,0:T(8,128)(2,1)S(1)} all-to-all(bf16[64,8,1152]{2,1,0:T(8,128)(2,1)S(1)} %pack.1), channel_id=1, replica_groups=mesh['x'=4,'z'=8,'core'=2,'tp'=8] {'x','z','core'}, dimensions={0} | all-to-all | bytes 2359296 | tf_op jit(solution)/shard_map/all_to_all | solution.py:265
  48.0 0.0 copy-done
  48.0 0.0 copy-done.1
  48.0 1.3 partial_values.1
  49.3 36.1 %all_to_all.26.got = bf16[8,520,128]{2,1,0:T(8,128)(2,1)S(1)} all-to-all(bf16[8,520,128]{2,1,0:T(8,128)(2,1)S(1)} %get-tuple-element.27), channel_id=1, replica_groups=mesh['x'=4,'z'=8,'core'=2,'tp'=8] {'tp'}, dimensions={0} | all-to-all | bytes 2129920 | tf_op jit(solution)/shard_map/all_to_all | solution.py:265
  85.4 0.3 loss.1
  85.7 31.4 %all_to_all.27.got = bf16[8,520,128]{2,1,0:T(8,128)(2,1)S(1)} all-to-all(bf16[8,520,128]{2,1,0:T(8,128)(2,1)S(1)} %get-tuple-element.28), channel_id=1, replica_groups=mesh['x'=4,'z'=8,'core'=2,'tp'=8] {'tp'}, dimensions={0} | all-to-all | bytes 2129920 | tf_op jit(solution)/shard_map/all_to_all | solution.py:265
  117.0 2.6 %grads.1 = (bf16[64,8,1152]{2,1,0:T(8,128)(2,1)}, bf16[512,1024]{1,0:T(8,128)(2,1)S(1)}, f32[8,1024]{1,0:T(8,128)S(1)}) custom-call(bf16[8,520,128]{2,1,0:T(8,128)(2,1)S(1)} %all_to_all.27.got, bf16[64,8,1152]{2,1,0:T(8,128)(2,1)S(1)} %all_to_all.25.rows.goals, f32[1,1024]{1,0:T(1,128)S(1)} %copy-done.1, bf16[1024,1024]{1,0:T(8,128)(2,1)S(1)} %bitcast.8, ...), custom_call_target="tpu_custom_call" | custom-call | flops 1073741824 | bytes 8388608 | tf_op jit(solution)/shard_map/grads/pallas_call | solution.py:301
  119.6 6.6 %all-to-all-start.3 = ((bf16[64,8,1152]{2,1,0:T(8,128)(2,1)}), bf16[64,8,1152]{2,1,0:T(8,128)(2,1)S(1)}, u32[]{:S(2)}, u32[]{:S(2)}) async-start(bf16[64,8,1152]{2,1,0:T(8,128)(2,1)} %get-tuple-element.39), calls=%async_computation.3 | async-start | bytes 2359296 | tf_op jit(solution)/shard_map/all_to_all | solution.py:265
  126.2 1.5 share.1
  127.8 2.4 %collective-permute-start = (bf16[528,1024]{1,0:T(8,128)(2,1)S(1)}, bf16[528,1024]{1,0:T(8,128)(2,1)S(1)}, u32[]{:S(2)}, u32[]{:S(2)}) collective-permute-start(bf16[528,1024]{1,0:T(8,128)(2,1)S(1)} %get-tuple-element.35), channel_id=1, source_target_pairs={{0,8},{8,0},{1,9},{9,1},{2,10},{10,2},{3,11},{11,3},{4,12},{12,4},... | collective-permute-start | bytes 3244040 | tf_op jit(solution)/shard_map/ppermute | solution.py:321
  130.1 2.3 %collective-permute-done.got = bf16[528,1024]{1,0:T(8,128)(2,1)S(1)} collective-permute-done((bf16[528,1024]{1,0:T(8,128)(2,1)S(1)}, bf16[528,1024]{1,0:T(8,128)(2,1)S(1)}, u32[]{:S(2)}, u32[]{:S(2)}) %collective-permute-start) | collective-permute-done | bytes 1081376 | tf_op jit(solution)/shard_map/ppermute | solution.py:321
  132.5 0.0 copy-start.2
  132.5 0.3 sum_core.1
  132.7 4.8 %collective-permute-start.1 = (bf16[1040,128]{1,0:T(8,128)(2,1)S(1)}, bf16[1040,128]{1,0:T(8,128)(2,1)S(1)}, u32[]{:S(2)}, u32[]{:S(2)}) collective-permute-start(bf16[1040,128]{1,0:T(8,128)(2,1)S(1)} %get-tuple-element.36), channel_id=1, source_target_pairs={{0,256},{128,384},{256,0},{384,128},{1,257},{129,385},{257,1},{385... | collective-permute-start | bytes 798728 | tf_op jit(solution)/shard_map/ppermute | solution.py:326
  137.5 2.7 %collective-permute-start.2 = (bf16[1040,128]{1,0:T(8,128)(2,1)S(1)}, bf16[1040,128]{1,0:T(8,128)(2,1)S(1)}, u32[]{:S(2)}, u32[]{:S(2)}) collective-permute-start(bf16[1040,128]{1,0:T(8,128)(2,1)S(1)} %get-tuple-element.37), channel_id=1, source_target_pairs={{0,384},{128,0},{256,128},{384,256},{1,385},{129,1},{257,129},{385... | collective-permute-start | bytes 798728 | tf_op jit(solution)/shard_map/ppermute | solution.py:326
  140.2 2.6 %collective-permute-start.3 = (bf16[1040,128]{1,0:T(8,128)(2,1)S(1)}, bf16[1040,128]{1,0:T(8,128)(2,1)S(1)}, u32[]{:S(2)}, u32[]{:S(2)}) collective-permute-start(bf16[1040,128]{1,0:T(8,128)(2,1)S(1)} %get-tuple-element.38), channel_id=1, source_target_pairs={{0,128},{128,256},{256,384},{384,0},{1,129},{129,257},{257,385},{3... | collective-permute-start | bytes 798728 | tf_op jit(solution)/shard_map/ppermute | solution.py:326
  142.8 14.8 %all-to-all-done.3.got = bf16[64,8,1152]{2,1,0:T(8,128)(2,1)S(1)} async-done(((bf16[64,8,1152]{2,1,0:T(8,128)(2,1)}), bf16[64,8,1152]{2,1,0:T(8,128)(2,1)S(1)}, u32[]{:S(2)}, u32[]{:S(2)}) %all-to-all-start.3) | async-done | bytes 1179680 | tf_op jit(solution)/shard_map/all_to_all | solution.py:265
  157.6 0.0 copy-done.2
  157.6 1.6 unpack.1
  159.2 0.0 collective-permute-done.1.refs_0_
  159.2 0.0 collective-permute-done.2.refs_1_
  159.2 0.0 collective-permute-done.3.refs_2_
  159.2 0.1 sum_x.1
  159.4 15.6 %all_to_all.28.got = bf16[8,136,128]{2,1,0:T(8,128)(2,1)S(1)} all-to-all(bf16[8,136,128]{2,1,0:T(8,128)(2,1)S(1)} %sum_x.1), channel_id=1, replica_groups=mesh['x'=4,'z'=8,'core'=2,'tp'=8] {'z'}, dimensions={0} | all-to-all | bytes 557056 | tf_op jit(solution)/shard_map/all_to_all | solution.py:265
  174.9 0.7 sum_z.1
Async XLA Ops:
  1.8 46.2 %copy-start = (bf16[1,1024,1024]{2,1,0:T(8,128)(2,1)S(1)}, bf16[1,1024,1024]{2,1,0:T(8,128)(2,1)}, u32[]{:S(2)}) copy-start(bf16[1,1024,1024]{2,1,0:T(8,128)(2,1)} %param.8) | copy-start | bytes 6291460
  1.8 46.1 %copy-start.1 = (f32[1,1024]{1,0:T(1,128)S(1)}, f32[1,1024]{1,0:T(1,128)}, u32[]{:S(2)}) copy-start(f32[1,1024]{1,0:T(1,128)} %gain.3) | copy-start | bytes 12292
  119.6 38.0 %all-to-all-start.3 = ((bf16[64,8,1152]{2,1,0:T(8,128)(2,1)}), bf16[64,8,1152]{2,1,0:T(8,128)(2,1)S(1)}, u32[]{:S(2)}, u32[]{:S(2)}) async-start(bf16[64,8,1152]{2,1,0:T(8,128)(2,1)} %get-tuple-element.39), calls=%async_computation.3 | async-start | bytes 2359296 | tf_op jit(solution)/shard_map/all_to_all | solution.py:265
  127.8 4.7 %collective-permute-start = (bf16[528,1024]{1,0:T(8,128)(2,1)S(1)}, bf16[528,1024]{1,0:T(8,128)(2,1)S(1)}, u32[]{:S(2)}, u32[]{:S(2)}) collective-permute-start(bf16[528,1024]{1,0:T(8,128)(2,1)S(1)} %get-tuple-element.35), channel_id=1, source_target_pairs={{0,8},{8,0},{1,9},{9,1},{2,10},{10,2},{3,11},{11,3},{4,12},{12,4},... | collective-permute-start | bytes 3244040 | tf_op jit(solution)/shard_map/ppermute | solution.py:321
  132.5 25.1 %copy-start.2 = (s32[32,1]{0,1:T(1,128)S(1)}, s32[32,1]{0,1:T(1,128)}, u32[]{:S(2)}) copy-start(s32[32,1]{0,1:T(1,128)} %param.7) | copy-start | bytes 388
  132.7 26.5 %collective-permute-start.1 = (bf16[1040,128]{1,0:T(8,128)(2,1)S(1)}, bf16[1040,128]{1,0:T(8,128)(2,1)S(1)}, u32[]{:S(2)}, u32[]{:S(2)}) collective-permute-start(bf16[1040,128]{1,0:T(8,128)(2,1)S(1)} %get-tuple-element.36), channel_id=1, source_target_pairs={{0,256},{128,384},{256,0},{384,128},{1,257},{129,385},{257,1},{385... | collective-permute-start | bytes 798728 | tf_op jit(solution)/shard_map/ppermute | solution.py:326
  137.5 21.7 %collective-permute-start.2 = (bf16[1040,128]{1,0:T(8,128)(2,1)S(1)}, bf16[1040,128]{1,0:T(8,128)(2,1)S(1)}, u32[]{:S(2)}, u32[]{:S(2)}) collective-permute-start(bf16[1040,128]{1,0:T(8,128)(2,1)S(1)} %get-tuple-element.37), channel_id=1, source_target_pairs={{0,384},{128,0},{256,128},{384,256},{1,385},{129,1},{257,129},{385... | collective-permute-start | bytes 798728 | tf_op jit(solution)/shard_map/ppermute | solution.py:326
  140.2 19.0 %collective-permute-start.3 = (bf16[1040,128]{1,0:T(8,128)(2,1)S(1)}, bf16[1040,128]{1,0:T(8,128)(2,1)S(1)}, u32[]{:S(2)}, u32[]{:S(2)}) collective-permute-start(bf16[1040,128]{1,0:T(8,128)(2,1)S(1)} %get-tuple-element.38), channel_id=1, source_target_pairs={{0,128},{128,256},{256,384},{384,0},{1,129},{129,257},{257,385},{3... | collective-permute-start | bytes 798728 | tf_op jit(solution)/shard_map/ppermute | solution.py:326
